TPU v7x, 512 devices: a whole 4x4x16 slice. The times are simulated.
512 devices in a mesh: strip: 128 (over z, x, core), col: 4 (over y).
Axes of the slice: x: 4, y: 4, z: 16, core: 2. Of those that a mesh axis runs over, the one named last changes fastest.
Arguments:
- positions: float32 [3, 1024, 1024], P(None, 'strip', 'col'), may hold values from -1.8 to 1.8
- target: float32 [3, 1024, 1024], P(None, 'strip', 'col'), may hold values from -1.8 to 1.8
- inertia: float32 [1024, 1024], P('strip', 'col'), may hold values from 1 to 4
- stiffness: float32 [3, 1024, 1024], P(None, 'strip', 'col'), may hold values from 0.5 to 2
- pin_columns: int32 [64], replicated, may hold values from 0 to 1023
- inverses: bfloat16 [512, 512, 512], P('strip'), may hold values from -0.05 to 0.55
Outputs:
- displaced: float32 [3, 1024, 1024], P(None, 'strip', 'col')
Inputs may be any that keep to these rules, and one draw needn't show every extreme that they name: `pin_columns`: a column may appear more than once.
All inputs are finite; a program needn't handle non-finite values.
Results may differ from a plain program's by a relative error of at most 0.0003.
Values sent between devices are 32-bit elements; how exact they have to be, the bound alone decides.
No kernel may reach another device: no remote copies, remote signals or barrier semaphores. Data moves between devices by JAX's collectives and lax.ppermute only.
A program may use at most 128 MiB of HBM per device.

v0:
```python
import jax
import jax.numpy as jnp
from jax import lax
from jax.sharding import Mesh
from jax.sharding import PartitionSpec as P

ITERS = 2
STRIP = ("strip_0", "strip_1", "strip_2")


pin_stiffness = 20.0
highest = lax.Precision.HIGHEST


def passed_along(value, axis, steps):
    count = lax.axis_size(axis)
    initial, last = (max(0, -steps), min(count, count - steps))
    return lax.ppermute(value, axis, [(source, source + steps) for source in range(initial, last)])


def extended(cells, sides, width):
    for axis, dim in sides:
        count = lax.axis_size(axis)
        ends = count - 1
        head = lax.slice_in_dim(cells, 0, width, axis=dim)
        tail = lax.slice_in_dim(cells, cells.shape[dim] - width, cells.shape[dim], axis=dim)
        cells = jnp.concatenate(
            [
                lax.ppermute(tail, axis, [(i, (i + 1) % count) for i in range(ends)]),
                cells,
                lax.ppermute(head, axis, [((i + 1) % count, i) for i in range(ends)]),
            ],
            axis=dim,
        )
    return cells


def neutral_like(value, identity):
    return jax.tree.map(
        lambda a, e: jnp.broadcast_to(jnp.asarray(e, a.dtype), a.shape), value, identity
    )


def prefix_by_axis(value, axes, combine, identity):
    before = start = neutral_like(value, identity)
    so_far = value
    for axis in reversed(axes):
        size, index = (lax.axis_size(axis), lax.axis_index(axis))
        pieces = jax.tree.map(lambda part: lax.all_gather(part, axis), so_far)
        inside, so_far = (start, start)
        for k in range(size):
            passed = k < index
            so_far = combine(so_far, jax.tree.map(lambda part: part[k], pieces))
            inside = jax.tree.map(lambda new, old: jnp.where(passed, new, old), so_far, inside)
        before = combine(inside, before)
    return before


def matmul(left_side, right_side):
    return jnp.dot(left_side, right_side, precision=highest, preferred_element_type=jnp.float32)


def times_transposed(rows_in, matrix):
    return lax.dot_general(
        rows_in,
        matrix,
        (((rows_in.ndim - 1,), (1,)), ((), ())),
        precision=highest,
        preferred_element_type=jnp.float32,
    )


def axis_vector(offset, direction):
    entries = [0.0, 0.0, 0.0]
    entries[direction] = float(offset)
    return jnp.array(entries, jnp.float32).reshape(3, 1, 1)


def edge_force(top_side, low_side, weight, rest_vec, rest_len):
    spacing = rest_vec + low_side - top_side
    length = jnp.sqrt(jnp.sum(spacing * spacing, axis=0, keepdims=True))
    projected = rest_len * spacing / jnp.maximum(length, 0.5 * rest_len)
    return weight[None] * (projected - rest_vec)


def spread(pulling, offset):
    return jnp.pad(-pulling, ((0, 0), (0, 0), (0, offset))) + jnp.pad(
        pulling, ((0, 0), (0, 0), (offset, 0))
    )


def shards(positions, target, inertia, stiffness, pin_columns, inverses):
    rows_dev = positions.shape[1]
    cols_dev = positions.shape[2]
    strips_dev = inverses.shape[0]
    strip_rows = rows_dev // strips_dev
    last_start = (strip_rows - 1) * cols_dev
    grid_rows = rows_dev * lax.axis_size(STRIP)
    grid_cols = cols_dev * lax.axis_size("col")
    row_start = lax.axis_index(STRIP) * rows_dev
    col_start = lax.axis_index("col") * cols_dev
    global_rows = row_start + jnp.arange(rows_dev, dtype=jnp.int32)
    wide_cols = col_start - 2 + jnp.arange(cols_dev + 4, dtype=jnp.int32)
    left_weights = passed_along(stiffness[:, :, -2:], "col", 1)
    right_blank = jnp.zeros((3, rows_dev, 2), jnp.float32)
    weights_ext = jnp.concatenate([left_weights, stiffness, right_blank], axis=2)
    edge_list = []
    for offset, channel in ((1, 0), (2, 2)):
        left_cols = wide_cols[: cols_dev + 4 - offset]
        inside = (left_cols >= 0) & (left_cols + offset <= grid_cols - 1)
        crossing = (left_cols + offset) // cols_dev != left_cols // cols_dev
        edge_weight = jnp.where(inside[None, :], weights_ext[channel][:, :-offset], 0.0)
        cross_weight = jnp.where(crossing[None, :], edge_weight, 0.0)
        edge_list.append((offset, edge_weight, cross_weight))
    vertical = jnp.where((global_rows < grid_rows - 1)[:, None], stiffness[1], 0.0)
    is_last = jnp.arange(rows_dev, dtype=jnp.int32) % strip_rows == strip_rows - 1
    weights_down = jnp.where(is_last[:, None], vertical, 0.0)
    weights_rows = vertical[strip_rows - 1 :: strip_rows][:, None, :]
    own_cols = col_start + jnp.arange(cols_dev, dtype=jnp.int32)
    pinned = jnp.any(pin_columns[:, None] == own_cols[None, :], axis=0) & (row_start == 0)
    pinned_row = jnp.where(pinned[None, :], positions[:, 0, :], 0.0)
    anchor = jnp.zeros_like(positions).at[:, 0, :].set(pinned_row)
    inertial = inertia[None] * target + pin_stiffness * anchor
    solve_mats = inverses.astype(jnp.float32)
    last_from_first = solve_mats[:, last_start:, :cols_dev]
    first_cols = solve_mats[:, :, :cols_dev]
    transfer = weights_rows.transpose(0, 2, 1) * last_from_first
    identity = jnp.eye(cols_dev, dtype=jnp.float32)

    def compose(product, factor):
        return (matmul(factor, product), None)

    device_map, unused = lax.scan(compose, identity, transfer)

    def combine(earlier, follower):
        return (
            matmul(follower[0], earlier[0]),
            times_transposed(earlier[1], follower[0]) + follower[1],
        )

    def carry_offset(carried, inputs):
        last_rows, weight_row, matrix = inputs
        return (weight_row * (last_rows + times_transposed(carried, matrix)), None)

    def finish(carried, inputs):
        solved, weight_row, matrix = inputs
        complete = solved + times_transposed(carried, matrix)
        return (weight_row * complete[:, last_start:], complete)

    displaced = positions
    for sweep_number in range(ITERS):
        widened = extended(displaced, (("col", 2),), 2)
        summed = jnp.zeros_like(widened)
        coupled = jnp.zeros_like(widened)
        for offset, edge_weight, cross_weight in edge_list:
            pulling = edge_force(
                widened[:, :, :-offset],
                widened[:, :, offset:],
                edge_weight,
                axis_vector(offset, 0),
                float(offset),
            )
            summed = summed + spread(pulling, offset)
            coupled = coupled + jnp.pad(
                cross_weight[None] * widened[:, :, offset:], ((0, 0), (0, 0), (0, offset))
            )
            coupled = coupled + jnp.pad(
                cross_weight[None] * widened[:, :, :-offset], ((0, 0), (0, 0), (offset, 0))
            )
        forces = summed[:, :, 2:-2]
        coupling = coupled[:, :, 2:-2]
        internal = edge_force(
            displaced[:, :-1], displaced[:, 1:], vertical[:-1], axis_vector(1, 1), 1.0
        )
        forces = (
            forces
            + jnp.pad(-internal, ((0, 0), (0, 1), (0, 0)))
            + jnp.pad(internal, ((0, 0), (1, 0), (0, 0)))
        )
        stacked = jnp.concatenate([displaced, vertical[None]], axis=0)
        beside_all = extended(stacked, ((STRIP, 1),), 1)
        next_row = beside_all[:3, -1:]
        to_below = edge_force(displaced[:, -1:], next_row, vertical[-1:], axis_vector(1, 1), 1.0)
        from_above = edge_force(
            beside_all[:3, :1], displaced[:, :1], beside_all[3, :1], axis_vector(1, 1), 1.0
        )
        forces = (
            forces
            + jnp.pad(-to_below, ((0, 0), (rows_dev - 1, 0), (0, 0)))
            + jnp.pad(from_above, ((0, 0), (0, rows_dev - 1), (0, 0)))
        )
        next_rows = jnp.concatenate([displaced[:, 1:], next_row], axis=1)
        rhs_field = inertial + forces + coupling + weights_down[None] * next_rows
        rhs_strips = rhs_field.reshape(3, strips_dev, strip_rows * cols_dev).transpose(1, 0, 2)
        base_solved = lax.dot_general(
            rhs_strips,
            solve_mats,
            (((2,), (2,)), ((0,), (0,))),
            precision=highest,
            preferred_element_type=jnp.float32,
        )
        zero_row = jnp.zeros((3, cols_dev), jnp.float32)
        device_offset, unused = lax.scan(
            carry_offset, zero_row, (base_solved[:, :, last_start:], weights_rows, last_from_first)
        )
        prefix = prefix_by_axis((device_map, device_offset), STRIP, combine, (identity, zero_row))
        incoming = prefix[1]
        unused, finished = lax.scan(finish, incoming, (base_solved, weights_rows, first_cols))
        displaced = finished.transpose(1, 0, 2).reshape(3, rows_dev, cols_dev)
    return displaced


def solution(mesh):
    split = Mesh(
        mesh.devices.reshape(16, 4, 2, mesh.shape["col"]), ("strip_0", "strip_1", "strip_2", "col")
    )
    return jax.shard_map(
        shards,
        mesh=split,
        in_specs=(
            P(None, STRIP, "col"),
            P(None, STRIP, "col"),
            P(STRIP, "col"),
            P(None, STRIP, "col"),
            P(),
            P(STRIP, None, None),
        ),
        out_specs=P(None, STRIP, "col"),
        check_vma=False,
    )
```

profile of v0, /device:TPU:24, one launch (start us, length us, event | category | flops | bytes accessed | tf_op | source)
XLA Modules:
  0.0 270.3 jit_solution(3223637138222591555)
XLA Ops:
  7.4 2.2 convert_element_type.43
  9.8 1.7 while.57
  11.6 2.3 all-gather
  16.6 1.3 collective-permute-start.1
  17.9 4.5 %collective-permute-start.2 = (f32[3,8,2]{2,1,0:T(8,128)}, f32[3,8,2]{2,1,0:T(8,128)S(1)}, u32[]{:S(2)}, u32[]{:S(2)}) collective-permute-start(f32[3,8,2]{2,1,0:T(8,128)} %get-tuple-element.366), channel_id=1, source_target_pairs={{1,0},{2,1},{3,2},{5,4},{6,5},{7,6},{9,8},{10,9},{11,10},{13,12},{... | collective-permute-start | bytes 584 | tf_op jit(solution)/shard_map/ppermute | solution.py:31
  22.5 1.3 collective-permute-start
  25.1 1.3 collective-permute-start.3
  26.4 3.6 %collective-permute-start.4 = (f32[4,1,256]{2,1,0:T(1,128)}, f32[4,1,256]{2,1,0:T(1,128)}, u32[]{:S(2)}, u32[]{:S(2)}) collective-permute-start(f32[4,1,256]{2,1,0:T(1,128)} %get-tuple-element.355), channel_id=1, source_target_pairs={{0,4},{4,8},{8,12},{12,16},{16,20},{20,24},{24,28},{28,32},{32,36}... | collective-permute-start | bytes 12296 | tf_op jit(solution)/shard_map/ppermute | solution.py:29
  31.2 20.6 %all-gather.18.cloned.1.call-done = f32[1024,256]{1,0:T(8,128)} async-done(((f32[256,256]{1,0:T(8,128)}), f32[1024,256]{1,0:T(8,128)}) %all-gather.18.cloned.1.call-update) | async-done | bytes 1048592 | tf_op jit(solution)/shard_map/all_gather | solution.py:49
  53.7 1.3 fusion.86
  55.1 1.4 fusion.90
  56.5 2.1 fusion.94
  59.4 1.6 slice.683
  61.1 1.9 fusion.81
  70.5 1.7 fusion.109
  72.2 1.4 while.60
  73.6 1.8 all-gather.9
  77.3 11.9 %all-gather.10 = f32[4,3,256]{2,1,0:T(4,128)S(1)} all-gather(f32[1,3,256]{2,1,0:T(4,128)S(1)} %bitcast.378), channel_id=6, replica_groups=mesh['strip_0'=16,'strip_1'=4,'strip_2'=2,'col'=4] {'strip_1'}, dimensions={0}, use_global_device_ids=true | all-gather | bytes 15360 | tf_op jit(solution)/shard_map/all_gather | solution.py:49
  90.5 1.3 convolution_add_fusion.38
  91.8 1.3 convolution_add_fusion.37
  93.0 1.3 convolution_add_fusion.36
  94.4 30.6 %all-gather.11 = f32[16,3,256]{2,1,0:T(4,128)S(1)} all-gather(f32[1,3,256]{2,1,0:T(4,128)S(1)} %bitcast.375), channel_id=7, replica_groups=mesh['strip_0'=16,'strip_1'=4,'strip_2'=2,'col'=4] {'strip_0'}, dimensions={0}, use_global_device_ids=true | all-gather | bytes 52224 | tf_op jit(solution)/shard_map/all_gather | solution.py:49
  127.1 11.4 %all-gather.20.cloned.1.call-done = f32[4096,256]{1,0:T(8,128)} async-done(((f32[256,256]{1,0:T(8,128)}), f32[4096,256]{1,0:T(8,128)}) %all-gather.20.cloned.1.call-update) | async-done | bytes 4194320 | tf_op jit(solution)/shard_map/all_gather | solution.py:49
  139.8 1.3 convolution_add_fusion.35
  142.3 1.3 convolution_add_fusion.33
  143.6 1.3 convolution_add_fusion.32
  144.9 1.3 convolution_add_fusion.31
  146.2 1.3 convolution_add_fusion.30
  147.4 1.3 convolution_add_fusion.29
  148.7 1.3 convolution_add_fusion.28
  150.0 1.3 convolution_add_fusion.27
  151.3 1.3 convolution_add_fusion.26
  152.5 1.3 convolution_add_fusion.25
  153.8 1.3 convolution_add_fusion.24
  155.1 1.3 convolution_add_fusion.23
  156.4 1.3 convolution_add_fusion.22
  157.6 1.3 fusion.33
  159.6 6.6 %while.58 = (s32[]{:T(128)}, f32[3,256]{1,0:T(4,128)S(1)}, f32[4,3,512]{2,1,0:T(4,128)S(1)}, f32[4,1,256]{2,1,0:T(1,128)S(1)}, f32[4,3,512]{2,1,0:T(4,128)S(1)}, /*index=5*/f32[4,512,256]{2,1,0:T(8,128)}, s32[]{:T(128)}) while((s32[]{:T(128)}, f32[3,256]{1,0:T(4,128)S(1)}, f32[4,3,512]{2,1,0:T(4,128)S(1)}, f32[4,1,256]{2,1,0:T(1,128)S(1)}, ...), condition=%wide.region_11.12_spmd, body=%wide.region_10.11_spmd.sunk | while | flops 4720898 | bytes 563289 | solution.py:208
  159.6 1.6 bitcast_dynamic-update-slice_fusion.4
  161.3 1.6 bitcast_dynamic-update-slice_fusion.4
  162.9 1.6 bitcast_dynamic-update-slice_fusion.4
  164.6 1.6 bitcast_dynamic-update-slice_fusion.4
  167.8 1.3 collective-permute-start.5
  169.1 4.5 %collective-permute-start.6 = (f32[3,8,2]{2,1,0:T(8,128)S(1)}, f32[3,8,2]{2,1,0:T(8,128)S(1)}, u32[]{:S(2)}, u32[]{:S(2)}) collective-permute-start(f32[3,8,2]{2,1,0:T(8,128)S(1)} %get-tuple-element.362), channel_id=1, source_target_pairs={{1,0},{2,1},{3,2},{5,4},{6,5},{7,6},{9,8},{10,9},{11,10},{13,12},{... | collective-permute-start | bytes 584 | tf_op jit(solution)/shard_map/ppermute | solution.py:31
  173.7 1.3 collective-permute-start.7
  175.0 3.2 %collective-permute-start.8 = (f32[4,1,256]{2,1,0:T(1,128)S(1)}, f32[4,1,256]{2,1,0:T(1,128)S(1)}, u32[]{:S(2)}, u32[]{:S(2)}) collective-permute-start(f32[4,1,256]{2,1,0:T(1,128)S(1)} %get-tuple-element.353), channel_id=1, source_target_pairs={{0,4},{4,8},{8,12},{12,16},{16,20},{20,24},{24,28},{28,32},{32,36}... | collective-permute-start | bytes 12296 | tf_op jit(solution)/shard_map/ppermute | solution.py:29
  184.7 1.7 fusion.107
  186.5 1.4 while.61
  187.9 2.5 all-gather.12
  191.6 12.0 %all-gather.13 = f32[4,3,256]{2,1,0:T(4,128)S(1)} all-gather(f32[1,3,256]{2,1,0:T(4,128)S(1)} %bitcast.377), channel_id=9, replica_groups=mesh['strip_0'=16,'strip_1'=4,'strip_2'=2,'col'=4] {'strip_1'}, dimensions={0}, use_global_device_ids=true | all-gather | bytes 15360 | tf_op jit(solution)/shard_map/all_gather | solution.py:49
  206.1 1.3 convolution_add_fusion.16
  207.7 28.8 %all-gather.14 = f32[16,3,256]{2,1,0:T(4,128)S(1)} all-gather(f32[1,3,256]{2,1,0:T(4,128)S(1)} %bitcast.374), channel_id=10, replica_groups=mesh['strip_0'=16,'strip_1'=4,'strip_2'=2,'col'=4] {'strip_0'}, dimensions={0}, use_global_device_ids=true | all-gather | bytes 52224 | tf_op jit(solution)/shard_map/all_gather | solution.py:49
  239.0 1.3 convolution_add_fusion.13
  240.3 1.3 convolution_add_fusion.12
  241.6 1.3 convolution_add_fusion.11
  242.9 1.3 convolution_add_fusion.10
  244.1 1.3 convolution_add_fusion.9
  245.4 1.3 convolution_add_fusion.8
  254.3 1.3 fusion.31
  256.3 6.6 %while.59 = (s32[]{:T(128)}, f32[3,256]{1,0:T(4,128)S(1)}, f32[4,3,512]{2,1,0:T(4,128)S(1)}, f32[4,1,256]{2,1,0:T(1,128)S(1)}, f32[4,3,512]{2,1,0:T(4,128)S(1)}, /*index=5*/f32[4,512,256]{2,1,0:T(8,128)}, s32[]{:T(128)}) while((s32[]{:T(128)}, f32[3,256]{1,0:T(4,128)S(1)}, f32[4,3,512]{2,1,0:T(4,128)S(1)}, f32[4,1,256]{2,1,0:T(1,128)S(1)}, ...), condition=%wide.region_20.21_spmd, body=%wide.region_19.20_spmd.sunk | while | flops 4720898 | bytes 563289 | solution.py:208
  256.3 1.6 bitcast_dynamic-update-slice_fusion.5
  257.9 1.6 bitcast_dynamic-update-slice_fusion.5
  259.6 1.6 bitcast_dynamic-update-slice_fusion.5
  261.2 1.6 bitcast_dynamic-update-slice_fusion.5
  (217 shorter events, 52.3 us)
Async XLA Ops:
  6.5 45.3 %all-gather.18.cloned.1.call-start = ((), (), s32[]{:S(2)}) async-start(), calls=%async_computation | async-start | bytes 1310720 | tf_op jit(solution)/shard_map/all_gather | solution.py:49
  7.4 53.7 %copy-start.11 = (f32[8,256]{1,0:T(8,128)}, f32[8,256]{1,0:T(8,128)S(1)}, u32[]{:S(2)}) copy-start(f32[8,256]{1,0:T(8,128)S(1)} %bitcast_select_fusion) | copy-start | bytes 24580
  9.8 6.1 %copy-start.2 = (f32[3,8,256]{2,1,0:T(8,128)S(1)}, f32[3,8,256]{2,1,0:T(8,128)}, u32[]{:S(2)}) copy-start(f32[3,8,256]{2,1,0:T(8,128)} %param.28) | copy-start | bytes 73732
  9.8 12.6 %copy-start.9 = (f32[3,8,256]{2,1,0:T(8,128)S(1)}, f32[3,8,256]{2,1,0:T(8,128)}, u32[]{:S(2)}) copy-start(f32[3,8,256]{2,1,0:T(8,128)} %param.31) | copy-start | bytes 73732
  9.8 20.2 %copy-start.27 = (s32[64]{0:T(128)S(1)}, s32[64]{0:T(128)}, u32[]{:S(2)}) copy-start(s32[64]{0:T(128)} %param.32) | copy-start | bytes 772
  9.8 20.3 %copy-start.20 = (f32[3]{0:T(128)S(1)}, f32[3]{0:T(128)}, u32[]{:S(2)}) copy-start(f32[3]{0:T(128)} %constant.208.clone) | copy-start | bytes 40
  11.5 47.8 %copy-start = (bf16[4,512,512]{2,1,0:T(8,128)(2,1)S(1)}, bf16[4,512,512]{2,1,0:T(8,128)(2,1)}, u32[]{:S(2)}) copy-start(bf16[4,512,512]{2,1,0:T(8,128)(2,1)} %param.33) | copy-start | bytes 6291460
  13.9 0.8 copy-start.1
  14.7 37.1 %copy-start.5 = (f32[256,256]{1,0:T(8,128)}, f32[256,256]{1,0:T(8,128)S(1)}, u32[]{:S(2)}) copy-start(f32[256,256]{1,0:T(8,128)S(1)} %fusion.45) | copy-start | bytes 786436
  15.8 122.7 %all-gather.20.cloned.1.call-start = ((), (), s32[]{:S(2)}) async-start(), calls=%async_computation.1 | async-start | bytes 4456448 | tf_op jit(solution)/shard_map/all_gather | solution.py:49
  16.6 46.9 %collective-permute-start.1 = (f32[3,8,2]{2,1,0:T(8,128)}, f32[3,8,2]{2,1,0:T(8,128)S(1)}, u32[]{:S(2)}, u32[]{:S(2)}) collective-permute-start(f32[3,8,2]{2,1,0:T(8,128)} %get-tuple-element.367), channel_id=1, source_target_pairs={{0,1},{1,2},{2,3},{4,5},{5,6},{6,7},{8,9},{9,10},{10,11},{12,13},{... | collective-permute-start | bytes 584 | tf_op jit(solution)/shard_map/ppermute | solution.py:29
  17.9 45.6 %collective-permute-start.2 = (f32[3,8,2]{2,1,0:T(8,128)}, f32[3,8,2]{2,1,0:T(8,128)S(1)}, u32[]{:S(2)}, u32[]{:S(2)}) collective-permute-start(f32[3,8,2]{2,1,0:T(8,128)} %get-tuple-element.366), channel_id=1, source_target_pairs={{1,0},{2,1},{3,2},{5,4},{6,5},{7,6},{9,8},{10,9},{11,10},{13,12},{... | collective-permute-start | bytes 584 | tf_op jit(solution)/shard_map/ppermute | solution.py:31
  22.5 42.6 %collective-permute-start = (f32[3,8,2]{2,1,0:T(8,128)S(1)}, f32[3,8,2]{2,1,0:T(8,128)S(1)}, u32[]{:S(2)}, u32[]{:S(2)}) collective-permute-start(f32[3,8,2]{2,1,0:T(8,128)S(1)} %slice.413), channel_id=1, source_target_pairs={{0,1},{1,2},{2,3},{4,5},{5,6},{6,7},{8,9},{9,10},{10,11},{12,13},{... | collective-permute-start | bytes 584 | tf_op jit(solution)/shard_map/ppermute | solution.py:18
  24.5 34.2 %copy-start.16 = (f32[1,8,256]{2,1,0:T(8,128)}, f32[1,8,256]{2,1,0:T(8,128)S(1)}, u32[]{:S(2)}) copy-start(f32[1,8,256]{2,1,0:T(8,128)S(1)} %get-tuple-element.320) | copy-start | bytes 24580
  25.1 42.9 %collective-permute-start.3 = (f32[4,1,256]{2,1,0:T(1,128)}, f32[4,1,256]{2,1,0:T(1,128)}, u32[]{:S(2)}, u32[]{:S(2)}) collective-permute-start(f32[4,1,256]{2,1,0:T(1,128)} %get-tuple-element.356), channel_id=1, source_target_pairs={{4,0},{8,4},{12,8},{16,12},{20,16},{24,20},{28,24},{32,28},{36,32}... | collective-permute-start | bytes 12296 | tf_op jit(solution)/shard_map/ppermute | solution.py:31
  26.4 41.0 %collective-permute-start.4 = (f32[4,1,256]{2,1,0:T(1,128)}, f32[4,1,256]{2,1,0:T(1,128)}, u32[]{:S(2)}, u32[]{:S(2)}) collective-permute-start(f32[4,1,256]{2,1,0:T(1,128)} %get-tuple-element.355), channel_id=1, source_target_pairs={{0,4},{4,8},{8,12},{12,16},{16,20},{20,24},{24,28},{28,32},{32,36}... | collective-permute-start | bytes 12296 | tf_op jit(solution)/shard_map/ppermute | solution.py:29
  53.1 0.7 copy-start.6
  55.1 3.7 %copy-start.3 = (f32[256,256]{1,0:T(8,128)}, f32[256,256]{1,0:T(8,128)S(1)}, u32[]{:S(2)}) copy-start(f32[256,256]{1,0:T(8,128)S(1)} %fusion.86) | copy-start | bytes 786436
  55.1 6.0 %copy-start.25 = (f32[3]{0:T(128)S(1)}, f32[3]{0:T(128)}, u32[]{:S(2)}) copy-start(f32[3]{0:T(128)} %constant.266) | copy-start | bytes 40
  56.5 2.2 copy-start.4
  65.8 28.6 %copy-start.10 = (f32[8,259]{1,0:T(8,128)}, f32[8,259]{1,0:T(8,128)S(1)}, u32[]{:S(2)}) copy-start(f32[8,259]{1,0:T(8,128)S(1)} %get-tuple-element.332) | copy-start | bytes 24868
  68.8 1.7 copy-start.19
  75.4 18.9 %copy-start.21 = (f32[2,3,256]{2,1,0:T(4,128)}, f32[2,3,256]{2,1,0:T(4,128)S(1)}, u32[]{:S(2)}) copy-start(f32[2,3,256]{2,1,0:T(4,128)S(1)} %all-gather.9) | copy-start | bytes 18436
  76.7 0.7 copy-start.23
  90.5 36.6 %copy-start.14 = (f32[3,256]{1,0:T(4,128)}, f32[3,256]{1,0:T(4,128)S(1)}, u32[]{:S(2)}) copy-start(f32[3,256]{1,0:T(4,128)S(1)} %fusion.78) | copy-start | bytes 9220
  138.5 20.5 %copy-start.7 = (f32[256,256]{1,0:T(8,128)S(1)}, f32[256,256]{1,0:T(8,128)}, u32[]{:S(2)}) copy-start(f32[256,256]{1,0:T(8,128)} %fusion.36) | copy-start | bytes 786436
  138.5 20.7 %copy-start.17 = (f32[3,256]{1,0:T(4,128)S(1)}, f32[3,256]{1,0:T(4,128)}, u32[]{:S(2)}) copy-start(f32[3,256]{1,0:T(4,128)} %fusion.81) | copy-start | bytes 9220
  138.5 20.8 %copy-start.22 = (f32[2,3,256]{2,1,0:T(4,128)S(1)}, f32[2,3,256]{2,1,0:T(4,128)}, u32[]{:S(2)}) copy-start(f32[2,3,256]{2,1,0:T(4,128)} %copy-done.21) | copy-start | bytes 18436
  138.5 20.8 %copy-start.24 = (f32[3,256]{1,0:T(4,128)S(1)}, f32[3,256]{1,0:T(4,128)}, u32[]{:S(2)}) copy-start(f32[3,256]{1,0:T(4,128)} %copy-done.23) | copy-start | bytes 9220
  138.5 20.8 %copy-start.26 = (f32[3,256]{1,0:T(4,128)S(1)}, f32[3,256]{1,0:T(4,128)}, u32[]{:S(2)}) copy-start(f32[3,256]{1,0:T(4,128)} %fusion.148) | copy-start | bytes 9220
  139.8 26.4 %copy-start.12 = (f32[3,256]{1,0:T(4,128)}, f32[3,256]{1,0:T(4,128)S(1)}, u32[]{:S(2)}) copy-start(f32[3,256]{1,0:T(4,128)S(1)} %fusion.34) | copy-start | bytes 9220
  159.6 30.8 %copy-start.18 = (f32[3,256]{1,0:T(4,128)S(1)}, f32[3,256]{1,0:T(4,128)}, u32[]{:S(2)}) copy-start(f32[3,256]{1,0:T(4,128)} %fusion.81) | copy-start | bytes 9220
  159.6 44.0 %copy-start.15 = (f32[3,256]{1,0:T(4,128)S(1)}, f32[3,256]{1,0:T(4,128)}, u32[]{:S(2)}) copy-start(f32[3,256]{1,0:T(4,128)} %copy-done.14) | copy-start | bytes 9220
  166.2 70.3 %copy-start.13 = (f32[3,256]{1,0:T(4,128)S(1)}, f32[3,256]{1,0:T(4,128)}, u32[]{:S(2)}) copy-start(f32[3,256]{1,0:T(4,128)} %copy-done.12) | copy-start | bytes 9220
  167.8 11.2 %collective-permute-start.5 = (f32[3,8,2]{2,1,0:T(8,128)S(1)}, f32[3,8,2]{2,1,0:T(8,128)S(1)}, u32[]{:S(2)}, u32[]{:S(2)}) collective-permute-start(f32[3,8,2]{2,1,0:T(8,128)S(1)} %get-tuple-element.363), channel_id=1, source_target_pairs={{0,1},{1,2},{2,3},{4,5},{5,6},{6,7},{8,9},{9,10},{10,11},{12,13},{... | collective-permute-start | bytes 584 | tf_op jit(solution)/shard_map/ppermute | solution.py:29
  169.1 9.9 %collective-permute-start.6 = (f32[3,8,2]{2,1,0:T(8,128)S(1)}, f32[3,8,2]{2,1,0:T(8,128)S(1)}, u32[]{:S(2)}, u32[]{:S(2)}) collective-permute-start(f32[3,8,2]{2,1,0:T(8,128)S(1)} %get-tuple-element.362), channel_id=1, source_target_pairs={{1,0},{2,1},{3,2},{5,4},{6,5},{7,6},{9,8},{10,9},{11,10},{13,12},{... | collective-permute-start | bytes 584 | tf_op jit(solution)/shard_map/ppermute | solution.py:31
  173.7 8.6 %collective-permute-start.7 = (f32[4,1,256]{2,1,0:T(1,128)S(1)}, f32[4,1,256]{2,1,0:T(1,128)S(1)}, u32[]{:S(2)}, u32[]{:S(2)}) collective-permute-start(f32[4,1,256]{2,1,0:T(1,128)S(1)} %get-tuple-element.354), channel_id=1, source_target_pairs={{4,0},{8,4},{12,8},{16,12},{20,16},{24,20},{28,24},{32,28},{36,32}... | collective-permute-start | bytes 12296 | tf_op jit(solution)/shard_map/ppermute | solution.py:31
  175.0 7.3 %collective-permute-start.8 = (f32[4,1,256]{2,1,0:T(1,128)S(1)}, f32[4,1,256]{2,1,0:T(1,128)S(1)}, u32[]{:S(2)}, u32[]{:S(2)}) collective-permute-start(f32[4,1,256]{2,1,0:T(1,128)S(1)} %get-tuple-element.353), channel_id=1, source_target_pairs={{0,4},{4,8},{8,12},{12,16},{16,20},{20,24},{24,28},{28,32},{32,36}... | collective-permute-start | bytes 12296 | tf_op jit(solution)/shard_map/ppermute | solution.py:29
  186.4 69.2 %copy-start.8 = (f32[256,256]{1,0:T(8,128)S(1)}, f32[256,256]{1,0:T(8,128)}, u32[]{:S(2)}) copy-start(f32[256,256]{1,0:T(8,128)} %fusion.36) | copy-start | bytes 786436
Sparse Core Ops, SparseCore 0:
  16.0 35.8 all-gather.17
  58.8 79.6 all-gather.19
where the time goes:
time: 273 us; the launch traced here: 270 us
  blocking collectives  90.1 us (33%)
  matrix products  83.7 us (31%)
  waiting for transfers between devices  32.1 us (12%)
  starting transfers between devices  22.4 us (8%)
  other arithmetic  19.9 us (7%)
  between operations  14.2 us (5%)
  local copies, waits for them, and re-layouts  7.1 us (3%)
    all_gather x7, blocking collectives, prefix_by_axis(): pieces = jax.tree.map(lambda part: lax.all_gather(part, axis), so_far)  90.1 us
    dot_general x63, matrix products, times_transposed(): lax.dot_general(rows_in, matrix, (((rows_in.ndim - 1,), (1,)), ((), ())),...  69.7 us
    all_gather x2, waiting for transfers between devices, prefix_by_axis(): pieces = jax.tree.map(lambda part: lax.all_gather(part, axis), so_far)  32 us
    ppermute x4, starting transfers between devices, extended(): lax.ppermute(head, axis, [((i + 1) % count, i) for i in range(ends)])  11.7 us
    dot_general x12, matrix products, matmul(): jnp.dot(left_side, right_side, precision=highest, preferred_element_type=...  10.5 us
    ppermute x4, starting transfers between devices, extended(): lax.ppermute(tail, axis, [(i, (i + 1) % count) for i in range(ends)])  9.39 us
  transfers between devices with their start and end apart: 11, of which 2 were waited for; matrix products, arithmetic and copies ran while one was open for 13% of the time, Pallas kernels for 0%

commit v1 on v0

v1 whole, which is shorter than its diff:
```python
import jax
import jax.numpy as jnp
from jax import lax
from jax.experimental import pallas as pl
from jax.experimental.pallas import tpu as pltpu
from jax.sharding import Mesh
from jax.sharding import PartitionSpec as P

F32 = jnp.float32
BF16 = jnp.bfloat16
STRIP = ("zh", "zl", "x", "c")
ZAX = ("zh", "zl")
PLANE = ("x", "c")
SIDES = ("c", "y")
CB = 256
PIN = 20.0
VMEM_LIMIT = 14 * 1024 * 1024


def dot(a, b):
    return lax.dot_general(a, b, (((1,), (0,)), ((), ())), preferred_element_type=F32)


def dot_t(a, b):
    return lax.dot_general(a, b, (((1,), (1,)), ((), ())), preferred_element_type=F32)


def pair(value):
    high = value.astype(BF16)
    low = (value - high.astype(F32)).astype(BF16)
    return high, low


def mm(a, b):
    return dot(a[0], b[0]) + (dot(a[0], b[1]) + dot(a[1], b[0]))


def eye():
    rows = lax.broadcasted_iota(jnp.int32, (CB, CB), 0)
    cols = lax.broadcasted_iota(jnp.int32, (CB, CB), 1)
    return jnp.where(rows == cols, 1.0, 0.0).astype(F32)


def stacked(value):
    high = value.astype(BF16)
    low = value - high.astype(F32)
    return jnp.concatenate([high.astype(F32), low], axis=0).astype(BF16)


def halves_sum(value):
    half = value.shape[0] // 2
    return value[:half] + value[half:]


def put_vector(vec_ref, slot, value):
    high = value.astype(BF16).astype(F32)
    vec_ref[0:3, slot * CB : (slot + 1) * CB] = high
    vec_ref[8:11, slot * CB : (slot + 1) * CB] = value - high


def apply_map(vec, high, low):
    return halves_sum(dot(vec, high) + dot(vec, low))


def call(kernel, outs, args, specs=None, scratch=(), flops=10**7, size=10**6, grid=None):
    vmem = pl.BlockSpec(memory_space=pltpu.VMEM)
    in_specs = [vmem] * len(args) if specs is None else [vmem if s is None else s for s in specs]
    many = isinstance(outs, (list, tuple))
    out_specs = [vmem] * len(outs) if many else vmem
    extra = {} if grid is None else {"grid": grid}
    return pl.pallas_call(
        kernel,
        out_shape=outs,
        in_specs=in_specs,
        out_specs=out_specs,
        scratch_shapes=list(scratch),
        compiler_params=pltpu.CompilerParams(vmem_limit_bytes=VMEM_LIMIT),
        cost_estimate=pl.CostEstimate(flops=flops, bytes_accessed=size, transcendentals=0),
        **extra,
    )(*args)


def sds(shape, dtype=F32):
    return jax.ShapeDtypeStruct(shape, dtype)


def local_map_kernel(inv_ref, stiff_ref, out_ref):
    first = dot_t(eye().astype(BF16), inv_ref[0]) * stiff_ref[1, 1:2, :]
    for k in range(1, 4):
        high, low = pair(first)
        first = (dot_t(high, inv_ref[k]) + dot_t(low, inv_ref[k])) * stiff_ref[
            1, 2 * k + 1 : 2 * k + 2, :
        ]
    out_ref[...] = first


def chip_map_kernel(both_ref, out_ref):
    product = mm(pair(both_ref[0]), pair(both_ref[1]))
    for k in range(4):
        out_ref[k] = product


def plane_product_kernel(chips_ref, *rest):
    out_ref = rest[-1]
    left = mm(pair(chips_ref[0]), pair(chips_ref[1]))
    right = mm(pair(chips_ref[2]), pair(chips_ref[3]))
    out_ref[...] = mm(pair(left), pair(right))


def low_bit():
    return lax.rem(lax.axis_index("zl"), 2)


def high_bit():
    return lax.div(lax.axis_index("zl"), 2)


def two_planes_kernel(own_ref, other_ref, *rest):
    out_ref = rest[-1]
    right = low_bit() == 1
    left_map = jnp.where(right, other_ref[...], own_ref[...])
    right_map = jnp.where(right, own_ref[...], other_ref[...])
    out_ref[...] = mm(pair(left_map), pair(right_map))


def four_planes_kernel(own_ref, other_ref, *rest):
    out_ref = rest[-1]
    right = high_bit() == 1
    start = pl.multiple_of(lax.axis_index("c") * 128, 128)
    own, other = own_ref[pl.ds(start, 128), :], other_ref[pl.ds(start, 128), :]
    left_map = jnp.where(right, other, own)
    right_map = jnp.where(right, own_ref[...], other_ref[...])
    out_ref[...] = mm(pair(left_map), pair(right_map))


def plane_maps_kernel(chips_ref, cores_ref, after_ref, wh_ref, wl_ref, eh_ref, el_ref, suf_ref, cur_ref):
    x = lax.axis_index("x")
    core = lax.axis_index("c")
    one = eye()
    chips = [pair(chips_ref[k]) for k in range(4)]

    def store(slot, col, value):
        high, low = pair(value)
        wh_ref[slot * CB : (slot + 1) * CB, col * CB : (col + 1) * CB] = high
        wl_ref[slot * CB : (slot + 1) * CB, col * CB : (col + 1) * CB] = low

    suffix = one
    suf_ref[3] = suffix
    store(3, 0, suffix)
    for k in (2, 1, 0):
        if k == 2:
            suffix = chips_ref[3]
        else:
            suffix = mm(chips[k + 1], pair(suffix))
        suf_ref[k] = suffix
        store(k, 0, suffix)
    store(4, 0, mm(pair(cores_ref[1]), pair(suf_ref[x])))
    store(4, 1, jnp.where(core == 1, one, 0.0))
    cur_ref[...] = jnp.where(core == 1, cores_ref[0], one)
    for k in (3, 2, 1, 0):

        @pl.when(k < x)
        def _():
            current = cur_ref[...]
            store(k, 1, current)
            cur_ref[...] = mm(chips[k], pair(current))

        @pl.when(k >= x)
        def _():
            store(k, 1, jnp.zeros((CB, CB), F32))

    high, low = pair(cur_ref[...])
    eh_ref[...] = high
    el_ref[...] = low


def group_maps_kernel(one_ref, two_ref, after_ref, out_ref, s_ref, e_ref):
    one = eye()
    sibling = one_ref[...]
    two = pair(two_ref[...])
    send = jnp.where(low_bit() == 0, sibling, one)
    take = jnp.where(low_bit() == 1, sibling, one)
    for k, value in ((0, send), (4, take)):
        parts = pair(value)
        out_ref[k] = parts[0]
        out_ref[k + 1] = parts[1]
    send = jnp.where(high_bit() == 0, mm(pair(send), two), send)
    take = jnp.where(high_bit() == 1, mm(two, pair(take)), take)
    for k, value in ((2, send), (6, take)):
        parts = pair(value)
        out_ref[k] = parts[0]
        out_ref[k + 1] = parts[1]
    s_ref[...] = send
    e_ref[...] = take


def joint_map(far_ref, s_ref, e_ref, out_ref):
    zh = lax.axis_index("zh")
    far = jnp.concatenate([far_ref[0], far_ref[1]], axis=0)
    left = jnp.where(zh == 0, s_ref[...], far)
    right = jnp.where(zh == 0, far, e_ref[...])
    joint = pair(mm(pair(left), pair(right)))
    out_ref[0] = joint[0]
    out_ref[1] = joint[1]


def edge_tiles(comps, weights):
    lane = lax.broadcasted_iota(jnp.int32, (8, 128), 1)
    right = jnp.zeros((8, 128), F32)
    left = jnp.zeros((8, 128), F32)
    for k, value in enumerate(comps + weights):
        mask = (lane == 2 * k) | (lane == 2 * k + 1)
        right = jnp.where(mask, pltpu.roll(value[:, 128:], (2 * k - 126) % 128, 1), right)
        if k < 3:
            left = jnp.where(mask, pltpu.roll(value[:, :128], 2 * k, 1), left)
    return left, right


def put_rows(out_ref, index, rows):
    for k in range(len(rows)):
        for h in range(2):
            spot = (slice(2 * k + h, 2 * k + h + 1), slice(None))
            out_ref[index + spot] = rows[k][:, 128 * h : 128 * (h + 1)]


def halo_kernel(u_ref, stiff_ref, after_ref, left_ref, right_ref, near_ref, cross_ref):
    core = lax.axis_index("c")
    comps = [u_ref[k] for k in range(3)]
    left, right = edge_tiles(comps, [stiff_ref[0], stiff_ref[2]])
    left_ref[...] = left
    right_ref[...] = right
    rows = comps + [stiff_ref[1]]
    put_rows(near_ref, (), [jnp.where(core == 0, r[7:8], r[0:1]) for r in rows])
    put_rows(cross_ref, (), [jnp.where(core == 0, r[0:1], r[7:8]) for r in rows])


def write_halos(comps, side_ref, row_ref):
    core = lax.axis_index("c")
    y = lax.axis_index("y")
    left, right = edge_tiles(comps, [])
    for j in range(8):
        side_ref[j] = jnp.zeros((8, 128), F32)
    side_ref[core * 4 + lax.rem(y + 1, 4)] = right
    side_ref[core * 4 + lax.rem(y + 3, 4)] = left
    rows = [c[0:1] for c in comps] + [jnp.zeros((1, CB), F32)]
    put_rows(side_ref, ((1 - core) * 4 + y,), rows)
    put_rows(row_ref, (), rows)


def row_of(tile, k):
    return jnp.concatenate([tile[2 * k : 2 * k + 1], tile[2 * k + 1 : 2 * k + 2]], axis=1)


def springs(ends, others, weight, rest, length):
    gaps = [o - e for o, e in zip(others, ends)]
    gaps = [g + r if r != 0.0 else g for g, r in zip(gaps, rest)]
    norm = jnp.sqrt(gaps[0] * gaps[0] + gaps[1] * gaps[1] + gaps[2] * gaps[2])
    factor = length / jnp.maximum(norm, 0.5 * length)
    return [weight * (g * factor - r if r != 0.0 else g * factor) for g, r in zip(gaps, rest)]


def solve_right_side(
    comps, inertial, from_left, from_right, below_rows, above_rows, above_weight, h_ext, b_ext,
    vertical, stiff_ref, inv_ref, base_ref,
):
    row = lax.broadcasted_iota(jnp.int32, (8, CB), 0)
    lane = lax.broadcasted_iota(jnp.int32, (8, 512), 1)
    wide = []
    for k in range(3):
        head = pltpu.roll(from_left, 126 - 2 * k, 1)
        tail = pltpu.roll(from_right, (-2 * k) % 128, 1) if k else from_right
        wide.append(jnp.concatenate([head, comps[k], tail], axis=1))
    total = [jnp.zeros((8, 512), F32)] * 3
    for offset, weight in ((1, h_ext), (2, b_ext)):
        shifted = [pltpu.roll(w, 512 - offset, 1) for w in wide]
        rest = (float(offset), 0.0, 0.0)
        pulls = springs(wide, shifted, weight, rest, float(offset))
        crossing = ((lane >= 128 - offset) & (lane < 128)) | (
            (lane >= 384 - offset) & (lane < 384)
        )
        across = jnp.where(crossing, weight, 0.0)
        for k in range(3):
            here = across * shifted[k] - pulls[k]
            there = across * wide[k] + pulls[k]
            total[k] = total[k] + here + pltpu.roll(there, offset, 1)
    lower = [
        jnp.where(row == 7, below_rows[k], pltpu.roll(comps[k], 7, 0)) for k in range(3)
    ]
    down = springs(comps, lower, vertical, (0.0, 1.0, 0.0), 1.0)
    upper = springs(
        above_rows, [c[0:1] for c in comps], above_weight, (0.0, 1.0, 0.0), 1.0
    )
    below_weight = jnp.where(lax.rem(row, 2) == 1, vertical, 0.0)
    rhs = []
    for k in range(3):
        received = jnp.where(row == 0, upper[k], pltpu.roll(down[k], 1, 0))
        rhs.append(
            inertial[k] + total[k][:, 128:384] + received - down[k] + below_weight * lower[k]
        )
    first = jnp.concatenate(rhs + [jnp.zeros((8, CB), F32)], axis=0)
    second = jnp.concatenate(
        [pltpu.roll(r, 7, 0) for r in rhs] + [jnp.zeros((8, CB), F32)], axis=0
    )
    wide_rhs = stacked(jnp.concatenate([first, second], axis=1))
    base = [jnp.zeros((8, CB), F32)] * 3
    for k in range(4):
        solved = halves_sum(dot_t(wide_rhs, inv_ref[k]))
        for j in range(3):
            part = solved[8 * j : 8 * j + 8]
            base[j] = jnp.where(
                row == 2 * k,
                part[:, :CB],
                jnp.where(row == 2 * k + 1, pltpu.roll(part[:, CB:], 1, 0), base[j]),
            )
    for j in range(3):
        base_ref[j] = base[j]
    weights = stiff_ref[1]
    last = base
    for k in range(1, 4):
        carried = jnp.concatenate(
            [weights * last[j] for j in range(3)] + [jnp.zeros((8, CB), F32)], axis=0
        )
        moved = halves_sum(dot_t(stacked(carried), inv_ref[k, CB:, :CB]))
        last = [
            jnp.where(row == 2 * k + 1, base[j] + pltpu.roll(moved[8 * j : 8 * j + 8], 2, 0), last[j])
            for j in range(3)
        ]
    rows = [(weights * last[j])[7:8] for j in range(3)]
    return jnp.concatenate(rows + [jnp.zeros((5, CB), F32)], axis=0)


def write_offsets(offset, chip_ref, msg_ref):
    core = lax.axis_index("c")
    x = lax.axis_index("x")
    chip = pair(chip_ref[1])
    onward = apply_map(stacked(offset), chip[0], chip[1])[0:3]
    raw = offset[0:3]
    onward = jnp.where(core == 0, onward, raw)
    for j in range(8):
        msg_ref[j] = jnp.where(x == j // 2, raw, onward)


def offsets_kernel(offset_ref, chip_ref, after_ref, msg_ref):
    write_offsets(offset_ref[...], chip_ref, msg_ref)


def first_side_kernel(
    u_ref, target_ref, inertia_ref, stiff_ref, pin_ref, left_ref, right_ref, near_ref, cross_ref,
    inv_ref, after_ref, base_ref, offset_ref, inertial_ref, ext_ref, above_ref,
):
    core = lax.axis_index("c")
    y = lax.axis_index("y")
    strip = (lax.axis_index("zh") * 4 + lax.axis_index("zl")) * 8 + lax.axis_index("x") * 2 + core
    comps = [u_ref[k] for k in range(3)]
    row = lax.broadcasted_iota(jnp.int32, (8, CB), 0)
    column = lax.broadcasted_iota(jnp.int32, (8, CB), 1) + y * CB
    hit = column < 0
    for k in range(pin_ref.shape[0]):
        hit = hit | (column == pin_ref[k])
    pinned = hit & (row == 0) & (strip == 0)
    inertial = []
    for k in range(3):
        value = inertia_ref[...] * target_ref[k] + PIN * jnp.where(pinned, comps[k], 0.0)
        inertial.append(value)
        inertial_ref[k] = value
    lane = lax.broadcasted_iota(jnp.int32, (8, 512), 1)
    from_left = left_ref[...]
    extended = []
    for k, channel, offset in ((3, 0, 1), (4, 2, 2)):
        head = pltpu.roll(from_left, 126 - 2 * k, 1)
        weight = jnp.concatenate([head, stiff_ref[channel], jnp.zeros((8, 128), F32)], axis=1)
        low = jnp.where(y == 0, 128, 128 - offset)
        high = jnp.where(y == 3, 384 - offset, 384)
        weight = jnp.where((lane >= low) & (lane < high), weight, 0.0)
        extended.append(weight)
        ext_ref[k - 3] = weight
    above = jnp.where(core == 0, cross_ref[...], near_ref[...])
    below = jnp.where(core == 0, near_ref[...], cross_ref[...])
    above_weight = jnp.where(strip == 0, 0.0, row_of(above, 3))
    above_ref[...] = jnp.broadcast_to(above_weight, (8, CB))
    vertical = jnp.where((row == 7) & (strip == 127), 0.0, stiff_ref[1])
    offset_ref[...] = solve_right_side(
        comps, inertial, from_left, right_ref[...], [row_of(below, k) for k in range(3)],
        [row_of(above, k) for k in range(3)], above_weight, extended[0], extended[1], vertical,
        stiff_ref, inv_ref, base_ref,
    )


def second_side_kernel(
    u_ref, stiff_ref, side_ref, row_ref, inv_ref, chip_ref, inertial_ref, ext_ref, above_ref,
    base_ref, msg_ref,
):
    core = lax.axis_index("c")
    y = lax.axis_index("y")
    strip = (lax.axis_index("zh") * 4 + lax.axis_index("zl")) * 8 + lax.axis_index("x") * 2 + core
    comps = [u_ref[k] for k in range(3)]
    row = lax.broadcasted_iota(jnp.int32, (8, CB), 0)
    partner = side_ref[(1 - core) * 4 + y]
    below = jnp.where(core == 0, partner, row_ref[...])
    above_weight = above_ref[0:1, :]
    divisor = jnp.where(strip == 0, 1.0, above_weight)
    above_rows = [u_ref[3, k : k + 1, :] / divisor for k in range(3)]
    vertical = jnp.where((row == 7) & (strip == 127), 0.0, stiff_ref[1])
    from_left = side_ref[core * 4 + lax.rem(y + 3, 4)]
    from_right = side_ref[core * 4 + lax.rem(y + 1, 4)]
    offset = solve_right_side(
        comps, [inertial_ref[k] for k in range(3)], from_left, from_right,
        [row_of(below, k) for k in range(3)], above_rows, above_weight, ext_ref[0], ext_ref[1],
        vertical, stiff_ref, inv_ref, base_ref,
    )
    write_offsets(offset, chip_ref, msg_ref)


def plane_vectors(got_ref, wh_ref, wl_ref, vec_ref):
    x = lax.axis_index("x")
    vec_ref[...] = jnp.zeros(vec_ref.shape, F32)
    for k in range(4):
        own = got_ref[2 * k + 1]
        put_vector(vec_ref, k, jnp.where(x == k, own, own + got_ref[2 * k]))
    put_vector(vec_ref, 4, got_ref[2 * x])
    return apply_map(vec_ref[...].astype(BF16), wh_ref[...], wl_ref[...])


def send_vectors(total, maps_ref, joint_ref, msg_ref):
    zh = lax.axis_index("zh")
    vec = stacked(total)
    pairs = apply_map(vec, maps_ref[0], maps_ref[1])[0:3]
    near = apply_map(vec, maps_ref[2], maps_ref[3])[0:3]
    far = apply_map(vec, joint_ref[0], joint_ref[1])[0:3]
    far = jnp.where(zh == 0, far, near)
    raw = total[0:3]
    for g in range(4):
        for h in range(2):
            inner = jnp.where(high_bit() == h, raw, pairs)
            value = jnp.where(zh == g, inner, near if g < 2 else far)
            msg_ref[4 * g + 2 * h] = value
            msg_ref[4 * g + 2 * h + 1] = value


def plane_kernel(got_ref, wh_ref, wl_ref, both_ref, vec_ref):
    both_ref[...] = plane_vectors(got_ref, wh_ref, wl_ref, vec_ref)


def send_kernel(both_ref, maps_ref, far_ref, s_ref, e_ref, joint_ref, msg_ref):
    joint_map(far_ref, s_ref, e_ref, joint_ref)
    send_vectors(both_ref[:, :CB], maps_ref, joint_ref, msg_ref)


def plane_send_kernel(got_ref, wh_ref, wl_ref, maps_ref, joint_ref, both_ref, msg_ref, vec_ref):
    both = plane_vectors(got_ref, wh_ref, wl_ref, vec_ref)
    both_ref[...] = both
    send_vectors(both[:, :CB], maps_ref, joint_ref, msg_ref)


def finish(
    got_ref, both_ref, maps_ref, joint_ref, eh_ref, el_ref, stiff_ref, base_ref, inv_ref, vec_ref
):
    zh = lax.axis_index("zh")
    row = lax.broadcasted_iota(jnp.int32, (8, CB), 0)
    none = jnp.zeros((3, CB), F32)
    vec_ref[...] = jnp.zeros(vec_ref.shape, F32)
    first_two = got_ref[4 * zh] + got_ref[4 * zh + 1]
    put_vector(vec_ref, 0, jnp.where(high_bit() == 1, first_two, none))
    sums = [
        (got_ref[4 * g] + got_ref[4 * g + 1]) + (got_ref[4 * g + 2] + got_ref[4 * g + 3])
        for g in range(3)
    ]
    lower = jnp.where(zh >= 1, sums[0], none) + jnp.where(zh >= 2, sums[1], none)
    put_vector(vec_ref, 1, jnp.where(zh == 3, sums[2], lower))
    put_vector(vec_ref, 2, jnp.where(zh == 3, lower, none))
    vec = vec_ref[...].astype(BF16)
    arrived = apply_map(vec[:, :CB], maps_ref[4], maps_ref[5])
    arrived = arrived + apply_map(vec[:, CB : 2 * CB], maps_ref[6], maps_ref[7])
    arrived = arrived + apply_map(vec[:, 2 * CB :], joint_ref[0], joint_ref[1])
    beside = jnp.where(low_bit() == 1, got_ref[4 * zh + 2 * high_bit()], none)
    arrived = arrived + jnp.concatenate([beside, jnp.zeros((5, CB), F32)], axis=0)
    came = both_ref[:, CB:] + apply_map(stacked(arrived), eh_ref[...], el_ref[...])
    weights = stiff_ref[1]
    state = [base_ref[k] for k in range(3)]
    blank = jnp.zeros((8, CB), F32)
    for k in range(4):
        if k == 0:
            source = [jnp.broadcast_to(came[j : j + 1], (8, CB)) for j in range(3)]
        else:
            source = [weights * state[j] for j in range(3)]
        moved = halves_sum(dot_t(stacked(jnp.concatenate(source + [blank], axis=0)), inv_ref[k]))
        for j in range(3):
            part = moved[8 * j : 8 * j + 8]
            state[j] = state[j] + jnp.where(
                row == 2 * k,
                pltpu.roll(part[:, :CB], 1, 0),
                jnp.where(row == 2 * k + 1, pltpu.roll(part[:, CB:], 2, 0), 0.0),
            )
    return state, came


def middle_kernel(
    got_ref, both_ref, maps_ref, joint_ref, eh_ref, el_ref, stiff_ref, base_ref, inv_ref,
    u_ref, side_ref, row_ref, vec_ref,
):
    state, came = finish(
        got_ref, both_ref, maps_ref, joint_ref, eh_ref, el_ref, stiff_ref, base_ref, inv_ref, vec_ref
    )
    for k in range(3):
        u_ref[k] = state[k]
    u_ref[3] = came
    write_halos(state, side_ref, row_ref)


def final_kernel(
    got_ref, both_ref, maps_ref, joint_ref, eh_ref, el_ref, stiff_ref, base_ref, inv_ref,
    u_ref, vec_ref,
):
    state, came = finish(
        got_ref, both_ref, maps_ref, joint_ref, eh_ref, el_ref, stiff_ref, base_ref, inv_ref, vec_ref
    )
    for k in range(3):
        u_ref[k] = state[k]


def swap(value, axes):
    return lax.all_to_all(value, axes, 0, 0)


def shards(positions, target, inertia, stiffness, pin_columns, inverses):
    smem = pl.BlockSpec(memory_space=pltpu.SMEM)
    anywhere = pl.BlockSpec(memory_space=pl.ANY)
    grid = (1,)

    def full(shape):
        return pl.BlockSpec(shape, lambda i: (0,) * len(shape))

    own_map = pl.pallas_call(
        local_map_kernel,
        grid=grid,
        out_shape=sds((CB, CB)),
        in_specs=[pl.BlockSpec((4, CB, CB), lambda i: (0, 1, 0)), full((3, 8, CB))],
        out_specs=full((CB, CB)),
        compiler_params=pltpu.CompilerParams(vmem_limit_bytes=VMEM_LIMIT),
        cost_estimate=pl.CostEstimate(flops=10**8, bytes_accessed=10**6, transcendentals=0),
    )(inverses, stiffness)
    core_maps = lax.all_gather(own_map, "c")
    chip_copies = call(chip_map_kernel, sds((4, CB, CB)), (core_maps,))
    chips = swap(chip_copies, "x")

    tile = sds((8, 128))
    left, right, near, cross = call(
        halo_kernel,
        [tile] * 4,
        (positions, stiffness, chip_copies),
        specs=[None, None, anywhere],
    )
    pairs = [(2 * k + 1, 2 * k + 2) for k in range(63)]
    from_right = lax.ppermute(left, "y", [(1, 0), (2, 1), (3, 2)])
    from_left = lax.ppermute(right, "y", [(0, 1), (1, 2), (2, 3)])
    cross = lax.ppermute(cross, STRIP, pairs + [(b, a) for a, b in pairs])
    near = lax.ppermute(near, "c", [(0, 1), (1, 0)])
    halos = (from_left, from_right, near, cross)

    square = sds((CB, CB))
    plane = call(
        plane_product_kernel, square, (chips,) + halos, specs=[None] + [anywhere] * 4
    )
    beside = lax.ppermute(plane, ZAX, [(k, k ^ 1) for k in range(16)])

    field = sds((3, 8, CB))
    vector = sds((8, CB))
    base, offset, inertial, ext, above = call(
        first_side_kernel,
        [field, vector, field, sds((2, 8, 512)), vector],
        (positions, target, inertia, stiffness, pin_columns) + halos + (inverses, plane),
        specs=[None] * 4 + [smem] + [None] * 5 + [anywhere],
        flops=10**8,
        size=3 * 10**6,
    )
    wide = sds((5 * CB, 2 * CB), BF16)
    xh, xl, eh, el = call(
        plane_maps_kernel,
        [wide, wide, sds((CB, CB), BF16), sds((CB, CB), BF16)],
        (chips, core_maps, plane),
        specs=[None, None, anywhere],
        scratch=[pltpu.VMEM((4, CB, CB), F32), pltpu.VMEM((CB, CB), F32)],
        flops=10**9,
    )
    two = call(
        two_planes_kernel, square, (plane, beside, base, eh), specs=[None, None, anywhere, anywhere]
    )
    other_two = lax.ppermute(two, ZAX, [(k, k ^ 2) for k in range(16)])

    msg = call(
        offsets_kernel, sds((8, 3, CB)), (offset, core_maps, two), specs=[None, None, anywhere]
    )
    got = swap(msg, PLANE)
    both = call(
        plane_kernel,
        sds((8, 2 * CB)),
        (got, xh, xl),
        scratch=[pltpu.VMEM((16, 5 * CB), F32)],
        size=3 * 10**6,
    )
    group_half = call(
        four_planes_kernel, sds((128, CB)), (two, other_two, both), specs=[None, None, anywhere]
    )
    steps = [(4 + k, k) for k in range(4)] + [(8 + k, 12 + k) for k in range(4)]
    far_half = lax.ppermute(group_half, ZAX, steps)
    maps, send_map, take_map = call(
        group_maps_kernel,
        [sds((8, CB, CB), BF16), square, square],
        (beside, other_two, group_half),
        specs=[None, None, anywhere],
        flops=5 * 10**8,
    )
    far_parts = lax.all_gather(far_half, "c")
    joint, msg = call(
        send_kernel,
        [sds((2, CB, CB), BF16), sds((16, 3, CB))],
        (both, maps, far_parts, send_map, take_map),
    )
    got = swap(msg, ZAX)
    sizes = ((16, 3, CB), (8, 2 * CB), (8, CB, CB), (2, CB, CB), (CB, CB), (CB, CB), (3, 8, CB), (3, 8, CB))
    finish_specs = [full(s) for s in sizes] + [pl.BlockSpec((4, 2 * CB, CB), lambda i: (0, 0, 0))]
    params = pltpu.CompilerParams(vmem_limit_bytes=VMEM_LIMIT)
    cost = pl.CostEstimate(flops=10**8, bytes_accessed=4 * 10**6, transcendentals=0)
    middle, side, edge = pl.pallas_call(
        middle_kernel,
        grid=grid,
        out_shape=[sds((4, 8, CB)), sds((8, 8, 128)), tile],
        in_specs=finish_specs,
        out_specs=[full((4, 8, CB)), full((8, 8, 128)), full((8, 128))],
        scratch_shapes=[pltpu.VMEM((16, 3 * CB), F32)],
        compiler_params=params,
        cost_estimate=cost,
    )(got, both, maps, joint, eh, el, stiffness, base, inverses)

    side = swap(side, SIDES)
    edge = lax.ppermute(edge, STRIP, [(b, a) for a, b in pairs])
    base, msg = call(
        second_side_kernel,
        [field, sds((8, 3, CB))],
        (middle, stiffness, side, edge, inverses, core_maps, inertial, ext, above),
        flops=10**8,
        size=3 * 10**6,
    )
    got = swap(msg, PLANE)
    both, msg = call(
        plane_send_kernel,
        [sds((8, 2 * CB)), sds((16, 3, CB))],
        (got, xh, xl, maps, joint),
        scratch=[pltpu.VMEM((16, 5 * CB), F32)],
        size=3 * 10**6,
    )
    got = swap(msg, ZAX)
    return pl.pallas_call(
        final_kernel,
        grid=grid,
        out_shape=field,
        in_specs=finish_specs,
        out_specs=full((3, 8, CB)),
        scratch_shapes=[pltpu.VMEM((16, 3 * CB), F32)],
        compiler_params=params,
        cost_estimate=cost,
    )(got, both, maps, joint, eh, el, stiffness, base, inverses)


def solution(mesh):
    split = Mesh(mesh.devices.reshape(4, 4, 4, 2, 4), ("zh", "zl", "x", "c", "y"))
    return jax.shard_map(
        shards,
        mesh=split,
        in_specs=(
            P(None, STRIP, "y"),
            P(None, STRIP, "y"),
            P(STRIP, "y"),
            P(None, STRIP, "y"),
            P(),
            P(STRIP, None, None),
        ),
        out_specs=P(None, STRIP, "y"),
        check_vma=False,
    )
```

time: 273 us -> 149 us (0.55)
  matrix products: 83.7 us -> 0 us
  blocking collectives: 90.1 us -> 65.9 us
  other arithmetic: 19.9 us -> 0 us
  Pallas kernels: 0 us -> 16.2 us
  between operations: 14.2 us -> 0.3 us
  starting transfers between devices: 22.4 us -> 28.6 us
  waiting for transfers between devices: 32.1 us -> 28.7 us
    all_gather x7 -> x2, blocking collectives: 90.1 us -> 4.16 us  [the longest x1 2.18 us: shards(): core_maps = lax.all_gather(own_map, 'c')]
    dot_general x77 -> x0, matrix products: 83.7 us -> none  [the longest x63 69.7 us: times_transposed(): lax.dot_general(rows_in, matrix, (((rows_in.ndim - 1,), (1,)), ((), ())),...]
    all_to_all x0 -> x4, blocking collectives: none -> 61.7 us  [swap(): return lax.all_to_all(value, axes, 0, 0)]
    all_gather x2 -> x0, waiting for transfers between devices: 32 us -> none  [prefix_by_axis(): pieces = jax.tree.map(lambda part: lax.all_gather(part, axis), so_far)]
    ppermute x9 -> x8, waiting for transfers between devices: 0.02 us -> 19.3 us  [the longest x1 18.3 us: shards(): far_half = lax.ppermute(group_half, ZAX, steps)]
    pallas_call x0 -> x16, Pallas kernels: none -> 16.2 us  [the longest x13 12.8 us: call(): pl.pallas_call(kernel, out_shape=outs, in_specs=in_specs, out_specs=out_s...]
    all_to_all x0 -> x2, waiting for transfers between devices: none -> 9.33 us  [swap(): return lax.all_to_all(value, axes, 0, 0)]
    all_to_all x0 -> x2, starting transfers between devices: none -> 9.11 us  [swap(): return lax.all_to_all(value, axes, 0, 0)]
  transfers between devices with their start and end apart: 11 -> 10, of which waited for: 2 -> 5; matrix products, arithmetic and copies ran while one was open for 13% -> 0% of each run, Pallas kernels for 0% -> 4%
where the time goes in v1:
time: 149 us; the launch traced here: 148 us
  blocking collectives  65.9 us (44%)
  waiting for transfers between devices  28.7 us (19%)
  starting transfers between devices  28.6 us (19%)
  Pallas kernels  16.2 us (11%)
  local copies, waits for them, and re-layouts  8.26 us (6%)
    all_to_all x4, blocking collectives, swap(): return lax.all_to_all(value, axes, 0, 0)  61.7 us
    ppermute x1, waiting for transfers between devices, shards(): far_half = lax.ppermute(group_half, ZAX, steps)  18.3 us
    pallas_call x13, Pallas kernels, call(): pl.pallas_call(kernel, out_shape=outs, in_specs=in_specs, out_specs=out_s...  12.8 us
    all_to_all x2, waiting for transfers between devices, swap(): return lax.all_to_all(value, axes, 0, 0)  9.33 us
    all_to_all x2, starting transfers between devices, swap(): return lax.all_to_all(value, axes, 0, 0)  9.11 us
    unnamed x50, local copies, waits for them, and re-layouts  8.26 us
    ppermute x1, starting transfers between devices, shards(): other_two = lax.ppermute(two, ZAX, [(k, k ^ 2) for k in range(16)])  5.17 us
    ppermute x1, starting transfers between devices, shards(): from_right = lax.ppermute(left, 'y', [(1, 0), (2, 1), (3, 2)])  4.55 us
  transfers between devices with their start and end apart: 10, of which 5 were waited for; matrix products, arithmetic and copies ran while one was open for 0% of the time, Pallas kernels for 4%

profile of v1, /device:TPU:24, one launch (start us, length us, event | category | flops | bytes accessed | tf_op | source)
XLA Modules:
  0.0 147.9 jit_solution(11055590672465884718)
XLA Ops:
  0.0 1.6 %copy-done = bf16[4,512,512]{2,1,0:T(8,128)(2,1)S(1)} copy-done((bf16[4,512,512]{2,1,0:T(8,128)(2,1)S(1)}, bf16[4,512,512]{2,1,0:T(8,128)(2,1)}, u32[]{:S(2)}) %copy-start) | copy-done | bytes 2097176
  1.6 0.7 copy-done.8
  2.3 0.8 shard_map.64
  3.1 2.2 %all-gather = f32[512,256]{1,0:T(8,128)S(1)} all-gather(f32[256,256]{1,0:T(8,128)S(1)} %shard_map.64), channel_id=2, replica_groups=mesh['zh'=4,'zl'=4,'x'=4,'c'=2,'y'=4] {'c'}, dimensions={0}, use_global_device_ids=true | all-gather | bytes 786432 | tf_op jit(solution)/shard_map/all_gather | solution.py:542
  5.3 1.3 shard_map.65.after_ref
  6.6 4.4 %all-to-all-start = ((f32[4,256,256]{2,1,0:T(8,128)}), f32[4,256,256]{2,1,0:T(8,128)}, u32[]{:S(2)}, u32[]{:S(2)}) async-start(f32[4,256,256]{2,1,0:T(8,128)} %shard_map.65.after_ref), calls=%async_computation | async-start | bytes 2097152 | tf_op jit(solution)/shard_map/all_to_all | solution.py:522
  11.0 0.0 copy-done.9
  11.0 0.0 copy-done.14
  11.0 0.0 copy-start.20
  11.0 0.0 copy-start.23
  11.1 0.0 copy-start.24
  11.1 0.1 shard_map.66
  11.1 1.4 collective-permute-start
  12.6 4.5 %collective-permute-start.1 = (f32[8,128]{1,0:T(8,128)S(1)}, f32[8,128]{1,0:T(8,128)S(1)}, u32[]{:S(2)}, u32[]{:S(2)}) collective-permute-start(f32[8,128]{1,0:T(8,128)S(1)} %get-tuple-element.31), channel_id=1, source_target_pairs={{1,0},{2,1},{3,2},{5,4},{6,5},{7,6},{9,8},{10,9},{11,10},{13,12},{... | collective-permute-start | bytes 12296 | tf_op jit(solution)/shard_map/ppermute | solution.py:554
  17.1 1.9 %collective-permute-start.2 = (f32[8,128]{1,0:T(8,128)S(1)}, f32[8,128]{1,0:T(8,128)S(1)}, u32[]{:S(2)}, u32[]{:S(2)}) collective-permute-start(f32[8,128]{1,0:T(8,128)S(1)} %get-tuple-element.32), channel_id=1, source_target_pairs={{0,4},{4,0},{1,5},{5,1},{2,6},{6,2},{3,7},{7,3},{8,12},{12,8},{9,1... | collective-permute-start | bytes 12296 | tf_op jit(solution)/shard_map/ppermute | solution.py:557
  19.1 0.7 collective-permute-start.3
  19.7 0.0 collective-permute-done.rest_0_.left_ref
  19.7 0.0 collective-permute-done.1.rest_1_.right_ref
  19.7 0.4 collective-permute-done.2.rest_2_.near_ref
  20.2 0.0 collective-permute-done.3.rest_3_.cross_ref
  20.2 6.5 %all-to-all-done.chips_ref = f32[4,256,256]{2,1,0:T(8,128)} async-done(((f32[4,256,256]{2,1,0:T(8,128)}), f32[4,256,256]{2,1,0:T(8,128)}, u32[]{:S(2)}, u32[]{:S(2)}) %all-to-all-start) | async-done | bytes 1048608 | tf_op jit(solution)/shard_map/all_to_all | solution.py:522
  26.7 2.0 %shard_map.67.after_ref.own_ref = f32[256,256]{1,0:T(8,128)S(1)} custom-call(f32[4,256,256]{2,1,0:T(8,128)} %all-to-all-done.chips_ref, f32[8,128]{1,0:T(8,128)S(1)} %collective-permute-done.rest_0_.left_ref, f32[8,128]{1,0:T(8,128)S(1)} %collective-permute-done.1.rest_1_.right_ref, f32[8,128]{1,0:T(8,128)S(1)} %collective-permute-done.2.rest_2_.near_ref, ...), custom_call_target="tpu_custom_call" | custom-call | flops 10000000 | bytes 1000000 | tf_op jit(solution)/shard_map/pallas_call | solution.py:71
  28.7 3.9 %collective-permute-start.4 = (f32[256,256]{1,0:T(8,128)S(1)}, f32[256,256]{1,0:T(8,128)S(1)}, u32[]{:S(2)}, u32[]{:S(2)}) collective-permute-start(f32[256,256]{1,0:T(8,128)S(1)} %shard_map.67.after_ref.own_ref), channel_id=1, source_target_pairs={{0,32},{32,0},{64,96},{96,64},{128,160},{160,128},{192,224},{224,1... | collective-permute-start | bytes 786440 | tf_op jit(solution)/shard_map/ppermute | solution.py:564
  32.6 0.0 copy-done.1
  32.6 0.0 copy-done.20
  32.6 0.0 copy-done.23
  32.6 1.9 %shard_map.68 = (f32[3,8,256]{2,1,0:T(8,128)S(1)}, f32[8,256]{1,0:T(8,128)S(1)}, f32[3,8,256]{2,1,0:T(8,128)S(1)}, f32[2,8,512]{2,1,0:T(8,128)S(1)}, f32[8,256]{1,0:T(8,128)S(1)}) custom-call(f32[3,8,256]{2,1,0:T(8,128)S(1)} %copy-done.14, f32[3,8,256]{2,1,0:T(8,128)S(1)} %copy-done.20, f32[8,256]{1,0:T(8,128)S(1)} %copy-done.23, ...), custom_call_target="tpu_custom_call" | custom-call | flops 100000000 | bytes 3000000 | tf_op jit(solution)/shard_map/pallas_call | solution.py:71
  34.5 0.0 copy-start.21
  34.5 0.6 copy-done.21
  35.1 2.4 %shard_map.69 = (bf16[1280,512]{1,0:T(8,128)(2,1)S(1)}, bf16[1280,512]{1,0:T(8,128)(2,1)S(1)}, bf16[256,256]{1,0:T(8,128)(2,1)S(1)}, bf16[256,256]{1,0:T(8,128)(2,1)S(1)}) custom-call(f32[4,256,256]{2,1,0:T(8,128)} %all-to-all-done.chips_ref, f32[2,256,256]{2,1,0:T(8,128)S(1)} %bitcast.3, f32[256,256]{1,0:T(8,128)S(1)} %shard_map.67.after_ref.own_ref), custom_call_target="tpu_custom_call" | custom-call | flops 1000000000 | bytes 1000000 | tf_op jit(solution)/shard_map/pallas_call | solution.py:71
  37.6 0.6 collective-permute-done.4.other_ref.one_ref
  38.2 0.3 shard_map.70.after_ref.own_ref
  38.5 5.2 %collective-permute-start.5 = (f32[256,256]{1,0:T(8,128)S(1)}, f32[256,256]{1,0:T(8,128)S(1)}, u32[]{:S(2)}, u32[]{:S(2)}) collective-permute-start(f32[256,256]{1,0:T(8,128)S(1)} %shard_map.70.after_ref.own_ref), channel_id=1, source_target_pairs={{0,64},{32,96},{64,0},{96,32},{128,192},{160,224},{192,128},{224,1... | collective-permute-start | bytes 786440 | tf_op jit(solution)/shard_map/ppermute | solution.py:588
  43.7 0.0 copy-done.2
  43.7 0.2 shard_map.71
  43.9 10.1 %all_to_all.30.got_ref = f32[8,3,256]{2,1,0:T(4,128)S(1)} all-to-all(f32[8,3,256]{2,1,0:T(4,128)S(1)} %shard_map.71), channel_id=1, replica_groups=mesh['zh'=4,'zl'=4,'x'=4,'c'=2,'y'=4] {'x','c'}, dimensions={0} | all-to-all | bytes 49152 | tf_op jit(solution)/shard_map/all_to_all | solution.py:522
  53.9 0.4 shard_map.72.rest_0_.both_ref
  54.4 0.0 copy-done.4
  54.4 0.0 collective-permute-done.5.other_ref.two_ref
  54.4 0.2 shard_map.73.after_ref
  54.6 1.3 collective-permute-start.6
  55.9 0.4 shard_map.74
  56.4 0.0 copy-start.10
  56.4 18.3 %collective-permute-done.6 = f32[128,256]{1,0:T(8,128)S(1)} collective-permute-done((f32[128,256]{1,0:T(8,128)S(1)}, f32[128,256]{1,0:T(8,128)S(1)}, u32[]{:S(2)}, u32[]{:S(2)}) %collective-permute-start.6) | collective-permute-done | bytes 131104 | tf_op jit(solution)/shard_map/ppermute | solution.py:605
  74.7 2.0 %all-gather.1 = f32[256,256]{1,0:T(8,128)S(1)} all-gather(f32[128,256]{1,0:T(8,128)S(1)} %collective-permute-done.6), channel_id=3, replica_groups=mesh['zh'=4,'zl'=4,'x'=4,'c'=2,'y'=4] {'c'}, dimensions={0}, use_global_device_ids=true | all-gather | bytes 393216 | tf_op jit(solution)/shard_map/all_gather | solution.py:613
  76.7 0.5 shard_map.75
  77.2 20.1 %all_to_all.31.got_ref = f32[16,3,256]{2,1,0:T(4,128)S(1)} all-to-all(f32[16,3,256]{2,1,0:T(4,128)S(1)} %get-tuple-element.42), channel_id=1, replica_groups=mesh['zh'=4,'zl'=4,'x'=4,'c'=2,'y'=4] {'zh','zl'}, dimensions={0} | all-to-all | bytes 98304 | tf_op jit(solution)/shard_map/all_to_all | solution.py:522
  97.3 1.0 shard_map.76
  98.3 0.6 copy-done.17
  99.0 0.6 copy-done.19
  99.6 4.7 %all-to-all-start.3 = ((f32[8,8,128]{2,1,0:T(8,128)}), f32[8,8,128]{2,1,0:T(8,128)}, u32[]{:S(2)}, u32[]{:S(2)}) async-start(f32[8,8,128]{2,1,0:T(8,128)} %copy-done.19), calls=%async_computation.3 | async-start | bytes 65536 | tf_op jit(solution)/shard_map/all_to_all | solution.py:522
  104.2 0.6 collective-permute-start.7
  104.9 0.0 collective-permute-done.7.row_ref
  104.9 2.8 %all-to-all-done.3.side_ref = f32[8,8,128]{2,1,0:T(8,128)} async-done(((f32[8,8,128]{2,1,0:T(8,128)}), f32[8,8,128]{2,1,0:T(8,128)}, u32[]{:S(2)}, u32[]{:S(2)}) %all-to-all-start.3) | async-done | bytes 32800 | tf_op jit(solution)/shard_map/all_to_all | solution.py:522
  107.7 1.0 copy-done.3
  108.8 0.7 copy-done.11
  109.5 0.8 copy-done.16
  110.3 0.8 copy-done.18
  111.0 0.7 copy-done.22
  111.8 2.4 %shard_map.77 = (f32[3,8,256]{2,1,0:T(8,128)S(1)}, f32[8,3,256]{2,1,0:T(4,128)S(1)}) custom-call(f32[4,8,256]{2,1,0:T(8,128)S(1)} %copy-done.18, f32[3,8,256]{2,1,0:T(8,128)S(1)} %copy-done.11, f32[8,8,128]{2,1,0:T(8,128)} %all-to-all-done.3.side_ref, f32[8,128]{1,0:T(8,128)S(1)} %collective-permute-done.7.row_ref, bf16[4,512,512]{2,1,0:T(8,128)(2,1)S(1)} %copy-done.1, ...), custom_call_target="tpu_custom_call" | custom-call | flops 100000000 | bytes 3000000 | tf_op jit(solution)/shard_map/pallas_call | solution.py:71
  114.2 14.8 %all_to_all.32.got_ref = f32[8,3,256]{2,1,0:T(4,128)S(1)} all-to-all(f32[8,3,256]{2,1,0:T(4,128)S(1)} %get-tuple-element.51), channel_id=1, replica_groups=mesh['zh'=4,'zl'=4,'x'=4,'c'=2,'y'=4] {'x','c'}, dimensions={0} | all-to-all | bytes 49152 | tf_op jit(solution)/shard_map/all_to_all | solution.py:522
  128.9 0.6 shard_map.78
  129.6 16.8 %all_to_all.33.got_ref = f32[16,3,256]{2,1,0:T(4,128)S(1)} all-to-all(f32[16,3,256]{2,1,0:T(4,128)S(1)} %get-tuple-element.52), channel_id=1, replica_groups=mesh['zh'=4,'zl'=4,'x'=4,'c'=2,'y'=4] {'zh','zl'}, dimensions={0} | all-to-all | bytes 98304 | tf_op jit(solution)/shard_map/all_to_all | solution.py:522
  146.4 1.6 %shard_map.79 = f32[3,8,256]{2,1,0:T(8,128)} custom-call(f32[16,3,256]{2,1,0:T(4,128)S(1)} %all_to_all.33.got_ref, f32[8,512]{1,0:T(8,128)S(1)} %get-tuple-element.53.both_ref, bf16[8,256,256]{2,1,0:T(8,128)(2,1)S(1)} %get-tuple-element.39.maps_ref, bf16[2,256,256]{2,1,0:T(8,128)(2,1)S(1)} %get-tuple-element.43.joint_ref, ...), custom_call_target="tpu_custom_call" | custom-call | flops 100000000 | bytes 4000000 | tf_op jit(solution)/shard_map/pallas_call | solution.py:653
  (28 shorter events, 0.0 us)
Async XLA Ops:
  0.0 1.6 %copy-start = (bf16[4,512,512]{2,1,0:T(8,128)(2,1)S(1)}, bf16[4,512,512]{2,1,0:T(8,128)(2,1)}, u32[]{:S(2)}) copy-start(bf16[4,512,512]{2,1,0:T(8,128)(2,1)} %inv_ref.9) | copy-start | bytes 6291460
  1.6 0.7 copy-start.8
  5.3 38.4 %copy-start.2 = (f32[512,256]{1,0:T(8,128)}, f32[512,256]{1,0:T(8,128)S(1)}, u32[]{:S(2)}) copy-start(f32[512,256]{1,0:T(8,128)S(1)} %all-gather) | copy-start | bytes 1572868
  6.6 4.4 %copy-start.9 = (f32[3,8,256]{2,1,0:T(8,128)S(1)}, f32[3,8,256]{2,1,0:T(8,128)}, u32[]{:S(2)}) copy-start(f32[3,8,256]{2,1,0:T(8,128)} %stiff_ref.11) | copy-start | bytes 73732
  6.6 4.4 %copy-start.14 = (f32[3,8,256]{2,1,0:T(8,128)S(1)}, f32[3,8,256]{2,1,0:T(8,128)}, u32[]{:S(2)}) copy-start(f32[3,8,256]{2,1,0:T(8,128)} %u_ref.3) | copy-start | bytes 73732
  6.6 20.1 %all-to-all-start = ((f32[4,256,256]{2,1,0:T(8,128)}), f32[4,256,256]{2,1,0:T(8,128)}, u32[]{:S(2)}, u32[]{:S(2)}) async-start(f32[4,256,256]{2,1,0:T(8,128)} %shard_map.65.after_ref), calls=%async_computation | async-start | bytes 2097152 | tf_op jit(solution)/shard_map/all_to_all | solution.py:522
  11.0 21.6 %copy-start.1 = (bf16[4,512,512]{2,1,0:T(8,128)(2,1)S(1)}, bf16[4,512,512]{2,1,0:T(8,128)(2,1)}, u32[]{:S(2)}) copy-start(bf16[4,512,512]{2,1,0:T(8,128)(2,1)} %inv_ref.9) | copy-start | bytes 6291460
  11.0 21.6 %copy-start.20 = (f32[3,8,256]{2,1,0:T(8,128)S(1)}, f32[3,8,256]{2,1,0:T(8,128)}, u32[]{:S(2)}) copy-start(f32[3,8,256]{2,1,0:T(8,128)} %target_ref.1) | copy-start | bytes 73732
  11.0 21.6 %copy-start.23 = (f32[8,256]{1,0:T(8,128)S(1)}, f32[8,256]{1,0:T(8,128)}, u32[]{:S(2)}) copy-start(f32[8,256]{1,0:T(8,128)} %inertia_ref.1) | copy-start | bytes 24580
  11.1 21.6 %copy-start.24 = (s32[64]{0:T(128)S(1)}, s32[64]{0:T(128)}, u32[]{:S(2)}) copy-start(s32[64]{0:T(128)} %pin_ref.1) | copy-start | bytes 772
  11.1 8.6 %collective-permute-start = (f32[8,128]{1,0:T(8,128)S(1)}, f32[8,128]{1,0:T(8,128)S(1)}, u32[]{:S(2)}, u32[]{:S(2)}) collective-permute-start(f32[8,128]{1,0:T(8,128)S(1)} %get-tuple-element.30), channel_id=1, source_target_pairs={{0,1},{1,2},{2,3},{4,5},{5,6},{6,7},{8,9},{9,10},{10,11},{12,13},{... | collective-permute-start | bytes 12296 | tf_op jit(solution)/shard_map/ppermute | solution.py:555
  12.6 7.2 %collective-permute-start.1 = (f32[8,128]{1,0:T(8,128)S(1)}, f32[8,128]{1,0:T(8,128)S(1)}, u32[]{:S(2)}, u32[]{:S(2)}) collective-permute-start(f32[8,128]{1,0:T(8,128)S(1)} %get-tuple-element.31), channel_id=1, source_target_pairs={{1,0},{2,1},{3,2},{5,4},{6,5},{7,6},{9,8},{10,9},{11,10},{13,12},{... | collective-permute-start | bytes 12296 | tf_op jit(solution)/shard_map/ppermute | solution.py:554
  17.1 3.1 %collective-permute-start.2 = (f32[8,128]{1,0:T(8,128)S(1)}, f32[8,128]{1,0:T(8,128)S(1)}, u32[]{:S(2)}, u32[]{:S(2)}) collective-permute-start(f32[8,128]{1,0:T(8,128)S(1)} %get-tuple-element.32), channel_id=1, source_target_pairs={{0,4},{4,0},{1,5},{5,1},{2,6},{6,2},{3,7},{7,3},{8,12},{12,8},{9,1... | collective-permute-start | bytes 12296 | tf_op jit(solution)/shard_map/ppermute | solution.py:557
  19.1 1.1 collective-permute-start.3
  28.7 9.5 %collective-permute-start.4 = (f32[256,256]{1,0:T(8,128)S(1)}, f32[256,256]{1,0:T(8,128)S(1)}, u32[]{:S(2)}, u32[]{:S(2)}) collective-permute-start(f32[256,256]{1,0:T(8,128)S(1)} %shard_map.67.after_ref.own_ref), channel_id=1, source_target_pairs={{0,32},{32,0},{64,96},{96,64},{128,160},{160,128},{192,224},{224,1... | collective-permute-start | bytes 786440 | tf_op jit(solution)/shard_map/ppermute | solution.py:564
  34.5 0.6 copy-start.21
  35.1 2.4 %copy-start.15 = (f32[2,8,512]{2,1,0:T(8,128)}, f32[2,8,512]{2,1,0:T(8,128)S(1)}, u32[]{:S(2)}) copy-start(f32[2,8,512]{2,1,0:T(8,128)S(1)} %get-tuple-element.49.ext_ref) | copy-start | bytes 98308
  37.6 16.8 %copy-start.4 = (bf16[1280,512]{1,0:T(8,128)(2,1)}, bf16[1280,512]{1,0:T(8,128)(2,1)S(1)}, u32[]{:S(2)}) copy-start(bf16[1280,512]{1,0:T(8,128)(2,1)S(1)} %get-tuple-element.37.wh_ref) | copy-start | bytes 3932164
  37.6 16.8 %copy-start.6 = (bf16[1280,512]{1,0:T(8,128)(2,1)}, bf16[1280,512]{1,0:T(8,128)(2,1)S(1)}, u32[]{:S(2)}) copy-start(bf16[1280,512]{1,0:T(8,128)(2,1)S(1)} %get-tuple-element.38.wl_ref) | copy-start | bytes 3932164
  37.6 59.7 %copy-start.12 = (bf16[256,256]{1,0:T(8,128)(2,1)}, bf16[256,256]{1,0:T(8,128)(2,1)S(1)}, u32[]{:S(2)}) copy-start(bf16[256,256]{1,0:T(8,128)(2,1)S(1)} %get-tuple-element.44.el_ref) | copy-start | bytes 393220
  38.5 15.9 %collective-permute-start.5 = (f32[256,256]{1,0:T(8,128)S(1)}, f32[256,256]{1,0:T(8,128)S(1)}, u32[]{:S(2)}, u32[]{:S(2)}) collective-permute-start(f32[256,256]{1,0:T(8,128)S(1)} %shard_map.70.after_ref.own_ref), channel_id=1, source_target_pairs={{0,64},{32,96},{64,0},{96,32},{128,192},{160,224},{192,128},{224,1... | collective-permute-start | bytes 786440 | tf_op jit(solution)/shard_map/ppermute | solution.py:588
  54.6 20.0 %collective-permute-start.6 = (f32[128,256]{1,0:T(8,128)S(1)}, f32[128,256]{1,0:T(8,128)S(1)}, u32[]{:S(2)}, u32[]{:S(2)}) collective-permute-start(f32[128,256]{1,0:T(8,128)S(1)} %shard_map.73.after_ref), channel_id=1, source_target_pairs={{128,0},{160,32},{192,64},{224,96},{256,384},{288,416},{320,448},{... | collective-permute-start | bytes 393224 | tf_op jit(solution)/shard_map/ppermute | solution.py:605
  56.4 40.9 %copy-start.10 = (f32[3,8,256]{2,1,0:T(8,128)S(1)}, f32[3,8,256]{2,1,0:T(8,128)}, u32[]{:S(2)}) copy-start(f32[3,8,256]{2,1,0:T(8,128)} %stiff_ref.11) | copy-start | bytes 73732
  98.3 0.6 copy-start.17
  98.9 0.6 copy-start.19
  99.6 8.2 %all-to-all-start.3 = ((f32[8,8,128]{2,1,0:T(8,128)}), f32[8,8,128]{2,1,0:T(8,128)}, u32[]{:S(2)}, u32[]{:S(2)}) async-start(f32[8,8,128]{2,1,0:T(8,128)} %copy-done.19), calls=%async_computation.3 | async-start | bytes 65536 | tf_op jit(solution)/shard_map/all_to_all | solution.py:522
  104.2 0.7 collective-permute-start.7
  107.7 1.0 copy-start.3
  108.8 0.7 copy-start.11
  109.5 0.8 copy-start.16
  110.3 0.8 copy-start.18
  111.0 0.7 copy-start.22
  111.8 17.2 %copy-start.5 = (bf16[1280,512]{1,0:T(8,128)(2,1)S(1)}, bf16[1280,512]{1,0:T(8,128)(2,1)}, u32[]{:S(2)}) copy-start(bf16[1280,512]{1,0:T(8,128)(2,1)} %copy-done.4) | copy-start | bytes 3932164
  111.8 17.2 %copy-start.7 = (bf16[1280,512]{1,0:T(8,128)(2,1)S(1)}, bf16[1280,512]{1,0:T(8,128)(2,1)}, u32[]{:S(2)}) copy-start(bf16[1280,512]{1,0:T(8,128)(2,1)} %copy-done.6) | copy-start | bytes 3932164
  128.9 17.4 %copy-start.13 = (bf16[256,256]{1,0:T(8,128)(2,1)S(1)}, bf16[256,256]{1,0:T(8,128)(2,1)}, u32[]{:S(2)}) copy-start(bf16[256,256]{1,0:T(8,128)(2,1)} %copy-done.12) | copy-start | bytes 393220

commit v2 on v1

--- a/solution.py
+++ b/solution.py
@@ -11,10 +11,10 @@
 STRIP = ("zh", "zl", "x", "c")
 ZAX = ("zh", "zl")
 PLANE = ("x", "c")
-SIDES = ("c", "y")
 CB = 256
 PIN = 20.0
 VMEM_LIMIT = 14 * 1024 * 1024
+WHOLE_VMEM = 64 * 1024 * 1024 - 96 * 1024
 
 
 def dot(a, b):
@@ -62,21 +62,19 @@
     return halves_sum(dot(vec, high) + dot(vec, low))
 
 
-def call(kernel, outs, args, specs=None, scratch=(), flops=10**7, size=10**6, grid=None):
+def call(kernel, outs, args, specs=None, scratch=(), flops=10**7, size=10**6, limit=VMEM_LIMIT):
     vmem = pl.BlockSpec(memory_space=pltpu.VMEM)
     in_specs = [vmem] * len(args) if specs is None else [vmem if s is None else s for s in specs]
     many = isinstance(outs, (list, tuple))
     out_specs = [vmem] * len(outs) if many else vmem
-    extra = {} if grid is None else {"grid": grid}
     return pl.pallas_call(
         kernel,
         out_shape=outs,
         in_specs=in_specs,
         out_specs=out_specs,
         scratch_shapes=list(scratch),
-        compiler_params=pltpu.CompilerParams(vmem_limit_bytes=VMEM_LIMIT),
+        compiler_params=pltpu.CompilerParams(vmem_limit_bytes=limit),
         cost_estimate=pl.CostEstimate(flops=flops, bytes_accessed=size, transcendentals=0),
-        **extra,
     )(*args)
 
 
@@ -84,25 +82,55 @@
     return jax.ShapeDtypeStruct(shape, dtype)
 
 
-def local_map_kernel(inv_ref, stiff_ref, out_ref):
+def local_map_kernel(inv_hbm, stiff_hbm, u_hbm, out_ref, inv_ref, stiff_ref, u_ref, sems):
+    copies = [
+        pltpu.make_async_copy(stiff_hbm, stiff_ref, sems.at[4]),
+        pltpu.make_async_copy(u_hbm, u_ref, sems.at[5]),
+    ]
+    copies += [
+        pltpu.make_async_copy(inv_hbm.at[k, CB : 2 * CB, 0:CB], inv_ref.at[k], sems.at[k])
+        for k in range(4)
+    ]
+    for copy in copies:
+        copy.start()
+    core = lax.axis_index("c")
+    copies[0].wait()
+    copies[2].wait()
     first = dot_t(eye().astype(BF16), inv_ref[0]) * stiff_ref[1, 1:2, :]
     for k in range(1, 4):
+        copies[2 + k].wait()
         high, low = pair(first)
         first = (dot_t(high, inv_ref[k]) + dot_t(low, inv_ref[k])) * stiff_ref[
             1, 2 * k + 1 : 2 * k + 2, :
         ]
-    out_ref[...] = first
-
-
-def chip_map_kernel(both_ref, out_ref):
-    product = mm(pair(both_ref[0]), pair(both_ref[1]))
+    out_ref[0:CB, :] = first
+    copies[1].wait()
+    rows = [u_ref[k] for k in range(3)] + [stiff_ref[1]]
+    rows = [jnp.where(core == 0, r[7:8], r[0:1]) for r in rows]
+    out_ref[CB : CB + 8, :] = jnp.concatenate(rows + rows, axis=0)
+
+
+def chip_map_kernel(both_ref, out_ref, near_ref):
+    core = lax.axis_index("c")
+    product = mm(pair(both_ref[0, 0:CB, :]), pair(both_ref[1, 0:CB, :]))
     for k in range(4):
         out_ref[k] = product
-
-
-def plane_product_kernel(chips_ref, *rest):
-    out_ref = rest[-1]
+    tails = [both_ref[k, CB : CB + 8, :] for k in range(2)]
+    near_ref[...] = jnp.where(core == 0, tails[1], tails[0])
+
+
+def plane_product_kernel(chips_hbm, *rest):
+    out_ref, chips_ref, sems = rest[-3:]
+    copies = [
+        pltpu.make_async_copy(chips_hbm.at[k], chips_ref.at[k], sems.at[k]) for k in range(4)
+    ]
+    for copy in copies:
+        copy.start()
+    copies[0].wait()
+    copies[1].wait()
     left = mm(pair(chips_ref[0]), pair(chips_ref[1]))
+    copies[2].wait()
+    copies[3].wait()
     right = mm(pair(chips_ref[2]), pair(chips_ref[3]))
     out_ref[...] = mm(pair(left), pair(right))
 
@@ -115,21 +143,30 @@
     return lax.div(lax.axis_index("zl"), 2)
 
 
+def own_half(ref):
+    return ref[pl.ds(pl.multiple_of(lax.axis_index("c") * 128, 128), 128), :]
+
+
+def joined(mine_ref, other_ref):
+    core = lax.axis_index("c")
+    mine, other = mine_ref[...], other_ref[...]
+    top = jnp.where(core == 0, mine, other)
+    return jnp.concatenate([top, jnp.where(core == 0, other, mine)], axis=0)
+
+
 def two_planes_kernel(own_ref, other_ref, *rest):
-    out_ref = rest[-1]
+    out_ref, half_ref = rest[-2:]
     right = low_bit() == 1
     left_map = jnp.where(right, other_ref[...], own_ref[...])
     right_map = jnp.where(right, own_ref[...], other_ref[...])
     out_ref[...] = mm(pair(left_map), pair(right_map))
-
-
-def four_planes_kernel(own_ref, other_ref, *rest):
-    out_ref = rest[-1]
+    half_ref[...] = own_half(out_ref)
+
+
+def four_planes_kernel(own_ref, mine_ref, other_ref, out_ref):
     right = high_bit() == 1
-    start = pl.multiple_of(lax.axis_index("c") * 128, 128)
-    own, other = own_ref[pl.ds(start, 128), :], other_ref[pl.ds(start, 128), :]
-    left_map = jnp.where(right, other, own)
-    right_map = jnp.where(right, own_ref[...], other_ref[...])
+    left_map = jnp.where(right, mine_ref[...], own_half(own_ref))
+    right_map = jnp.where(right, own_ref[...], joined(mine_ref, other_ref))
     out_ref[...] = mm(pair(left_map), pair(right_map))
 
 
@@ -154,9 +191,9 @@
             suffix = mm(chips[k + 1], pair(suffix))
         suf_ref[k] = suffix
         store(k, 0, suffix)
-    store(4, 0, mm(pair(cores_ref[1]), pair(suf_ref[x])))
+    store(4, 0, mm(pair(cores_ref[1, 0:CB, :]), pair(suf_ref[x])))
     store(4, 1, jnp.where(core == 1, one, 0.0))
-    cur_ref[...] = jnp.where(core == 1, cores_ref[0], one)
+    cur_ref[...] = jnp.where(core == 1, cores_ref[0, 0:CB, :], one)
     for k in (3, 2, 1, 0):
 
         @pl.when(k < x)
@@ -174,10 +211,10 @@
     el_ref[...] = low
 
 
-def group_maps_kernel(one_ref, two_ref, after_ref, out_ref, s_ref, e_ref):
+def group_maps_kernel(one_ref, mine_ref, other_ref, after_ref, out_ref, s_ref, e_ref):
     one = eye()
     sibling = one_ref[...]
-    two = pair(two_ref[...])
+    two = pair(joined(mine_ref, other_ref))
     send = jnp.where(low_bit() == 0, sibling, one)
     take = jnp.where(low_bit() == 1, sibling, one)
     for k, value in ((0, send), (4, take)):
@@ -194,9 +231,9 @@
     e_ref[...] = take
 
 
-def joint_map(far_ref, s_ref, e_ref, out_ref):
+def joint_map(mine_ref, other_ref, s_ref, e_ref, out_ref):
     zh = lax.axis_index("zh")
-    far = jnp.concatenate([far_ref[0], far_ref[1]], axis=0)
+    far = joined(mine_ref, other_ref)
     left = jnp.where(zh == 0, s_ref[...], far)
     right = jnp.where(zh == 0, far, e_ref[...])
     joint = pair(mm(pair(left), pair(right)))
@@ -216,39 +253,14 @@
     return left, right
 
 
-def put_rows(out_ref, index, rows):
-    for k in range(len(rows)):
-        for h in range(2):
-            spot = (slice(2 * k + h, 2 * k + h + 1), slice(None))
-            out_ref[index + spot] = rows[k][:, 128 * h : 128 * (h + 1)]
-
-
-def halo_kernel(u_ref, stiff_ref, after_ref, left_ref, right_ref, near_ref, cross_ref):
+def halo_kernel(u_ref, stiff_ref, after_ref, left_ref, right_ref, cross_ref):
     core = lax.axis_index("c")
     comps = [u_ref[k] for k in range(3)]
     left, right = edge_tiles(comps, [stiff_ref[0], stiff_ref[2]])
     left_ref[...] = left
     right_ref[...] = right
-    rows = comps + [stiff_ref[1]]
-    put_rows(near_ref, (), [jnp.where(core == 0, r[7:8], r[0:1]) for r in rows])
-    put_rows(cross_ref, (), [jnp.where(core == 0, r[0:1], r[7:8]) for r in rows])
-
-
-def write_halos(comps, side_ref, row_ref):
-    core = lax.axis_index("c")
-    y = lax.axis_index("y")
-    left, right = edge_tiles(comps, [])
-    for j in range(8):
-        side_ref[j] = jnp.zeros((8, 128), F32)
-    side_ref[core * 4 + lax.rem(y + 1, 4)] = right
-    side_ref[core * 4 + lax.rem(y + 3, 4)] = left
-    rows = [c[0:1] for c in comps] + [jnp.zeros((1, CB), F32)]
-    put_rows(side_ref, ((1 - core) * 4 + y,), rows)
-    put_rows(row_ref, (), rows)
-
-
-def row_of(tile, k):
-    return jnp.concatenate([tile[2 * k : 2 * k + 1], tile[2 * k + 1 : 2 * k + 2]], axis=1)
+    for k, rows in enumerate(comps + [stiff_ref[1]]):
+        cross_ref[k : k + 1, :] = jnp.where(core == 0, rows[0:1], rows[7:8])
 
 
 def springs(ends, others, weight, rest, length):
@@ -332,7 +344,7 @@
 def write_offsets(offset, chip_ref, msg_ref):
     core = lax.axis_index("c")
     x = lax.axis_index("x")
-    chip = pair(chip_ref[1])
+    chip = pair(chip_ref[1, 0:CB, :])
     onward = apply_map(stacked(offset), chip[0], chip[1])[0:3]
     raw = offset[0:3]
     onward = jnp.where(core == 0, onward, raw)
@@ -374,38 +386,35 @@
         weight = jnp.where((lane >= low) & (lane < high), weight, 0.0)
         extended.append(weight)
         ext_ref[k - 3] = weight
-    above = jnp.where(core == 0, cross_ref[...], near_ref[...])
-    below = jnp.where(core == 0, near_ref[...], cross_ref[...])
-    above_weight = jnp.where(strip == 0, 0.0, row_of(above, 3))
+    near, cross = near_ref[0:4, :], cross_ref[...]
+    above = jnp.where(core == 0, cross, near)
+    below = jnp.where(core == 0, near, cross)
+    above_weight = jnp.where(strip == 0, 0.0, above[3:4])
     above_ref[...] = jnp.broadcast_to(above_weight, (8, CB))
     vertical = jnp.where((row == 7) & (strip == 127), 0.0, stiff_ref[1])
     offset_ref[...] = solve_right_side(
-        comps, inertial, from_left, right_ref[...], [row_of(below, k) for k in range(3)],
-        [row_of(above, k) for k in range(3)], above_weight, extended[0], extended[1], vertical,
+        comps, inertial, from_left, right_ref[...], [below[k : k + 1] for k in range(3)],
+        [above[k : k + 1] for k in range(3)], above_weight, extended[0], extended[1], vertical,
         stiff_ref, inv_ref, base_ref,
     )
 
 
 def second_side_kernel(
-    u_ref, stiff_ref, side_ref, row_ref, inv_ref, chip_ref, inertial_ref, ext_ref, above_ref,
-    base_ref, msg_ref,
+    u_ref, stiff_ref, left_ref, right_ref, row_ref, inv_ref, chip_ref, inertial_ref, ext_ref,
+    above_ref, base_ref, msg_ref,
 ):
     core = lax.axis_index("c")
     y = lax.axis_index("y")
     strip = (lax.axis_index("zh") * 4 + lax.axis_index("zl")) * 8 + lax.axis_index("x") * 2 + core
     comps = [u_ref[k] for k in range(3)]
     row = lax.broadcasted_iota(jnp.int32, (8, CB), 0)
-    partner = side_ref[(1 - core) * 4 + y]
-    below = jnp.where(core == 0, partner, row_ref[...])
     above_weight = above_ref[0:1, :]
     divisor = jnp.where(strip == 0, 1.0, above_weight)
     above_rows = [u_ref[3, k : k + 1, :] / divisor for k in range(3)]
     vertical = jnp.where((row == 7) & (strip == 127), 0.0, stiff_ref[1])
-    from_left = side_ref[core * 4 + lax.rem(y + 3, 4)]
-    from_right = side_ref[core * 4 + lax.rem(y + 1, 4)]
     offset = solve_right_side(
-        comps, [inertial_ref[k] for k in range(3)], from_left, from_right,
-        [row_of(below, k) for k in range(3)], above_rows, above_weight, ext_ref[0], ext_ref[1],
+        comps, [inertial_ref[k] for k in range(3)], left_ref[...], right_ref[...],
+        [row_ref[k : k + 1, :] for k in range(3)], above_rows, above_weight, ext_ref[0], ext_ref[1],
         vertical, stiff_ref, inv_ref, base_ref,
     )
     write_offsets(offset, chip_ref, msg_ref)
@@ -441,8 +450,8 @@
     both_ref[...] = plane_vectors(got_ref, wh_ref, wl_ref, vec_ref)
 
 
-def send_kernel(both_ref, maps_ref, far_ref, s_ref, e_ref, joint_ref, msg_ref):
-    joint_map(far_ref, s_ref, e_ref, joint_ref)
+def send_kernel(both_ref, maps_ref, mine_ref, other_ref, s_ref, e_ref, joint_ref, msg_ref):
+    joint_map(mine_ref, other_ref, s_ref, e_ref, joint_ref)
     send_vectors(both_ref[:, :CB], maps_ref, joint_ref, msg_ref)
 
 
@@ -496,7 +505,7 @@
 
 def middle_kernel(
     got_ref, both_ref, maps_ref, joint_ref, eh_ref, el_ref, stiff_ref, base_ref, inv_ref,
-    u_ref, side_ref, row_ref, vec_ref,
+    u_ref, left_ref, right_ref, row_ref, vec_ref,
 ):
     state, came = finish(
         got_ref, both_ref, maps_ref, joint_ref, eh_ref, el_ref, stiff_ref, base_ref, inv_ref, vec_ref
@@ -504,7 +513,10 @@
     for k in range(3):
         u_ref[k] = state[k]
     u_ref[3] = came
-    write_halos(state, side_ref, row_ref)
+    left, right = edge_tiles(state, [])
+    left_ref[...] = left
+    right_ref[...] = right
+    row_ref[...] = jnp.concatenate([state[0][0:1], state[1][0:1], state[2][0:1], state[0][0:1]], axis=0)
 
 
 def final_kernel(
@@ -530,36 +542,49 @@
     def full(shape):
         return pl.BlockSpec(shape, lambda i: (0,) * len(shape))
 
-    own_map = pl.pallas_call(
+    hbm = pl.BlockSpec(memory_space=pltpu.HBM)
+    own_map = call(
         local_map_kernel,
-        grid=grid,
-        out_shape=sds((CB, CB)),
-        in_specs=[pl.BlockSpec((4, CB, CB), lambda i: (0, 1, 0)), full((3, 8, CB))],
-        out_specs=full((CB, CB)),
-        compiler_params=pltpu.CompilerParams(vmem_limit_bytes=VMEM_LIMIT),
-        cost_estimate=pl.CostEstimate(flops=10**8, bytes_accessed=10**6, transcendentals=0),
-    )(inverses, stiffness)
+        sds((CB + 8, CB)),
+        (inverses, stiffness, positions),
+        specs=[hbm] * 3,
+        scratch=[
+            pltpu.VMEM((4, CB, CB), BF16),
+            pltpu.VMEM((3, 8, CB), F32),
+            pltpu.VMEM((3, 8, CB), F32),
+            pltpu.SemaphoreType.DMA((6,)),
+        ],
+        flops=10**8,
+        limit=WHOLE_VMEM,
+    )
     core_maps = lax.all_gather(own_map, "c")
-    chip_copies = call(chip_map_kernel, sds((4, CB, CB)), (core_maps,))
+    chip_copies, near = call(chip_map_kernel, [sds((4, CB, CB)), sds((8, CB))], (core_maps,))
     chips = swap(chip_copies, "x")
 
     tile = sds((8, 128))
-    left, right, near, cross = call(
+    rows = sds((4, CB))
+    left, right, cross = call(
         halo_kernel,
-        [tile] * 4,
+        [tile, tile, rows],
         (positions, stiffness, chip_copies),
         specs=[None, None, anywhere],
     )
     pairs = [(2 * k + 1, 2 * k + 2) for k in range(63)]
-    from_right = lax.ppermute(left, "y", [(1, 0), (2, 1), (3, 2)])
-    from_left = lax.ppermute(right, "y", [(0, 1), (1, 2), (2, 3)])
+    to_left = [(1, 0), (2, 1), (3, 2)]
+    to_right = [(0, 1), (1, 2), (2, 3)]
+    cores = [(0, 1), (1, 0)]
+    from_right = lax.ppermute(left, "y", to_left)
+    from_left = lax.ppermute(right, "y", to_right)
     cross = lax.ppermute(cross, STRIP, pairs + [(b, a) for a, b in pairs])
-    near = lax.ppermute(near, "c", [(0, 1), (1, 0)])
     halos = (from_left, from_right, near, cross)
 
     square = sds((CB, CB))
     plane = call(
-        plane_product_kernel, square, (chips,) + halos, specs=[None] + [anywhere] * 4
+        plane_product_kernel,
+        square,
+        (chips, from_left, from_right, cross),
+        specs=[hbm] + [anywhere] * 3,
+        scratch=[pltpu.VMEM((4, CB, CB), F32), pltpu.SemaphoreType.DMA((4,))],
     )
     beside = lax.ppermute(plane, ZAX, [(k, k ^ 1) for k in range(16)])
 
@@ -582,13 +607,21 @@
         scratch=[pltpu.VMEM((4, CB, CB), F32), pltpu.VMEM((CB, CB), F32)],
         flops=10**9,
     )
-    two = call(
-        two_planes_kernel, square, (plane, beside, base, eh), specs=[None, None, anywhere, anywhere]
-    )
-    other_two = lax.ppermute(two, ZAX, [(k, k ^ 2) for k in range(16)])
+    half = sds((128, CB))
+    two, two_half = call(
+        two_planes_kernel,
+        [square, half],
+        (plane, beside, base, eh),
+        specs=[None, None, anywhere, anywhere],
+    )
+    two_mine = lax.ppermute(two_half, ZAX, [(k, k ^ 2) for k in range(16)])
+    two_other = lax.ppermute(two_mine, "c", cores)
+    group_half = call(four_planes_kernel, half, (two, two_mine, two_other))
+    steps = [(4 + k, k) for k in range(4)] + [(8 + k, 12 + k) for k in range(4)]
+    far_mine = lax.ppermute(group_half, ZAX, steps)
 
     msg = call(
-        offsets_kernel, sds((8, 3, CB)), (offset, core_maps, two), specs=[None, None, anywhere]
+        offsets_kernel, sds((8, 3, CB)), (offset, core_maps, group_half), specs=[None, None, anywhere]
     )
     got = swap(msg, PLANE)
     both = call(
@@ -598,46 +631,44 @@
         scratch=[pltpu.VMEM((16, 5 * CB), F32)],
         size=3 * 10**6,
     )
-    group_half = call(
-        four_planes_kernel, sds((128, CB)), (two, other_two, both), specs=[None, None, anywhere]
-    )
-    steps = [(4 + k, k) for k in range(4)] + [(8 + k, 12 + k) for k in range(4)]
-    far_half = lax.ppermute(group_half, ZAX, steps)
     maps, send_map, take_map = call(
         group_maps_kernel,
         [sds((8, CB, CB), BF16), square, square],
-        (beside, other_two, group_half),
-        specs=[None, None, anywhere],
+        (beside, two_mine, two_other, both),
+        specs=[None, None, None, anywhere],
         flops=5 * 10**8,
     )
-    far_parts = lax.all_gather(far_half, "c")
+    far_mine, both, maps = lax.optimization_barrier((far_mine, both, maps))
+    far_other = lax.ppermute(far_mine, "c", cores)
     joint, msg = call(
         send_kernel,
         [sds((2, CB, CB), BF16), sds((16, 3, CB))],
-        (both, maps, far_parts, send_map, take_map),
+        (both, maps, far_mine, far_other, send_map, take_map),
     )
     got = swap(msg, ZAX)
     sizes = ((16, 3, CB), (8, 2 * CB), (8, CB, CB), (2, CB, CB), (CB, CB), (CB, CB), (3, 8, CB), (3, 8, CB))
     finish_specs = [full(s) for s in sizes] + [pl.BlockSpec((4, 2 * CB, CB), lambda i: (0, 0, 0))]
     params = pltpu.CompilerParams(vmem_limit_bytes=VMEM_LIMIT)
     cost = pl.CostEstimate(flops=10**8, bytes_accessed=4 * 10**6, transcendentals=0)
-    middle, side, edge = pl.pallas_call(
+    middle, left, right, low_row = pl.pallas_call(
         middle_kernel,
         grid=grid,
-        out_shape=[sds((4, 8, CB)), sds((8, 8, 128)), tile],
+        out_shape=[sds((4, 8, CB)), tile, tile, rows],
         in_specs=finish_specs,
-        out_specs=[full((4, 8, CB)), full((8, 8, 128)), full((8, 128))],
+        out_specs=[full((4, 8, CB)), full((8, 128)), full((8, 128)), full((4, CB))],
         scratch_shapes=[pltpu.VMEM((16, 3 * CB), F32)],
         compiler_params=params,
         cost_estimate=cost,
     )(got, both, maps, joint, eh, el, stiffness, base, inverses)
 
-    side = swap(side, SIDES)
-    edge = lax.ppermute(edge, STRIP, [(b, a) for a, b in pairs])
+    low_row = lax.ppermute(low_row, STRIP, [(k + 1, k) for k in range(127)])
+    from_right = lax.ppermute(left, "y", to_left)
+    from_left = lax.ppermute(right, "y", to_right)
     base, msg = call(
         second_side_kernel,
         [field, sds((8, 3, CB))],
-        (middle, stiffness, side, edge, inverses, core_maps, inertial, ext, above),
+        (middle, stiffness, from_left, from_right, low_row, inverses, core_maps)
+        + (inertial, ext, above),
         flops=10**8,
         size=3 * 10**6,
     )

time: 149 us -> 139 us (0.933)
  local copies, waits for them, and re-layouts: 8.26 us -> 0.03 us
  blocking collectives: 65.9 us -> 60.2 us
  starting transfers between devices: 28.6 us -> 32.2 us
    ppermute x6 -> x9, starting transfers between devices: 15 us -> 23.4 us  [the longest x2 9.09 us: shards(): from_right = lax.ppermute(left, 'y', to_left)]
    unnamed x50 -> x12, local copies, waits for them, and re-layouts: 8.26 us -> 0.03 us
    all_to_all x2 -> x1, starting transfers between devices: 9.11 us -> 4.29 us  [swap(): return lax.all_to_all(value, axes, 0, 0)]
    all_to_all x4, blocking collectives: 61.7 us -> 57.8 us  [swap(): return lax.all_to_all(value, axes, 0, 0)]
    pallas_call x13 -> x14, Pallas kernels: 12.8 us -> 14.8 us  [call(): pl.pallas_call(kernel, out_shape=outs, in_specs=in_specs, out_specs=out_s...]
    all_gather x1 -> x0, blocking collectives: 1.98 us -> none  [shards(): far_parts = lax.all_gather(far_half, 'c')]
    all_to_all x2 -> x1, waiting for transfers between devices: 9.33 us -> 8.33 us  [swap(): return lax.all_to_all(value, axes, 0, 0)]
    ppermute x6 -> x9, waiting for transfers between devices: 18.8 us -> 18.7 us  [the longest x1 8.79 us: shards(): far_mine = lax.ppermute(group_half, ZAX, steps)]
  transfers between devices with their start and end apart: 10 -> 12, of which waited for: 5 -> 8; matrix products, arithmetic and copies ran while one was open for 0% -> 0% of each run, Pallas kernels for 4% -> 4%
where the time goes in v2:
time: 139 us; the launch traced here: 138 us
  blocking collectives  60.2 us (43%)
  starting transfers between devices  32.2 us (23%)
  waiting for transfers between devices  28.3 us (20%)
  Pallas kernels  17.4 us (13%)
    all_to_all x4, blocking collectives, swap(): return lax.all_to_all(value, axes, 0, 0)  57.8 us
    pallas_call x14, Pallas kernels, call(): pl.pallas_call(kernel, out_shape=outs, in_specs=in_specs, out_specs=out_s...  14.8 us
    ppermute x2, starting transfers between devices, shards(): from_right = lax.ppermute(left, 'y', to_left)  9.09 us
    ppermute x1, waiting for transfers between devices, shards(): far_mine = lax.ppermute(group_half, ZAX, steps)  8.79 us
    all_to_all x1, waiting for transfers between devices, swap(): return lax.all_to_all(value, axes, 0, 0)  8.33 us
    ppermute x1, starting transfers between devices, shards(): two_mine = lax.ppermute(two_half, ZAX, [(k, k ^ 2) for k in range(16)])  5.17 us
    ppermute x1, waiting for transfers between devices, shards(): two_mine = lax.ppermute(two_half, ZAX, [(k, k ^ 2) for k in range(16)])  4.9 us
    all_to_all x1, starting transfers between devices, swap(): return lax.all_to_all(value, axes, 0, 0)  4.29 us
  transfers between devices with their start and end apart: 12, of which 8 were waited for; matrix products, arithmetic and copies ran while one was open for 0% of the time, Pallas kernels for 4%

profile of v2, /device:TPU:24, one launch (start us, length us, event | category | flops | bytes accessed | tf_op | source)
XLA Modules:
  0.0 138.3 jit_solution(14175654647723943768)
XLA Ops:
  0.0 2.9 %shard_map.64 = f32[264,256]{1,0:T(8,128)} custom-call(bf16[4,512,512]{2,1,0:T(8,128)(2,1)} %inv_ref.7, f32[3,8,256]{2,1,0:T(8,128)} %stiff_ref.9, f32[3,8,256]{2,1,0:T(8,128)} %u_ref.3), custom_call_target="tpu_custom_call" | custom-call | flops 100000000 | bytes 1000000 | tf_op jit(solution)/shard_map/pallas_call | solution.py:70
  2.9 2.4 %all-gather = f32[528,256]{1,0:T(8,128)S(1)} all-gather(f32[264,256]{1,0:T(8,128)} %shard_map.64), channel_id=2, replica_groups=mesh['zh'=4,'zl'=4,'x'=4,'c'=2,'y'=4] {'c'}, dimensions={0}, use_global_device_ids=true | all-gather | bytes 811008 | tf_op jit(solution)/shard_map/all_gather | solution.py:560
  5.3 0.0 copy-start.1
  5.3 0.0 copy-start.2
  5.3 1.2 shard_map.65
  6.6 4.3 %all-to-all-start = ((f32[4,256,256]{2,1,0:T(8,128)}), f32[4,256,256]{2,1,0:T(8,128)}, u32[]{:S(2)}, u32[]{:S(2)}) async-start(f32[4,256,256]{2,1,0:T(8,128)} %get-tuple-element.37.after_ref), calls=%async_computation | async-start | bytes 2097152 | tf_op jit(solution)/shard_map/all_to_all | solution.py:534
  10.9 0.0 copy-done.1
  10.9 0.0 copy-done.2
  10.9 0.0 copy-start
  10.9 0.0 copy-start.3
  10.9 0.0 copy-start.4
  10.9 0.0 copy-start.5
  10.9 0.1 shard_map.66
  11.0 1.4 %collective-permute-start = (f32[8,128]{1,0:T(8,128)S(1)}, f32[8,128]{1,0:T(8,128)S(1)}, u32[]{:S(2)}, u32[]{:S(2)}) collective-permute-start(f32[8,128]{1,0:T(8,128)S(1)} %get-tuple-element.38), channel_id=1, source_target_pairs={{0,1},{1,2},{2,3},{4,5},{5,6},{6,7},{8,9},{9,10},{10,11},{12,13},{... | collective-permute-start | bytes 12296 | tf_op jit(solution)/shard_map/ppermute | solution.py:577
  12.4 4.5 %collective-permute-start.1 = (f32[8,128]{1,0:T(8,128)S(1)}, f32[8,128]{1,0:T(8,128)S(1)}, u32[]{:S(2)}, u32[]{:S(2)}) collective-permute-start(f32[8,128]{1,0:T(8,128)S(1)} %get-tuple-element.39), channel_id=1, source_target_pairs={{1,0},{2,1},{3,2},{5,4},{6,5},{7,6},{9,8},{10,9},{11,10},{13,12},{... | collective-permute-start | bytes 12296 | tf_op jit(solution)/shard_map/ppermute | solution.py:576
  17.0 0.7 collective-permute-start.2
  17.6 0.0 collective-permute-done.rest_0_.left_ref
  17.6 0.6 collective-permute-done.1.rest_1_.right_ref
  18.3 0.0 collective-permute-done.2.rest_2_.cross_ref
  18.3 8.3 %all-to-all-done.chips_hbm.chips_ref = f32[4,256,256]{2,1,0:T(8,128)} async-done(((f32[4,256,256]{2,1,0:T(8,128)}), f32[4,256,256]{2,1,0:T(8,128)}, u32[]{:S(2)}, u32[]{:S(2)}) %all-to-all-start) | async-done | bytes 1048608 | tf_op jit(solution)/shard_map/all_to_all | solution.py:534
  26.6 2.0 %shard_map.67.after_ref.own_ref = f32[256,256]{1,0:T(8,128)S(1)} custom-call(f32[4,256,256]{2,1,0:T(8,128)} %all-to-all-done.chips_hbm.chips_ref, f32[8,128]{1,0:T(8,128)S(1)} %collective-permute-done.rest_0_.left_ref, f32[8,128]{1,0:T(8,128)S(1)} %collective-permute-done.1.rest_1_.right_ref, f32[4,256]{1,0:T(4,128)S(1)} %collective-permute-done.2.rest_2_.cross_ref), custom_call_target="tpu_custom_call" | custom-call | flops 10000000 | bytes 1000000 | tf_op jit(solution)/shard_map/pallas_call | solution.py:70
  28.6 3.8 %collective-permute-start.3 = (f32[256,256]{1,0:T(8,128)S(1)}, f32[256,256]{1,0:T(8,128)S(1)}, u32[]{:S(2)}, u32[]{:S(2)}) collective-permute-start(f32[256,256]{1,0:T(8,128)S(1)} %shard_map.67.after_ref.own_ref), channel_id=1, source_target_pairs={{0,32},{32,0},{64,96},{96,64},{128,160},{160,128},{192,224},{224,1... | collective-permute-start | bytes 786440 | tf_op jit(solution)/shard_map/ppermute | solution.py:589
  32.5 0.0 copy-done
  32.5 0.0 copy-done.3
  32.5 0.0 copy-done.4
  32.5 0.0 copy-done.5
  32.5 1.9 %shard_map.68 = (f32[3,8,256]{2,1,0:T(8,128)S(1)}, f32[8,256]{1,0:T(8,128)S(1)}, f32[3,8,256]{2,1,0:T(8,128)S(1)}, f32[2,8,512]{2,1,0:T(8,128)S(1)}, f32[8,256]{1,0:T(8,128)S(1)}) custom-call(f32[3,8,256]{2,1,0:T(8,128)S(1)} %copy-done.2, f32[3,8,256]{2,1,0:T(8,128)S(1)} %copy-done.3, f32[8,256]{1,0:T(8,128)S(1)} %copy-done.4, f32[3,8,256]{2,1,0:T(8,128)S(1)} %copy-done.1, ...), custom_call_target="tpu_custom_call" | custom-call | flops 100000000 | bytes 3000000 | tf_op jit(solution)/shard_map/pallas_call | solution.py:70
  34.4 2.4 %shard_map.69 = (bf16[1280,512]{1,0:T(8,128)(2,1)S(1)}, bf16[1280,512]{1,0:T(8,128)(2,1)S(1)}, bf16[256,256]{1,0:T(8,128)(2,1)S(1)}, bf16[256,256]{1,0:T(8,128)(2,1)S(1)}) custom-call(f32[4,256,256]{2,1,0:T(8,128)} %all-to-all-done.chips_hbm.chips_ref, f32[2,264,256]{2,1,0:T(8,128)S(1)} %bitcast.2, f32[256,256]{1,0:T(8,128)S(1)} %shard_map.67.after_ref.own_ref), custom_call_target="tpu_custom_call" | custom-call | flops 1000000000 | bytes 1000000 | tf_op jit(solution)/shard_map/pallas_call | solution.py:70
  36.8 1.3 collective-permute-done.3.other_ref.one_ref
  38.1 0.3 shard_map.70
  38.4 5.2 %collective-permute-start.4 = (f32[128,256]{1,0:T(8,128)S(1)}, f32[128,256]{1,0:T(8,128)S(1)}, u32[]{:S(2)}, u32[]{:S(2)}) collective-permute-start(f32[128,256]{1,0:T(8,128)S(1)} %get-tuple-element.45), channel_id=1, source_target_pairs={{0,64},{32,96},{64,0},{96,32},{128,192},{160,224},{192,128},{224,1... | collective-permute-start | bytes 393224 | tf_op jit(solution)/shard_map/ppermute | solution.py:617
  43.6 4.9 %collective-permute-done.4.mine_ref = f32[128,256]{1,0:T(8,128)S(1)} collective-permute-done((f32[128,256]{1,0:T(8,128)S(1)}, f32[128,256]{1,0:T(8,128)S(1)}, u32[]{:S(2)}, u32[]{:S(2)}) %collective-permute-start.4) | collective-permute-done | bytes 131104 | tf_op jit(solution)/shard_map/ppermute | solution.py:617
  48.5 1.9 %collective-permute-start.5 = (f32[128,256]{1,0:T(8,128)S(1)}, f32[128,256]{1,0:T(8,128)S(1)}, u32[]{:S(2)}, u32[]{:S(2)}) collective-permute-start(f32[128,256]{1,0:T(8,128)S(1)} %collective-permute-done.4.mine_ref), channel_id=1, source_target_pairs={{0,4},{4,0},{1,5},{5,1},{2,6},{6,2},{3,7},{7,3},{8,12},{12,8},{9,1... | collective-permute-start | bytes 393224 | tf_op jit(solution)/shard_map/ppermute | solution.py:618
  50.4 1.3 collective-permute-done.5.other_ref
  51.7 0.2 shard_map.71.after_ref
  52.0 1.3 collective-permute-start.6
  53.3 0.2 shard_map.72
  53.4 9.5 %all_to_all.25.got_ref = f32[8,3,256]{2,1,0:T(4,128)S(1)} all-to-all(f32[8,3,256]{2,1,0:T(4,128)S(1)} %shard_map.72), channel_id=1, replica_groups=mesh['zh'=4,'zl'=4,'x'=4,'c'=2,'y'=4] {'x','c'}, dimensions={0} | all-to-all | bytes 49152 | tf_op jit(solution)/shard_map/all_to_all | solution.py:534
  63.0 0.4 shard_map.73.after_ref.both_ref
  63.4 0.5 shard_map.74
  63.9 8.8 %collective-permute-done.6.mine_ref = f32[128,256]{1,0:T(8,128)S(1)} collective-permute-done((f32[128,256]{1,0:T(8,128)S(1)}, f32[128,256]{1,0:T(8,128)S(1)}, u32[]{:S(2)}, u32[]{:S(2)}) %collective-permute-start.6) | collective-permute-done | bytes 131104 | tf_op jit(solution)/shard_map/ppermute | solution.py:621
  72.7 1.9 %collective-permute-start.7 = (f32[128,256]{1,0:T(8,128)S(1)}, f32[128,256]{1,0:T(8,128)S(1)}, u32[]{:S(2)}, u32[]{:S(2)}) collective-permute-start(f32[128,256]{1,0:T(8,128)S(1)} %collective-permute-done.6.mine_ref), channel_id=1, source_target_pairs={{0,4},{4,0},{1,5},{5,1},{2,6},{6,2},{3,7},{7,3},{8,12},{12,8},{9,1... | collective-permute-start | bytes 393224 | tf_op jit(solution)/shard_map/ppermute | solution.py:642
  74.6 1.3 collective-permute-done.7.other_ref
  75.9 0.5 shard_map.75
  76.4 21.3 %all_to_all.26.got_ref = f32[16,3,256]{2,1,0:T(4,128)S(1)} all-to-all(f32[16,3,256]{2,1,0:T(4,128)S(1)} %get-tuple-element.55), channel_id=1, replica_groups=mesh['zh'=4,'zl'=4,'x'=4,'c'=2,'y'=4] {'zh','zl'}, dimensions={0} | all-to-all | bytes 98304 | tf_op jit(solution)/shard_map/all_to_all | solution.py:534
  97.7 1.0 shard_map.76
  98.7 1.3 collective-permute-start.8
  100.0 4.5 %collective-permute-start.9 = (f32[8,128]{1,0:T(8,128)S(1)}, f32[8,128]{1,0:T(8,128)S(1)}, u32[]{:S(2)}, u32[]{:S(2)}) collective-permute-start(f32[8,128]{1,0:T(8,128)S(1)} %get-tuple-element.60), channel_id=1, source_target_pairs={{1,0},{2,1},{3,2},{5,4},{6,5},{7,6},{9,8},{10,9},{11,10},{13,12},{... | collective-permute-start | bytes 12296 | tf_op jit(solution)/shard_map/ppermute | solution.py:665
  104.6 1.3 collective-permute-start.10
  105.9 0.0 collective-permute-done.8.left_ref
  105.9 0.0 collective-permute-done.9.right_ref
  105.9 1.7 %collective-permute-done.10.row_ref = f32[4,256]{1,0:T(4,128)S(1)} collective-permute-done((f32[4,256]{1,0:T(4,128)S(1)}, f32[4,256]{1,0:T(4,128)S(1)}, u32[]{:S(2)}, u32[]{:S(2)}) %collective-permute-start.10) | collective-permute-done | bytes 4128 | tf_op jit(solution)/shard_map/ppermute | solution.py:664
  107.6 1.5 %shard_map.77 = (f32[3,8,256]{2,1,0:T(8,128)S(1)}, f32[8,3,256]{2,1,0:T(4,128)S(1)}) custom-call(f32[4,8,256]{2,1,0:T(8,128)S(1)} %get-tuple-element.58.u_ref, f32[3,8,256]{2,1,0:T(8,128)S(1)} %copy-done.1, f32[8,128]{1,0:T(8,128)S(1)} %collective-permute-done.8.left_ref, f32[8,128]{1,0:T(8,128)S(1)} %collective-permute-done.9.right_ref, ...), custom_call_target="tpu_custom_call" | custom-call | flops 100000000 | bytes 3000000 | tf_op jit(solution)/shard_map/pallas_call | solution.py:70
  109.1 10.1 %all_to_all.27.got_ref = f32[8,3,256]{2,1,0:T(4,128)S(1)} all-to-all(f32[8,3,256]{2,1,0:T(4,128)S(1)} %get-tuple-element.65), channel_id=1, replica_groups=mesh['zh'=4,'zl'=4,'x'=4,'c'=2,'y'=4] {'x','c'}, dimensions={0} | all-to-all | bytes 49152 | tf_op jit(solution)/shard_map/all_to_all | solution.py:534
  119.2 0.6 shard_map.78
  119.8 16.9 %all_to_all.28.got_ref = f32[16,3,256]{2,1,0:T(4,128)S(1)} all-to-all(f32[16,3,256]{2,1,0:T(4,128)S(1)} %get-tuple-element.66), channel_id=1, replica_groups=mesh['zh'=4,'zl'=4,'x'=4,'c'=2,'y'=4] {'zh','zl'}, dimensions={0} | all-to-all | bytes 98304 | tf_op jit(solution)/shard_map/all_to_all | solution.py:534
  136.7 1.6 %shard_map.79 = f32[3,8,256]{2,1,0:T(8,128)} custom-call(f32[16,3,256]{2,1,0:T(4,128)S(1)} %all_to_all.28.got_ref, f32[8,512]{1,0:T(8,128)S(1)} %get-tuple-element.67.both_ref, bf16[8,256,256]{2,1,0:T(8,128)(2,1)S(1)} %get-tuple-element.51.maps_ref, bf16[2,256,256]{2,1,0:T(8,128)(2,1)S(1)} %get-tuple-element.56.joint_ref, ...), custom_call_target="tpu_custom_call" | custom-call | flops 100000000 | bytes 4000000 | tf_op jit(solution)/shard_map/pallas_call | solution.py:684
Async XLA Ops:
  5.3 5.5 %copy-start.1 = (f32[3,8,256]{2,1,0:T(8,128)S(1)}, f32[3,8,256]{2,1,0:T(8,128)}, u32[]{:S(2)}) copy-start(f32[3,8,256]{2,1,0:T(8,128)} %stiff_ref.9) | copy-start | bytes 73732
  5.3 5.5 %copy-start.2 = (f32[3,8,256]{2,1,0:T(8,128)S(1)}, f32[3,8,256]{2,1,0:T(8,128)}, u32[]{:S(2)}) copy-start(f32[3,8,256]{2,1,0:T(8,128)} %u_ref.3) | copy-start | bytes 73732
  6.6 20.0 %all-to-all-start = ((f32[4,256,256]{2,1,0:T(8,128)}), f32[4,256,256]{2,1,0:T(8,128)}, u32[]{:S(2)}, u32[]{:S(2)}) async-start(f32[4,256,256]{2,1,0:T(8,128)} %get-tuple-element.37.after_ref), calls=%async_computation | async-start | bytes 2097152 | tf_op jit(solution)/shard_map/all_to_all | solution.py:534
  10.9 21.6 %copy-start = (bf16[4,512,512]{2,1,0:T(8,128)(2,1)S(1)}, bf16[4,512,512]{2,1,0:T(8,128)(2,1)}, u32[]{:S(2)}) copy-start(bf16[4,512,512]{2,1,0:T(8,128)(2,1)} %inv_ref.7) | copy-start | bytes 6291460
  10.9 21.6 %copy-start.3 = (f32[3,8,256]{2,1,0:T(8,128)S(1)}, f32[3,8,256]{2,1,0:T(8,128)}, u32[]{:S(2)}) copy-start(f32[3,8,256]{2,1,0:T(8,128)} %target_ref.1) | copy-start | bytes 73732
  10.9 21.6 %copy-start.4 = (f32[8,256]{1,0:T(8,128)S(1)}, f32[8,256]{1,0:T(8,128)}, u32[]{:S(2)}) copy-start(f32[8,256]{1,0:T(8,128)} %inertia_ref.1) | copy-start | bytes 24580
  10.9 21.6 %copy-start.5 = (s32[64]{0:T(128)S(1)}, s32[64]{0:T(128)}, u32[]{:S(2)}) copy-start(s32[64]{0:T(128)} %pin_ref.1) | copy-start | bytes 772
  11.0 6.6 %collective-permute-start = (f32[8,128]{1,0:T(8,128)S(1)}, f32[8,128]{1,0:T(8,128)S(1)}, u32[]{:S(2)}, u32[]{:S(2)}) collective-permute-start(f32[8,128]{1,0:T(8,128)S(1)} %get-tuple-element.38), channel_id=1, source_target_pairs={{0,1},{1,2},{2,3},{4,5},{5,6},{6,7},{8,9},{9,10},{10,11},{12,13},{... | collective-permute-start | bytes 12296 | tf_op jit(solution)/shard_map/ppermute | solution.py:577
  12.4 5.9 %collective-permute-start.1 = (f32[8,128]{1,0:T(8,128)S(1)}, f32[8,128]{1,0:T(8,128)S(1)}, u32[]{:S(2)}, u32[]{:S(2)}) collective-permute-start(f32[8,128]{1,0:T(8,128)S(1)} %get-tuple-element.39), channel_id=1, source_target_pairs={{1,0},{2,1},{3,2},{5,4},{6,5},{7,6},{9,8},{10,9},{11,10},{13,12},{... | collective-permute-start | bytes 12296 | tf_op jit(solution)/shard_map/ppermute | solution.py:576
  17.0 1.3 collective-permute-start.2
  28.6 9.5 %collective-permute-start.3 = (f32[256,256]{1,0:T(8,128)S(1)}, f32[256,256]{1,0:T(8,128)S(1)}, u32[]{:S(2)}, u32[]{:S(2)}) collective-permute-start(f32[256,256]{1,0:T(8,128)S(1)} %shard_map.67.after_ref.own_ref), channel_id=1, source_target_pairs={{0,32},{32,0},{64,96},{96,64},{128,160},{160,128},{192,224},{224,1... | collective-permute-start | bytes 786440 | tf_op jit(solution)/shard_map/ppermute | solution.py:589
  38.4 10.1 %collective-permute-start.4 = (f32[128,256]{1,0:T(8,128)S(1)}, f32[128,256]{1,0:T(8,128)S(1)}, u32[]{:S(2)}, u32[]{:S(2)}) collective-permute-start(f32[128,256]{1,0:T(8,128)S(1)} %get-tuple-element.45), channel_id=1, source_target_pairs={{0,64},{32,96},{64,0},{96,32},{128,192},{160,224},{192,128},{224,1... | collective-permute-start | bytes 393224 | tf_op jit(solution)/shard_map/ppermute | solution.py:617
  48.5 3.2 %collective-permute-start.5 = (f32[128,256]{1,0:T(8,128)S(1)}, f32[128,256]{1,0:T(8,128)S(1)}, u32[]{:S(2)}, u32[]{:S(2)}) collective-permute-start(f32[128,256]{1,0:T(8,128)S(1)} %collective-permute-done.4.mine_ref), channel_id=1, source_target_pairs={{0,4},{4,0},{1,5},{5,1},{2,6},{6,2},{3,7},{7,3},{8,12},{12,8},{9,1... | collective-permute-start | bytes 393224 | tf_op jit(solution)/shard_map/ppermute | solution.py:618
  52.0 20.7 %collective-permute-start.6 = (f32[128,256]{1,0:T(8,128)S(1)}, f32[128,256]{1,0:T(8,128)S(1)}, u32[]{:S(2)}, u32[]{:S(2)}) collective-permute-start(f32[128,256]{1,0:T(8,128)S(1)} %shard_map.71.after_ref), channel_id=1, source_target_pairs={{128,0},{160,32},{192,64},{224,96},{256,384},{288,416},{320,448},{... | collective-permute-start | bytes 393224 | tf_op jit(solution)/shard_map/ppermute | solution.py:621
  72.7 3.2 %collective-permute-start.7 = (f32[128,256]{1,0:T(8,128)S(1)}, f32[128,256]{1,0:T(8,128)S(1)}, u32[]{:S(2)}, u32[]{:S(2)}) collective-permute-start(f32[128,256]{1,0:T(8,128)S(1)} %collective-permute-done.6.mine_ref), channel_id=1, source_target_pairs={{0,4},{4,0},{1,5},{5,1},{2,6},{6,2},{3,7},{7,3},{8,12},{12,8},{9,1... | collective-permute-start | bytes 393224 | tf_op jit(solution)/shard_map/ppermute | solution.py:642
  98.7 7.2 %collective-permute-start.8 = (f32[8,128]{1,0:T(8,128)S(1)}, f32[8,128]{1,0:T(8,128)S(1)}, u32[]{:S(2)}, u32[]{:S(2)}) collective-permute-start(f32[8,128]{1,0:T(8,128)S(1)} %get-tuple-element.59), channel_id=1, source_target_pairs={{0,1},{1,2},{2,3},{4,5},{5,6},{6,7},{8,9},{9,10},{10,11},{12,13},{... | collective-permute-start | bytes 12296 | tf_op jit(solution)/shard_map/ppermute | solution.py:666
  100.0 5.9 %collective-permute-start.9 = (f32[8,128]{1,0:T(8,128)S(1)}, f32[8,128]{1,0:T(8,128)S(1)}, u32[]{:S(2)}, u32[]{:S(2)}) collective-permute-start(f32[8,128]{1,0:T(8,128)S(1)} %get-tuple-element.60), channel_id=1, source_target_pairs={{1,0},{2,1},{3,2},{5,4},{6,5},{7,6},{9,8},{10,9},{11,10},{13,12},{... | collective-permute-start | bytes 12296 | tf_op jit(solution)/shard_map/ppermute | solution.py:665
  104.6 3.1 %collective-permute-start.10 = (f32[4,256]{1,0:T(4,128)S(1)}, f32[4,256]{1,0:T(4,128)S(1)}, u32[]{:S(2)}, u32[]{:S(2)}) collective-permute-start(f32[4,256]{1,0:T(4,128)S(1)} %get-tuple-element.61), channel_id=1, source_target_pairs={{4,0},{8,4},{12,8},{16,12},{20,16},{24,20},{28,24},{32,28},{36,32}... | collective-permute-start | bytes 12296 | tf_op jit(solution)/shard_map/ppermute | solution.py:664

commit v3 on v2

--- a/solution.py
+++ b/solution.py
@@ -112,109 +112,120 @@
 
 def chip_map_kernel(both_ref, out_ref, near_ref):
     core = lax.axis_index("c")
-    product = mm(pair(both_ref[0, 0:CB, :]), pair(both_ref[1, 0:CB, :]))
-    for k in range(4):
-        out_ref[k] = product
+    out_ref[...] = mm(pair(both_ref[0, 0:CB, :]), pair(both_ref[1, 0:CB, :]))
     tails = [both_ref[k, CB : CB + 8, :] for k in range(2)]
     near_ref[...] = jnp.where(core == 0, tails[1], tails[0])
 
 
-def plane_product_kernel(chips_hbm, *rest):
-    out_ref, chips_ref, sems = rest[-3:]
-    copies = [
-        pltpu.make_async_copy(chips_hbm.at[k], chips_ref.at[k], sems.at[k]) for k in range(4)
-    ]
-    for copy in copies:
-        copy.start()
-    copies[0].wait()
-    copies[1].wait()
-    left = mm(pair(chips_ref[0]), pair(chips_ref[1]))
-    copies[2].wait()
-    copies[3].wait()
-    right = mm(pair(chips_ref[2]), pair(chips_ref[3]))
-    out_ref[...] = mm(pair(left), pair(right))
-
-
-def low_bit():
-    return lax.rem(lax.axis_index("zl"), 2)
-
-
-def high_bit():
-    return lax.div(lax.axis_index("zl"), 2)
-
-
-def own_half(ref):
-    return ref[pl.ds(pl.multiple_of(lax.axis_index("c") * 128, 128), 128), :]
+def low_bit(axis="zl"):
+    return lax.rem(lax.axis_index(axis), 2)
+
+
+def high_bit(axis="zl"):
+    return lax.div(lax.axis_index(axis), 2)
+
+
+def in_order(own, other, right):
+    return jnp.where(right, other, own), jnp.where(right, own, other)
+
+
+def two_chips_kernel(own_ref, other_ref, cross_ref, from_left_ref, from_right_ref, out_ref, row_ref):
+    left_map, right_map = in_order(own_ref[...], other_ref[...], low_bit("x") == 1)
+    out_ref[...] = mm(pair(left_map), pair(right_map))
+    row_ref[...] = cross_ref[...]
+
+
+def four_chips_kernel(own_ref, other_ref, after_ref, out_ref):
+    left_map, right_map = in_order(own_ref[...], other_ref[...], high_bit("x") == 1)
+    out_ref[...] = mm(pair(left_map), pair(right_map))
+
+
+def rows_of_half(half):
+    return jnp.concatenate([half[:128], half[128:]], axis=1)
+
+
+def half_of_rows(rows):
+    return jnp.concatenate([rows[:, :128], rows[:, 128:]], axis=0)
 
 
 def joined(mine_ref, other_ref):
     core = lax.axis_index("c")
-    mine, other = mine_ref[...], other_ref[...]
-    top = jnp.where(core == 0, mine, other)
-    return jnp.concatenate([top, jnp.where(core == 0, other, mine)], axis=0)
+    first, second = in_order(mine_ref[...], other_ref[...], core == 1)
+    columns = jnp.concatenate([first, second], axis=1)
+    rows = jnp.concatenate([rows_of_half(first), rows_of_half(second)], axis=0)
+    return jnp.where(high_bit() == 0, columns, rows)
 
 
 def two_planes_kernel(own_ref, other_ref, *rest):
     out_ref, half_ref = rest[-2:]
-    right = low_bit() == 1
-    left_map = jnp.where(right, other_ref[...], own_ref[...])
-    right_map = jnp.where(right, own_ref[...], other_ref[...])
-    out_ref[...] = mm(pair(left_map), pair(right_map))
-    half_ref[...] = own_half(out_ref)
-
-
-def four_planes_kernel(own_ref, mine_ref, other_ref, out_ref):
-    right = high_bit() == 1
-    left_map = jnp.where(right, mine_ref[...], own_half(own_ref))
-    right_map = jnp.where(right, own_ref[...], joined(mine_ref, other_ref))
-    out_ref[...] = mm(pair(left_map), pair(right_map))
-
-
-def plane_maps_kernel(chips_ref, cores_ref, after_ref, wh_ref, wl_ref, eh_ref, el_ref, suf_ref, cur_ref):
-    x = lax.axis_index("x")
+    core = lax.axis_index("c")
+    left_map, right_map = in_order(own_ref[...], other_ref[...], low_bit() == 1)
+    product = mm(pair(left_map), pair(right_map))
+    out_ref[...] = product
+    columns = jnp.where(core == 0, product[:, :128], product[:, 128:])
+    rows = half_of_rows(jnp.where(core == 0, product[:128], product[128:]))
+    half_ref[...] = jnp.where(high_bit() == 0, rows, columns)
+
+
+def four_planes_kernel(own_ref, half_ref, out_ref):
+    own = pair(own_ref[...])
+    half = half_ref[...]
+    columns = mm(own, pair(half))
+    rows = half_of_rows(mm(pair(rows_of_half(half)), own))
+    out_ref[...] = jnp.where(high_bit() == 0, columns, rows)
+
+
+def plane_maps_kernel(
+    own_ref, sib_ref, two_ref, far_ref, cores_ref, after_ref, wh_ref, wl_ref, eh_ref, el_ref, sends_ref
+):
     core = lax.axis_index("c")
     one = eye()
-    chips = [pair(chips_ref[k]) for k in range(4)]
+    low, high = low_bit("x"), high_bit("x")
+    own, sib, two, far = own_ref[...], sib_ref[...], two_ref[...], far_ref[...]
+    first, second = cores_ref[0, 0:CB, :], cores_ref[1, 0:CB, :]
 
     def store(slot, col, value):
-        high, low = pair(value)
-        wh_ref[slot * CB : (slot + 1) * CB, col * CB : (col + 1) * CB] = high
-        wl_ref[slot * CB : (slot + 1) * CB, col * CB : (col + 1) * CB] = low
-
-    suffix = one
-    suf_ref[3] = suffix
-    store(3, 0, suffix)
-    for k in (2, 1, 0):
-        if k == 2:
-            suffix = chips_ref[3]
-        else:
-            suffix = mm(chips[k + 1], pair(suffix))
-        suf_ref[k] = suffix
-        store(k, 0, suffix)
-    store(4, 0, mm(pair(cores_ref[1, 0:CB, :]), pair(suf_ref[x])))
-    store(4, 1, jnp.where(core == 1, one, 0.0))
-    cur_ref[...] = jnp.where(core == 1, cores_ref[0, 0:CB, :], one)
-    for k in (3, 2, 1, 0):
-
-        @pl.when(k < x)
-        def _():
-            current = cur_ref[...]
-            store(k, 1, current)
-            cur_ref[...] = mm(chips[k], pair(current))
-
-        @pl.when(k >= x)
-        def _():
-            store(k, 1, jnp.zeros((CB, CB), F32))
-
-    high, low = pair(cur_ref[...])
-    eh_ref[...] = high
-    el_ref[...] = low
-
-
-def group_maps_kernel(one_ref, mine_ref, other_ref, after_ref, out_ref, s_ref, e_ref):
+        parts = pair(value)
+        wh_ref[slot * CB : (slot + 1) * CB, col * CB : (col + 1) * CB] = parts[0]
+        wl_ref[slot * CB : (slot + 1) * CB, col * CB : (col + 1) * CB] = parts[1]
+
+    sib_after = jnp.where(low == 0, sib, one)
+    rest = pair(jnp.where(high == 0, far, one))
+    to_end = mm(pair(sib_after), rest)
+    store(0, 0, mm(pair(second), pair(to_end)))
+    store(1, 0, to_end)
+    store(2, 0, mm(pair(jnp.where(low == 0, one, own)), rest))
+    store(3, 0, jnp.where(high == 1, two, one))
+    none = jnp.zeros((CB, CB), F32)
+    core_before = jnp.where(core == 1, first, one)
+    chip_before = mm(pair(jnp.where(low == 1, sib, one)), pair(core_before))
+    store(0, 1, jnp.where(core == 1, one, none))
+    store(1, 1, none)
+    store(2, 1, jnp.where(low == 1, core_before, none))
+    store(3, 1, jnp.where(high == 1, chip_before, none))
+    parts = pair(mm(pair(jnp.where(high == 1, far, one)), pair(chip_before)))
+    eh_ref[...] = parts[0]
+    el_ref[...] = parts[1]
+    core_after = jnp.where(core == 0, second, one)
+    parts = pair(core_after)
+    sends_ref[0] = parts[0]
+    sends_ref[1] = parts[1]
+    parts = pair(mm(parts, pair(sib_after)))
+    sends_ref[2] = parts[0]
+    sends_ref[3] = parts[1]
+
+
+def bundle_kernel(two_ref, far_ref, after_ref, out_ref):
+    out_ref[0] = two_ref[...]
+    out_ref[1] = far_ref[...]
+
+
+def group_maps_kernel(both_ref, one_ref, mine_ref, other_ref, out_ref, joint_ref, msg_ref):
+    zh = lax.axis_index("zh")
     one = eye()
     sibling = one_ref[...]
-    two = pair(joined(mine_ref, other_ref))
+    two = pair(joined(mine_ref.at[0], other_ref.at[0]))
+    far = joined(mine_ref.at[1], other_ref.at[1])
     send = jnp.where(low_bit() == 0, sibling, one)
     take = jnp.where(low_bit() == 1, sibling, one)
     for k, value in ((0, send), (4, take)):
@@ -227,18 +238,12 @@
         parts = pair(value)
         out_ref[k] = parts[0]
         out_ref[k + 1] = parts[1]
-    s_ref[...] = send
-    e_ref[...] = take
-
-
-def joint_map(mine_ref, other_ref, s_ref, e_ref, out_ref):
-    zh = lax.axis_index("zh")
-    far = joined(mine_ref, other_ref)
-    left = jnp.where(zh == 0, s_ref[...], far)
-    right = jnp.where(zh == 0, far, e_ref[...])
+    left = jnp.where(zh == 0, send, far)
+    right = jnp.where(zh == 0, far, take)
     joint = pair(mm(pair(left), pair(right)))
-    out_ref[0] = joint[0]
-    out_ref[1] = joint[1]
+    joint_ref[0] = joint[0]
+    joint_ref[1] = joint[1]
+    send_vectors(both_ref[:, :CB], out_ref, joint_ref, msg_ref)
 
 
 def edge_tiles(comps, weights):
@@ -341,19 +346,22 @@
     return jnp.concatenate(rows + [jnp.zeros((5, CB), F32)], axis=0)
 
 
-def write_offsets(offset, chip_ref, msg_ref):
+def write_offsets(offset, sends_ref, msg_ref):
     core = lax.axis_index("c")
     x = lax.axis_index("x")
-    chip = pair(chip_ref[1, 0:CB, :])
-    onward = apply_map(stacked(offset), chip[0], chip[1])[0:3]
+    vec = stacked(offset)
     raw = offset[0:3]
-    onward = jnp.where(core == 0, onward, raw)
-    for j in range(8):
-        msg_ref[j] = jnp.where(x == j // 2, raw, onward)
-
-
-def offsets_kernel(offset_ref, chip_ref, after_ref, msg_ref):
-    write_offsets(offset_ref[...], chip_ref, msg_ref)
+    beside = jnp.where(core == 0, apply_map(vec, sends_ref[0], sends_ref[1])[0:3], raw)
+    far = apply_map(vec, sends_ref[2], sends_ref[3])[0:3]
+    for k in range(4):
+        value = jnp.where(high_bit("x") == k // 2, beside, far)
+        value = jnp.where(x == k, raw, value)
+        msg_ref[2 * k] = value
+        msg_ref[2 * k + 1] = value
+
+
+def offsets_kernel(offset_ref, sends_ref, after_ref, msg_ref):
+    write_offsets(offset_ref[...], sends_ref, msg_ref)
 
 
 def first_side_kernel(
@@ -400,7 +408,7 @@
 
 
 def second_side_kernel(
-    u_ref, stiff_ref, left_ref, right_ref, row_ref, inv_ref, chip_ref, inertial_ref, ext_ref,
+    u_ref, stiff_ref, left_ref, right_ref, row_ref, inv_ref, sends_ref, inertial_ref, ext_ref,
     above_ref, base_ref, msg_ref,
 ):
     core = lax.axis_index("c")
@@ -417,16 +425,19 @@
         [row_ref[k : k + 1, :] for k in range(3)], above_rows, above_weight, ext_ref[0], ext_ref[1],
         vertical, stiff_ref, inv_ref, base_ref,
     )
-    write_offsets(offset, chip_ref, msg_ref)
+    write_offsets(offset, sends_ref, msg_ref)
 
 
 def plane_vectors(got_ref, wh_ref, wl_ref, vec_ref):
     x = lax.axis_index("x")
+    sib = x + 1 - 2 * low_bit("x")
+    far = 4 - 4 * high_bit("x")
     vec_ref[...] = jnp.zeros(vec_ref.shape, F32)
-    for k in range(4):
-        own = got_ref[2 * k + 1]
-        put_vector(vec_ref, k, jnp.where(x == k, own, own + got_ref[2 * k]))
-    put_vector(vec_ref, 4, got_ref[2 * x])
+    put_vector(vec_ref, 0, got_ref[2 * x])
+    put_vector(vec_ref, 1, got_ref[2 * x + 1])
+    put_vector(vec_ref, 2, got_ref[2 * sib] + got_ref[2 * sib + 1])
+    others = (got_ref[far] + got_ref[far + 1]) + (got_ref[far + 2] + got_ref[far + 3])
+    put_vector(vec_ref, 3, others)
     return apply_map(vec_ref[...].astype(BF16), wh_ref[...], wl_ref[...])
 
 
@@ -448,11 +459,6 @@
 
 def plane_kernel(got_ref, wh_ref, wl_ref, both_ref, vec_ref):
     both_ref[...] = plane_vectors(got_ref, wh_ref, wl_ref, vec_ref)
-
-
-def send_kernel(both_ref, maps_ref, mine_ref, other_ref, s_ref, e_ref, joint_ref, msg_ref):
-    joint_map(mine_ref, other_ref, s_ref, e_ref, joint_ref)
-    send_vectors(both_ref[:, :CB], maps_ref, joint_ref, msg_ref)
 
 
 def plane_send_kernel(got_ref, wh_ref, wl_ref, maps_ref, joint_ref, both_ref, msg_ref, vec_ref):
@@ -492,7 +498,7 @@
             source = [jnp.broadcast_to(came[j : j + 1], (8, CB)) for j in range(3)]
         else:
             source = [weights * state[j] for j in range(3)]
-        moved = halves_sum(dot_t(stacked(jnp.concatenate(source + [blank], axis=0)), inv_ref[k]))
+        moved = halves_sum(dot_t(stacked(jnp.concatenate(source + [blank], axis=0)), inv_ref[k, :, :CB]))
         for j in range(3):
             part = moved[8 * j : 8 * j + 8]
             state[j] = state[j] + jnp.where(
@@ -537,10 +543,6 @@
 def shards(positions, target, inertia, stiffness, pin_columns, inverses):
     smem = pl.BlockSpec(memory_space=pltpu.SMEM)
     anywhere = pl.BlockSpec(memory_space=pl.ANY)
-    grid = (1,)
-
-    def full(shape):
-        return pl.BlockSpec(shape, lambda i: (0,) * len(shape))
 
     hbm = pl.BlockSpec(memory_space=pltpu.HBM)
     own_map = call(
@@ -558,33 +560,32 @@
         limit=WHOLE_VMEM,
     )
     core_maps = lax.all_gather(own_map, "c")
-    chip_copies, near = call(chip_map_kernel, [sds((4, CB, CB)), sds((8, CB))], (core_maps,))
-    chips = swap(chip_copies, "x")
+    square = sds((CB, CB))
+    chip, near = call(chip_map_kernel, [square, sds((8, CB))], (core_maps,))
+    sib_chip = lax.ppermute(chip, "x", [(k, k ^ 1) for k in range(4)])
 
     tile = sds((8, 128))
     rows = sds((4, CB))
     left, right, cross = call(
-        halo_kernel,
-        [tile, tile, rows],
-        (positions, stiffness, chip_copies),
-        specs=[None, None, anywhere],
-    )
-    pairs = [(2 * k + 1, 2 * k + 2) for k in range(63)]
+        halo_kernel, [tile, tile, rows], (positions, stiffness, chip), specs=[None, None, anywhere]
+    )
     to_left = [(1, 0), (2, 1), (3, 2)]
     to_right = [(0, 1), (1, 2), (2, 3)]
     cores = [(0, 1), (1, 0)]
     from_right = lax.ppermute(left, "y", to_left)
     from_left = lax.ppermute(right, "y", to_right)
+    two_chips, cross = call(
+        two_chips_kernel,
+        [square, rows],
+        (chip, sib_chip, cross, from_left, from_right),
+        specs=[None] * 3 + [anywhere] * 2,
+    )
+    far_chips = lax.ppermute(two_chips, "x", [(k, k ^ 2) for k in range(4)])
+    pairs = [(2 * k + 1, 2 * k + 2) for k in range(63)]
     cross = lax.ppermute(cross, STRIP, pairs + [(b, a) for a, b in pairs])
     halos = (from_left, from_right, near, cross)
-
-    square = sds((CB, CB))
     plane = call(
-        plane_product_kernel,
-        square,
-        (chips, from_left, from_right, cross),
-        specs=[hbm] + [anywhere] * 3,
-        scratch=[pltpu.VMEM((4, CB, CB), F32), pltpu.SemaphoreType.DMA((4,))],
+        four_chips_kernel, square, (two_chips, far_chips, cross), specs=[None, None, anywhere]
     )
     beside = lax.ppermute(plane, ZAX, [(k, k ^ 1) for k in range(16)])
 
@@ -598,16 +599,16 @@
         flops=10**8,
         size=3 * 10**6,
     )
-    wide = sds((5 * CB, 2 * CB), BF16)
-    xh, xl, eh, el = call(
+    wide = sds((4 * CB, 2 * CB), BF16)
+    narrow = sds((CB, CB), BF16)
+    xh, xl, eh, el, sends = call(
         plane_maps_kernel,
-        [wide, wide, sds((CB, CB), BF16), sds((CB, CB), BF16)],
-        (chips, core_maps, plane),
-        specs=[None, None, anywhere],
-        scratch=[pltpu.VMEM((4, CB, CB), F32), pltpu.VMEM((CB, CB), F32)],
+        [wide, wide, narrow, narrow, sds((4, CB, CB), BF16)],
+        (chip, sib_chip, two_chips, far_chips, core_maps, plane),
+        specs=[None] * 5 + [anywhere],
         flops=10**9,
     )
-    half = sds((128, CB))
+    half = sds((CB, 128))
     two, two_half = call(
         two_planes_kernel,
         [square, half],
@@ -615,51 +616,39 @@
         specs=[None, None, anywhere, anywhere],
     )
     two_mine = lax.ppermute(two_half, ZAX, [(k, k ^ 2) for k in range(16)])
-    two_other = lax.ppermute(two_mine, "c", cores)
-    group_half = call(four_planes_kernel, half, (two, two_mine, two_other))
+    group_half = call(four_planes_kernel, half, (two, two_mine))
     steps = [(4 + k, k) for k in range(4)] + [(8 + k, 12 + k) for k in range(4)]
     far_mine = lax.ppermute(group_half, ZAX, steps)
 
     msg = call(
-        offsets_kernel, sds((8, 3, CB)), (offset, core_maps, group_half), specs=[None, None, anywhere]
+        offsets_kernel, sds((8, 3, CB)), (offset, sends, group_half), specs=[None, None, anywhere]
     )
     got = swap(msg, PLANE)
     both = call(
         plane_kernel,
         sds((8, 2 * CB)),
         (got, xh, xl),
-        scratch=[pltpu.VMEM((16, 5 * CB), F32)],
+        scratch=[pltpu.VMEM((16, 4 * CB), F32)],
         size=3 * 10**6,
     )
-    maps, send_map, take_map = call(
+    mine = call(
+        bundle_kernel, sds((2, CB, 128)), (two_mine, far_mine, both), specs=[None, None, anywhere]
+    )
+    other = lax.ppermute(mine, "c", cores)
+    maps, joint, msg = call(
         group_maps_kernel,
-        [sds((8, CB, CB), BF16), square, square],
-        (beside, two_mine, two_other, both),
-        specs=[None, None, None, anywhere],
+        [sds((8, CB, CB), BF16), sds((2, CB, CB), BF16), sds((16, 3, CB))],
+        (both, beside, mine, other),
         flops=5 * 10**8,
     )
-    far_mine, both, maps = lax.optimization_barrier((far_mine, both, maps))
-    far_other = lax.ppermute(far_mine, "c", cores)
-    joint, msg = call(
-        send_kernel,
-        [sds((2, CB, CB), BF16), sds((16, 3, CB))],
-        (both, maps, far_mine, far_other, send_map, take_map),
-    )
     got = swap(msg, ZAX)
-    sizes = ((16, 3, CB), (8, 2 * CB), (8, CB, CB), (2, CB, CB), (CB, CB), (CB, CB), (3, 8, CB), (3, 8, CB))
-    finish_specs = [full(s) for s in sizes] + [pl.BlockSpec((4, 2 * CB, CB), lambda i: (0, 0, 0))]
-    params = pltpu.CompilerParams(vmem_limit_bytes=VMEM_LIMIT)
-    cost = pl.CostEstimate(flops=10**8, bytes_accessed=4 * 10**6, transcendentals=0)
-    middle, left, right, low_row = pl.pallas_call(
+    middle, left, right, low_row = call(
         middle_kernel,
-        grid=grid,
-        out_shape=[sds((4, 8, CB)), tile, tile, rows],
-        in_specs=finish_specs,
-        out_specs=[full((4, 8, CB)), full((8, 128)), full((8, 128)), full((4, CB))],
-        scratch_shapes=[pltpu.VMEM((16, 3 * CB), F32)],
-        compiler_params=params,
-        cost_estimate=cost,
-    )(got, both, maps, joint, eh, el, stiffness, base, inverses)
+        [sds((4, 8, CB)), tile, tile, rows],
+        (got, both, maps, joint, eh, el, stiffness, base, inverses),
+        scratch=[pltpu.VMEM((16, 3 * CB), F32)],
+        flops=10**8,
+    )
 
     low_row = lax.ppermute(low_row, STRIP, [(k + 1, k) for k in range(127)])
     from_right = lax.ppermute(left, "y", to_left)
@@ -667,7 +656,7 @@
     base, msg = call(
         second_side_kernel,
         [field, sds((8, 3, CB))],
-        (middle, stiffness, from_left, from_right, low_row, inverses, core_maps)
+        (middle, stiffness, from_left, from_right, low_row, inverses, sends)
         + (inertial, ext, above),
         flops=10**8,
         size=3 * 10**6,
@@ -677,20 +666,17 @@
         plane_send_kernel,
         [sds((8, 2 * CB)), sds((16, 3, CB))],
         (got, xh, xl, maps, joint),
-        scratch=[pltpu.VMEM((16, 5 * CB), F32)],
+        scratch=[pltpu.VMEM((16, 4 * CB), F32)],
         size=3 * 10**6,
     )
     got = swap(msg, ZAX)
-    return pl.pallas_call(
+    return call(
         final_kernel,
-        grid=grid,
-        out_shape=field,
-        in_specs=finish_specs,
-        out_specs=full((3, 8, CB)),
-        scratch_shapes=[pltpu.VMEM((16, 3 * CB), F32)],
-        compiler_params=params,
-        cost_estimate=cost,
-    )(got, both, maps, joint, eh, el, stiffness, base, inverses)
+        field,
+        (got, both, maps, joint, eh, el, stiffness, base, inverses),
+        scratch=[pltpu.VMEM((16, 3 * CB), F32)],
+        flops=10**8,
+    )
 
 
 def solution(mesh):

time: 139 us -> 137 us (0.986)
  waiting for transfers between devices: 28.3 us -> 18.7 us
  Pallas kernels: 17.4 us -> 13.8 us
  starting transfers between devices: 32.2 us -> 35.8 us
  blocking collectives: 60.2 us -> 63.6 us
  local copies, waits for them, and re-layouts: 0.03 us -> 2.87 us
    all_to_all x1 -> x0, waiting for transfers between devices: 8.33 us -> none  [swap(): return lax.all_to_all(value, axes, 0, 0)]
    ppermute x2 -> x3, starting transfers between devices: 3.82 us -> 9.97 us  [the longest x1 4.64 us: shards(): far_chips = lax.ppermute(two_chips, 'x', [(k, k ^ 2) for k in range(4)])]
    all_to_all x1 -> x0, starting transfers between devices: 4.29 us -> none  [swap(): return lax.all_to_all(value, axes, 0, 0)]
    ppermute x1, waiting for transfers between devices: 8.79 us -> 4.65 us  [shards(): far_mine = lax.ppermute(group_half, ZAX, steps)]
    ppermute x2 -> x3, waiting for transfers between devices: 2.63 us -> 6.55 us  [the longest x1 5.05 us: shards(): far_chips = lax.ppermute(two_chips, 'x', [(k, k ^ 2) for k in range(4)])]
    all_to_all x4, blocking collectives: 57.8 us -> 61 us  [swap(): return lax.all_to_all(value, axes, 0, 0)]
    unnamed x12 -> x14, local copies, waits for them, and re-layouts: 0.03 us -> 2.87 us
    pallas_call x2 -> x0, Pallas kernels: 2.59 us -> none  [the longest x1 1.57 us: shards(): pl.pallas_call(final_kernel, grid=grid, out_shape=field, in_specs=finish_...]
  transfers between devices with their start and end apart: 12 -> 12, of which waited for: 8 -> 6; matrix products, arithmetic and copies ran while one was open for 0% -> 0% of each run, Pallas kernels for 4% -> 3%
where the time goes in v3:
time: 137 us; the launch traced here: 135 us
  blocking collectives  63.6 us (46%)
  starting transfers between devices  35.8 us (26%)
  waiting for transfers between devices  18.7 us (14%)
  Pallas kernels  13.8 us (10%)
  local copies, waits for them, and re-layouts  2.87 us (2%)
    all_to_all x4, blocking collectives, swap(): return lax.all_to_all(value, axes, 0, 0)  61 us
    pallas_call x17, Pallas kernels, call(): pl.pallas_call(kernel, out_shape=outs, in_specs=in_specs, out_specs=out_s...  13.8 us
    ppermute x2, starting transfers between devices, shards(): from_right = lax.ppermute(left, 'y', to_left)  9.68 us
    ppermute x1, starting transfers between devices, shards(): two_mine = lax.ppermute(two_half, ZAX, [(k, k ^ 2) for k in range(16)])  5.18 us
    ppermute x1, starting transfers between devices, shards(): beside = lax.ppermute(plane, ZAX, [(k, k ^ 1) for k in range(16)])  5.14 us
    ppermute x1, waiting for transfers between devices, shards(): far_chips = lax.ppermute(two_chips, 'x', [(k, k ^ 2) for k in range(4)])  5.05 us
    ppermute x1, waiting for transfers between devices, shards(): far_mine = lax.ppermute(group_half, ZAX, steps)  4.65 us
    ppermute x1, starting transfers between devices, shards(): far_chips = lax.ppermute(two_chips, 'x', [(k, k ^ 2) for k in range(4)])  4.64 us
  transfers between devices with their start and end apart: 12, of which 6 were waited for; matrix products, arithmetic and copies ran while one was open for 0% of the time, Pallas kernels for 3%

profile of v3, /device:TPU:24, one launch (start us, length us, event | category | flops | bytes accessed | tf_op | source)
XLA Modules:
  0.0 135.0 jit_solution(9788826440609013969)
XLA Ops:
  0.0 0.0 copy-start.1
  0.0 0.0 copy-start.5
  0.0 2.9 %shard_map.64 = f32[264,256]{1,0:T(8,128)} custom-call(bf16[4,512,512]{2,1,0:T(8,128)(2,1)} %inv_ref.7, f32[3,8,256]{2,1,0:T(8,128)} %stiff_ref.9, f32[3,8,256]{2,1,0:T(8,128)} %u_ref.3), custom_call_target="tpu_custom_call" | custom-call | flops 100000000 | bytes 1000000 | tf_op jit(solution)/shard_map/pallas_call | solution.py:70
  2.9 0.0 copy-start
  2.9 2.5 %all-gather = f32[528,256]{1,0:T(8,128)S(1)} all-gather(f32[264,256]{1,0:T(8,128)} %shard_map.64), channel_id=2, replica_groups=mesh['zh'=4,'zl'=4,'x'=4,'c'=2,'y'=4] {'c'}, dimensions={0}, use_global_device_ids=true | all-gather | bytes 811008 | tf_op jit(solution)/shard_map/all_gather | solution.py:562
  5.5 0.3 shard_map.65
  5.8 3.4 %collective-permute-start.2 = (f32[256,256]{1,0:T(8,128)S(1)}, f32[256,256]{1,0:T(8,128)S(1)}, u32[]{:S(2)}, u32[]{:S(2)}) collective-permute-start(f32[256,256]{1,0:T(8,128)S(1)} %get-tuple-element.35.after_ref.own_ref), channel_id=1, source_target_pairs={{0,8},{8,0},{16,24},{24,16},{1,9},{9,1},{17,25},{25,17},{2,10},{10... | collective-permute-start | bytes 786440 | tf_op jit(solution)/shard_map/ppermute | solution.py:565
  9.2 0.0 copy-done.1
  9.2 0.0 copy-start.2
  9.2 0.7 copy-done.2
  9.9 0.1 shard_map.66
  10.0 1.3 collective-permute-start
  11.3 4.5 %collective-permute-start.1 = (f32[8,128]{1,0:T(8,128)S(1)}, f32[8,128]{1,0:T(8,128)S(1)}, u32[]{:S(2)}, u32[]{:S(2)}) collective-permute-start(f32[8,128]{1,0:T(8,128)S(1)} %get-tuple-element.37), channel_id=1, source_target_pairs={{1,0},{2,1},{3,2},{5,4},{6,5},{7,6},{9,8},{10,9},{11,10},{13,12},{... | collective-permute-start | bytes 12296 | tf_op jit(solution)/shard_map/ppermute | solution.py:575
  15.8 0.0 collective-permute-done.from_left_ref.left_ref
  15.8 1.3 collective-permute-done.1.from_right_ref.right_ref
  17.1 0.0 collective-permute-done.2.other_ref.sib_ref
  17.1 0.3 shard_map.67
  17.4 4.6 %collective-permute-start.4 = (f32[256,256]{1,0:T(8,128)S(1)}, f32[256,256]{1,0:T(8,128)S(1)}, u32[]{:S(2)}, u32[]{:S(2)}) collective-permute-start(f32[256,256]{1,0:T(8,128)S(1)} %get-tuple-element.41.own_ref.two_ref), channel_id=1, source_target_pairs={{0,16},{8,24},{16,0},{24,8},{1,17},{9,25},{17,1},{25,9},{2,18},{10... | collective-permute-start | bytes 786440 | tf_op jit(solution)/shard_map/ppermute | solution.py:583
  22.1 0.7 collective-permute-start.3
  22.8 0.0 collective-permute-done.3.after_ref.cross_ref
  22.8 5.0 %collective-permute-done.4.other_ref.far_ref = f32[256,256]{1,0:T(8,128)S(1)} collective-permute-done((f32[256,256]{1,0:T(8,128)S(1)}, f32[256,256]{1,0:T(8,128)S(1)}, u32[]{:S(2)}, u32[]{:S(2)}) %collective-permute-start.4) | collective-permute-done | bytes 262176 | tf_op jit(solution)/shard_map/ppermute | solution.py:583
  27.8 0.3 shard_map.68.after_ref.own_ref
  28.1 5.1 %collective-permute-start.5 = (f32[256,256]{1,0:T(8,128)S(1)}, f32[256,256]{1,0:T(8,128)S(1)}, u32[]{:S(2)}, u32[]{:S(2)}) collective-permute-start(f32[256,256]{1,0:T(8,128)S(1)} %shard_map.68.after_ref.own_ref), channel_id=1, source_target_pairs={{0,32},{32,0},{64,96},{96,64},{128,160},{160,128},{192,224},{224,1... | collective-permute-start | bytes 786440 | tf_op jit(solution)/shard_map/ppermute | solution.py:590
  33.3 0.0 copy-done.5
  33.3 0.0 copy-done
  33.3 0.0 copy-start.3
  33.3 0.7 copy-done.3
  34.0 0.0 copy-start.4
  34.0 0.7 copy-done.4
  34.8 0.0 copy-start.6
  34.8 0.7 copy-done.6
  35.4 1.9 %shard_map.69 = (f32[3,8,256]{2,1,0:T(8,128)S(1)}, f32[8,256]{1,0:T(8,128)S(1)}, f32[3,8,256]{2,1,0:T(8,128)S(1)}, f32[2,8,512]{2,1,0:T(8,128)S(1)}, f32[8,256]{1,0:T(8,128)S(1)}) custom-call(f32[3,8,256]{2,1,0:T(8,128)S(1)} %copy-done.3, f32[3,8,256]{2,1,0:T(8,128)S(1)} %copy-done.4, f32[8,256]{1,0:T(8,128)S(1)} %copy-done.5, f32[3,8,256]{2,1,0:T(8,128)S(1)} %copy-done.1, ...), custom_call_target="tpu_custom_call" | custom-call | flops 100000000 | bytes 3000000 | tf_op jit(solution)/shard_map/pallas_call | solution.py:70
  37.3 1.3 shard_map.70
  38.6 0.0 collective-permute-done.5.other_ref.one_ref
  38.6 0.3 shard_map.71
  38.9 5.2 %collective-permute-start.6 = (f32[256,128]{1,0:T(8,128)S(1)}, f32[256,128]{1,0:T(8,128)S(1)}, u32[]{:S(2)}, u32[]{:S(2)}) collective-permute-start(f32[256,128]{1,0:T(8,128)S(1)} %get-tuple-element.47), channel_id=1, source_target_pairs={{0,64},{32,96},{64,0},{96,32},{128,192},{160,224},{192,128},{224,1... | collective-permute-start | bytes 393224 | tf_op jit(solution)/shard_map/ppermute | solution.py:618
  44.1 4.4 %collective-permute-done.6.half_ref.two_ref = f32[256,128]{1,0:T(8,128)S(1)} collective-permute-done((f32[256,128]{1,0:T(8,128)S(1)}, f32[256,128]{1,0:T(8,128)S(1)}, u32[]{:S(2)}, u32[]{:S(2)}) %collective-permute-start.6) | collective-permute-done | bytes 131104 | tf_op jit(solution)/shard_map/ppermute | solution.py:618
  48.6 0.3 shard_map.72.after_ref
  48.9 1.3 collective-permute-start.7
  50.2 0.2 shard_map.73
  50.4 11.1 %all_to_all.20.got_ref = f32[8,3,256]{2,1,0:T(4,128)S(1)} all-to-all(f32[8,3,256]{2,1,0:T(4,128)S(1)} %shard_map.73), channel_id=1, replica_groups=mesh['zh'=4,'zl'=4,'x'=4,'c'=2,'y'=4] {'x','c'}, dimensions={0} | all-to-all | bytes 49152 | tf_op jit(solution)/shard_map/all_to_all | solution.py:540
  61.4 0.4 shard_map.74.after_ref.both_ref
  61.8 4.6 %collective-permute-done.7.far_ref = f32[256,128]{1,0:T(8,128)S(1)} collective-permute-done((f32[256,128]{1,0:T(8,128)S(1)}, f32[256,128]{1,0:T(8,128)S(1)}, u32[]{:S(2)}, u32[]{:S(2)}) %collective-permute-start.7) | collective-permute-done | bytes 131104 | tf_op jit(solution)/shard_map/ppermute | solution.py:621
  66.5 1.9 %collective-permute-start.8 = (f32[2,256,128]{2,1,0:T(8,128)S(1)}, f32[2,256,128]{2,1,0:T(8,128)S(1)}, u32[]{:S(2)}, u32[]{:S(2)}) collective-permute-start(f32[2,256,128]{2,1,0:T(8,128)S(1)} %shard_map.75.mine_ref), channel_id=1, source_target_pairs={{0,4},{4,0},{1,5},{5,1},{2,6},{6,2},{3,7},{7,3},{8,12},{12,8},{9,1... | collective-permute-start | bytes 786440 | tf_op jit(solution)/shard_map/ppermute | solution.py:637
  68.4 1.5 %collective-permute-done.8.other_ref = f32[2,256,128]{2,1,0:T(8,128)S(1)} collective-permute-done((f32[2,256,128]{2,1,0:T(8,128)S(1)}, f32[2,256,128]{2,1,0:T(8,128)S(1)}, u32[]{:S(2)}, u32[]{:S(2)}) %collective-permute-start.8) | collective-permute-done | bytes 262176 | tf_op jit(solution)/shard_map/ppermute | solution.py:637
  69.9 1.0 shard_map.76
  70.9 23.0 %all_to_all.21.got_ref = f32[16,3,256]{2,1,0:T(4,128)S(1)} all-to-all(f32[16,3,256]{2,1,0:T(4,128)S(1)} %get-tuple-element.50), channel_id=1, replica_groups=mesh['zh'=4,'zl'=4,'x'=4,'c'=2,'y'=4] {'zh','zl'}, dimensions={0} | all-to-all | bytes 98304 | tf_op jit(solution)/shard_map/all_to_all | solution.py:540
  93.8 1.0 shard_map.77
  94.9 1.3 collective-permute-start.9
  96.2 5.1 %collective-permute-start.10 = (f32[8,128]{1,0:T(8,128)S(1)}, f32[8,128]{1,0:T(8,128)S(1)}, u32[]{:S(2)}, u32[]{:S(2)}) collective-permute-start(f32[8,128]{1,0:T(8,128)S(1)} %get-tuple-element.56), channel_id=1, source_target_pairs={{1,0},{2,1},{3,2},{5,4},{6,5},{7,6},{9,8},{10,9},{11,10},{13,12},{... | collective-permute-start | bytes 12296 | tf_op jit(solution)/shard_map/ppermute | solution.py:654
  101.3 1.3 collective-permute-start.11
  102.6 0.0 collective-permute-done.9.left_ref
  102.6 0.0 collective-permute-done.10.right_ref
  102.6 1.7 %collective-permute-done.11.row_ref = f32[4,256]{1,0:T(4,128)S(1)} collective-permute-done((f32[4,256]{1,0:T(4,128)S(1)}, f32[4,256]{1,0:T(4,128)S(1)}, u32[]{:S(2)}, u32[]{:S(2)}) %collective-permute-start.11) | collective-permute-done | bytes 4128 | tf_op jit(solution)/shard_map/ppermute | solution.py:653
  104.4 1.5 %shard_map.78 = (f32[3,8,256]{2,1,0:T(8,128)S(1)}, f32[8,3,256]{2,1,0:T(4,128)S(1)}) custom-call(f32[4,8,256]{2,1,0:T(8,128)S(1)} %get-tuple-element.54.u_ref, f32[3,8,256]{2,1,0:T(8,128)S(1)} %copy-done.1, f32[8,128]{1,0:T(8,128)S(1)} %collective-permute-done.9.left_ref, f32[8,128]{1,0:T(8,128)S(1)} %collective-permute-done.10.right_ref, ...), custom_call_target="tpu_custom_call" | custom-call | flops 100000000 | bytes 3000000 | tf_op jit(solution)/shard_map/pallas_call | solution.py:70
  105.9 10.1 %all_to_all.22.got_ref = f32[8,3,256]{2,1,0:T(4,128)S(1)} all-to-all(f32[8,3,256]{2,1,0:T(4,128)S(1)} %get-tuple-element.61), channel_id=1, replica_groups=mesh['zh'=4,'zl'=4,'x'=4,'c'=2,'y'=4] {'x','c'}, dimensions={0} | all-to-all | bytes 49152 | tf_op jit(solution)/shard_map/all_to_all | solution.py:540
  116.0 0.6 shard_map.79
  116.5 16.9 %all_to_all.23.got_ref = f32[16,3,256]{2,1,0:T(4,128)S(1)} all-to-all(f32[16,3,256]{2,1,0:T(4,128)S(1)} %get-tuple-element.62), channel_id=1, replica_groups=mesh['zh'=4,'zl'=4,'x'=4,'c'=2,'y'=4] {'zh','zl'}, dimensions={0} | all-to-all | bytes 98304 | tf_op jit(solution)/shard_map/all_to_all | solution.py:540
  133.5 1.6 %shard_map.80 = f32[3,8,256]{2,1,0:T(8,128)} custom-call(f32[16,3,256]{2,1,0:T(4,128)S(1)} %all_to_all.23.got_ref, f32[8,512]{1,0:T(8,128)S(1)} %get-tuple-element.63.both_ref, bf16[8,256,256]{2,1,0:T(8,128)(2,1)S(1)} %get-tuple-element.51.maps_ref, bf16[2,256,256]{2,1,0:T(8,128)(2,1)S(1)} %get-tuple-element.52.joint_ref, ...), custom_call_target="tpu_custom_call" | custom-call | flops 100000000 | bytes 1000000 | tf_op jit(solution)/shard_map/pallas_call | solution.py:70
  (1 shorter events, 0.0 us)
Async XLA Ops:
  0.0 9.2 %copy-start.1 = (f32[3,8,256]{2,1,0:T(8,128)S(1)}, f32[3,8,256]{2,1,0:T(8,128)}, u32[]{:S(2)}) copy-start(f32[3,8,256]{2,1,0:T(8,128)} %stiff_ref.9) | copy-start | bytes 73732
  0.0 33.3 %copy-start.5 = (f32[8,256]{1,0:T(8,128)S(1)}, f32[8,256]{1,0:T(8,128)}, u32[]{:S(2)}) copy-start(f32[8,256]{1,0:T(8,128)} %inertia_ref.1) | copy-start | bytes 24580
  2.9 30.4 %copy-start = (bf16[4,512,512]{2,1,0:T(8,128)(2,1)S(1)}, bf16[4,512,512]{2,1,0:T(8,128)(2,1)}, u32[]{:S(2)}) copy-start(bf16[4,512,512]{2,1,0:T(8,128)(2,1)} %inv_ref.7) | copy-start | bytes 6291460
  5.8 11.4 %collective-permute-start.2 = (f32[256,256]{1,0:T(8,128)S(1)}, f32[256,256]{1,0:T(8,128)S(1)}, u32[]{:S(2)}, u32[]{:S(2)}) collective-permute-start(f32[256,256]{1,0:T(8,128)S(1)} %get-tuple-element.35.after_ref.own_ref), channel_id=1, source_target_pairs={{0,8},{8,0},{16,24},{24,16},{1,9},{9,1},{17,25},{25,17},{2,10},{10... | collective-permute-start | bytes 786440 | tf_op jit(solution)/shard_map/ppermute | solution.py:565
  9.2 0.7 copy-start.2
  10.0 5.8 %collective-permute-start = (f32[8,128]{1,0:T(8,128)S(1)}, f32[8,128]{1,0:T(8,128)S(1)}, u32[]{:S(2)}, u32[]{:S(2)}) collective-permute-start(f32[8,128]{1,0:T(8,128)S(1)} %get-tuple-element.36), channel_id=1, source_target_pairs={{0,1},{1,2},{2,3},{4,5},{5,6},{6,7},{8,9},{9,10},{10,11},{12,13},{... | collective-permute-start | bytes 12296 | tf_op jit(solution)/shard_map/ppermute | solution.py:576
  11.3 5.9 %collective-permute-start.1 = (f32[8,128]{1,0:T(8,128)S(1)}, f32[8,128]{1,0:T(8,128)S(1)}, u32[]{:S(2)}, u32[]{:S(2)}) collective-permute-start(f32[8,128]{1,0:T(8,128)S(1)} %get-tuple-element.37), channel_id=1, source_target_pairs={{1,0},{2,1},{3,2},{5,4},{6,5},{7,6},{9,8},{10,9},{11,10},{13,12},{... | collective-permute-start | bytes 12296 | tf_op jit(solution)/shard_map/ppermute | solution.py:575
  17.4 10.4 %collective-permute-start.4 = (f32[256,256]{1,0:T(8,128)S(1)}, f32[256,256]{1,0:T(8,128)S(1)}, u32[]{:S(2)}, u32[]{:S(2)}) collective-permute-start(f32[256,256]{1,0:T(8,128)S(1)} %get-tuple-element.41.own_ref.two_ref), channel_id=1, source_target_pairs={{0,16},{8,24},{16,0},{24,8},{1,17},{9,25},{17,1},{25,9},{2,18},{10... | collective-permute-start | bytes 786440 | tf_op jit(solution)/shard_map/ppermute | solution.py:583
  22.1 0.7 collective-permute-start.3
  28.1 10.5 %collective-permute-start.5 = (f32[256,256]{1,0:T(8,128)S(1)}, f32[256,256]{1,0:T(8,128)S(1)}, u32[]{:S(2)}, u32[]{:S(2)}) collective-permute-start(f32[256,256]{1,0:T(8,128)S(1)} %shard_map.68.after_ref.own_ref), channel_id=1, source_target_pairs={{0,32},{32,0},{64,96},{96,64},{128,160},{160,128},{192,224},{224,1... | collective-permute-start | bytes 786440 | tf_op jit(solution)/shard_map/ppermute | solution.py:590
  33.3 0.7 copy-start.3
  34.0 0.7 copy-start.4
  34.8 0.7 copy-start.6
  38.9 9.6 %collective-permute-start.6 = (f32[256,128]{1,0:T(8,128)S(1)}, f32[256,128]{1,0:T(8,128)S(1)}, u32[]{:S(2)}, u32[]{:S(2)}) collective-permute-start(f32[256,128]{1,0:T(8,128)S(1)} %get-tuple-element.47), channel_id=1, source_target_pairs={{0,64},{32,96},{64,0},{96,32},{128,192},{160,224},{192,128},{224,1... | collective-permute-start | bytes 393224 | tf_op jit(solution)/shard_map/ppermute | solution.py:618
  48.9 17.6 %collective-permute-start.7 = (f32[256,128]{1,0:T(8,128)S(1)}, f32[256,128]{1,0:T(8,128)S(1)}, u32[]{:S(2)}, u32[]{:S(2)}) collective-permute-start(f32[256,128]{1,0:T(8,128)S(1)} %shard_map.72.after_ref), channel_id=1, source_target_pairs={{128,0},{160,32},{192,64},{224,96},{256,384},{288,416},{320,448},{... | collective-permute-start | bytes 393224 | tf_op jit(solution)/shard_map/ppermute | solution.py:621
  66.5 3.4 %collective-permute-start.8 = (f32[2,256,128]{2,1,0:T(8,128)S(1)}, f32[2,256,128]{2,1,0:T(8,128)S(1)}, u32[]{:S(2)}, u32[]{:S(2)}) collective-permute-start(f32[2,256,128]{2,1,0:T(8,128)S(1)} %shard_map.75.mine_ref), channel_id=1, source_target_pairs={{0,4},{4,0},{1,5},{5,1},{2,6},{6,2},{3,7},{7,3},{8,12},{12,8},{9,1... | collective-permute-start | bytes 786440 | tf_op jit(solution)/shard_map/ppermute | solution.py:637
  94.9 7.8 %collective-permute-start.9 = (f32[8,128]{1,0:T(8,128)S(1)}, f32[8,128]{1,0:T(8,128)S(1)}, u32[]{:S(2)}, u32[]{:S(2)}) collective-permute-start(f32[8,128]{1,0:T(8,128)S(1)} %get-tuple-element.55), channel_id=1, source_target_pairs={{0,1},{1,2},{2,3},{4,5},{5,6},{6,7},{8,9},{9,10},{10,11},{12,13},{... | collective-permute-start | bytes 12296 | tf_op jit(solution)/shard_map/ppermute | solution.py:655
  96.2 6.5 %collective-permute-start.10 = (f32[8,128]{1,0:T(8,128)S(1)}, f32[8,128]{1,0:T(8,128)S(1)}, u32[]{:S(2)}, u32[]{:S(2)}) collective-permute-start(f32[8,128]{1,0:T(8,128)S(1)} %get-tuple-element.56), channel_id=1, source_target_pairs={{1,0},{2,1},{3,2},{5,4},{6,5},{7,6},{9,8},{10,9},{11,10},{13,12},{... | collective-permute-start | bytes 12296 | tf_op jit(solution)/shard_map/ppermute | solution.py:654
  101.3 3.1 %collective-permute-start.11 = (f32[4,256]{1,0:T(4,128)S(1)}, f32[4,256]{1,0:T(4,128)S(1)}, u32[]{:S(2)}, u32[]{:S(2)}) collective-permute-start(f32[4,256]{1,0:T(4,128)S(1)} %get-tuple-element.57), channel_id=1, source_target_pairs={{4,0},{8,4},{12,8},{16,12},{20,16},{24,20},{28,24},{32,28},{36,32}... | collective-permute-start | bytes 12296 | tf_op jit(solution)/shard_map/ppermute | solution.py:653

commit v4 on v3

--- a/solution.py
+++ b/solution.py
@@ -129,13 +129,14 @@
     return jnp.where(right, other, own), jnp.where(right, own, other)
 
 
-def two_chips_kernel(own_ref, other_ref, cross_ref, from_left_ref, from_right_ref, out_ref, row_ref):
+def two_chips_kernel(own_ref, other_ref, cross_ref, after_ref, out_ref, row_ref):
     left_map, right_map = in_order(own_ref[...], other_ref[...], low_bit("x") == 1)
     out_ref[...] = mm(pair(left_map), pair(right_map))
     row_ref[...] = cross_ref[...]
 
 
-def four_chips_kernel(own_ref, other_ref, after_ref, out_ref):
+def four_chips_kernel(own_ref, other_ref, edge_ref, after_ref, out_ref, tile_ref):
+    tile_ref[...] = edge_ref[...]
     left_map, right_map = in_order(own_ref[...], other_ref[...], high_bit("x") == 1)
     out_ref[...] = mm(pair(left_map), pair(right_map))
 
@@ -167,7 +168,7 @@
     half_ref[...] = jnp.where(high_bit() == 0, rows, columns)
 
 
-def four_planes_kernel(own_ref, half_ref, out_ref):
+def four_planes_kernel(own_ref, half_ref, after_ref, out_ref):
     own = pair(own_ref[...])
     half = half_ref[...]
     columns = mm(own, pair(half))
@@ -360,7 +361,7 @@
         msg_ref[2 * k + 1] = value
 
 
-def offsets_kernel(offset_ref, sends_ref, after_ref, msg_ref):
+def offsets_kernel(offset_ref, sends_ref, msg_ref):
     write_offsets(offset_ref[...], sends_ref, msg_ref)
 
 
@@ -573,56 +574,57 @@
     to_right = [(0, 1), (1, 2), (2, 3)]
     cores = [(0, 1), (1, 0)]
     from_right = lax.ppermute(left, "y", to_left)
-    from_left = lax.ppermute(right, "y", to_right)
     two_chips, cross = call(
         two_chips_kernel,
         [square, rows],
-        (chip, sib_chip, cross, from_left, from_right),
-        specs=[None] * 3 + [anywhere] * 2,
+        (chip, sib_chip, cross, from_right),
+        specs=[None] * 3 + [anywhere],
     )
     far_chips = lax.ppermute(two_chips, "x", [(k, k ^ 2) for k in range(4)])
     pairs = [(2 * k + 1, 2 * k + 2) for k in range(63)]
     cross = lax.ppermute(cross, STRIP, pairs + [(b, a) for a, b in pairs])
+    plane, right = call(
+        four_chips_kernel,
+        [square, tile],
+        (two_chips, far_chips, right, cross),
+        specs=[None] * 3 + [anywhere],
+    )
+    beside = lax.ppermute(plane, ZAX, [(k, k ^ 1) for k in range(16)])
+
+    from_left = lax.ppermute(right, "y", to_right)
+    half = sds((CB, 128))
+    two, two_half = call(
+        two_planes_kernel, [square, half], (plane, beside, from_left), specs=[None, None, anywhere]
+    )
+    two_mine = lax.ppermute(two_half, ZAX, [(k, k ^ 2) for k in range(16)])
+
     halos = (from_left, from_right, near, cross)
-    plane = call(
-        four_chips_kernel, square, (two_chips, far_chips, cross), specs=[None, None, anywhere]
-    )
-    beside = lax.ppermute(plane, ZAX, [(k, k ^ 1) for k in range(16)])
-
     field = sds((3, 8, CB))
     vector = sds((8, CB))
     base, offset, inertial, ext, above = call(
         first_side_kernel,
         [field, vector, field, sds((2, 8, 512)), vector],
-        (positions, target, inertia, stiffness, pin_columns) + halos + (inverses, plane),
+        (positions, target, inertia, stiffness, pin_columns) + halos + (inverses, two),
         specs=[None] * 4 + [smem] + [None] * 5 + [anywhere],
         flops=10**8,
         size=3 * 10**6,
     )
+    group_half = call(
+        four_planes_kernel, half, (two, two_mine, base), specs=[None, None, anywhere]
+    )
+    steps = [(4 + k, k) for k in range(4)] + [(8 + k, 12 + k) for k in range(4)]
+    far_mine = lax.ppermute(group_half, ZAX, steps)
+
     wide = sds((4 * CB, 2 * CB), BF16)
     narrow = sds((CB, CB), BF16)
     xh, xl, eh, el, sends = call(
         plane_maps_kernel,
         [wide, wide, narrow, narrow, sds((4, CB, CB), BF16)],
-        (chip, sib_chip, two_chips, far_chips, core_maps, plane),
+        (chip, sib_chip, two_chips, far_chips, core_maps, group_half),
         specs=[None] * 5 + [anywhere],
         flops=10**9,
     )
-    half = sds((CB, 128))
-    two, two_half = call(
-        two_planes_kernel,
-        [square, half],
-        (plane, beside, base, eh),
-        specs=[None, None, anywhere, anywhere],
-    )
-    two_mine = lax.ppermute(two_half, ZAX, [(k, k ^ 2) for k in range(16)])
-    group_half = call(four_planes_kernel, half, (two, two_mine))
-    steps = [(4 + k, k) for k in range(4)] + [(8 + k, 12 + k) for k in range(4)]
-    far_mine = lax.ppermute(group_half, ZAX, steps)
-
-    msg = call(
-        offsets_kernel, sds((8, 3, CB)), (offset, sends, group_half), specs=[None, None, anywhere]
-    )
+    msg = call(offsets_kernel, sds((8, 3, CB)), (offset, sends))
     got = swap(msg, PLANE)
     both = call(
         plane_kernel,

time: 137 us -> 136 us (level)
  waiting for transfers between devices: 18.7 us -> 23.9 us
  starting transfers between devices: 35.8 us -> 31.4 us
    ppermute x2, waiting for transfers between devices: 0.01 us -> 7.94 us  [shards(): from_left = lax.ppermute(right, 'y', to_right)]
    ppermute x2, starting transfers between devices: 9.68 us -> 5.29 us  [shards(): from_right = lax.ppermute(left, 'y', to_left)]
    ppermute x1, waiting for transfers between devices: 4.45 us -> 0.87 us  [shards(): two_mine = lax.ppermute(two_half, ZAX, [(k, k ^ 2) for k in range(16)])]
    ppermute x1, waiting for transfers between devices: 0.01 us -> 2.05 us  [shards(): sib_chip = lax.ppermute(chip, 'x', [(k, k ^ 1) for k in range(4)])]
  transfers between devices with their start and end apart: 12 -> 12, of which waited for: 6 -> 10; matrix products, arithmetic and copies ran while one was open for 0% -> 0% of each run, Pallas kernels for 3% -> 3%
where the time goes in v4:
time: 136 us; the launch traced here: 135 us
  blocking collectives  62.7 us (46%)
  starting transfers between devices  31.4 us (23%)
  waiting for transfers between devices  23.9 us (18%)
  Pallas kernels  13.8 us (10%)
  local copies, waits for them, and re-layouts  2.87 us (2%)
    all_to_all x4, blocking collectives, swap(): return lax.all_to_all(value, axes, 0, 0)  60.1 us
    pallas_call x17, Pallas kernels, call(): pl.pallas_call(kernel, out_shape=outs, in_specs=in_specs, out_specs=out_s...  13.8 us
    ppermute x2, waiting for transfers between devices, shards(): from_left = lax.ppermute(right, 'y', to_right)  7.94 us
    ppermute x1, waiting for transfers between devices, shards(): far_chips = lax.ppermute(two_chips, 'x', [(k, k ^ 2) for k in range(4)])  5.34 us
    ppermute x2, starting transfers between devices, shards(): from_right = lax.ppermute(left, 'y', to_left)  5.29 us
    ppermute x1, starting transfers between devices, shards(): two_mine = lax.ppermute(two_half, ZAX, [(k, k ^ 2) for k in range(16)])  5.18 us
    ppermute x1, starting transfers between devices, shards(): far_chips = lax.ppermute(two_chips, 'x', [(k, k ^ 2) for k in range(4)])  4.93 us
    ppermute x1, starting transfers between devices, shards(): beside = lax.ppermute(plane, ZAX, [(k, k ^ 1) for k in range(16)])  4.85 us
  transfers between devices with their start and end apart: 12, of which 10 were waited for; matrix products, arithmetic and copies ran while one was open for 0% of the time, Pallas kernels for 3%

profile of v4, /device:TPU:24, one launch (start us, length us, event | category | flops | bytes accessed | tf_op | source)
XLA Modules:
  0.0 134.8 jit_solution(376236728576275939)
XLA Ops:
  0.0 0.0 copy-start.1
  0.0 0.0 copy-start.5
  0.0 2.9 %shard_map.64 = f32[264,256]{1,0:T(8,128)} custom-call(bf16[4,512,512]{2,1,0:T(8,128)(2,1)} %inv_ref.7, f32[3,8,256]{2,1,0:T(8,128)} %stiff_ref.9, f32[3,8,256]{2,1,0:T(8,128)} %u_ref.3), custom_call_target="tpu_custom_call" | custom-call | flops 100000000 | bytes 1000000 | tf_op jit(solution)/shard_map/pallas_call | solution.py:70
  2.9 0.0 copy-start
  2.9 2.5 %all-gather = f32[528,256]{1,0:T(8,128)S(1)} all-gather(f32[264,256]{1,0:T(8,128)} %shard_map.64), channel_id=2, replica_groups=mesh['zh'=4,'zl'=4,'x'=4,'c'=2,'y'=4] {'c'}, dimensions={0}, use_global_device_ids=true | all-gather | bytes 811008 | tf_op jit(solution)/shard_map/all_gather | solution.py:563
  5.5 0.3 shard_map.65
  5.7 3.4 %collective-permute-start = (f32[256,256]{1,0:T(8,128)S(1)}, f32[256,256]{1,0:T(8,128)S(1)}, u32[]{:S(2)}, u32[]{:S(2)}) collective-permute-start(f32[256,256]{1,0:T(8,128)S(1)} %get-tuple-element.37.after_ref.own_ref), channel_id=1, source_target_pairs={{0,8},{8,0},{16,24},{24,16},{1,9},{9,1},{17,25},{25,17},{2,10},{10... | collective-permute-start | bytes 786440 | tf_op jit(solution)/shard_map/ppermute | solution.py:566
  9.1 0.0 copy-done.1
  9.2 0.0 copy-start.2
  9.2 0.7 copy-done.2
  9.9 0.1 shard_map.66
  10.0 2.6 %collective-permute-start.1 = (f32[8,128]{1,0:T(8,128)S(1)}, f32[8,128]{1,0:T(8,128)S(1)}, u32[]{:S(2)}, u32[]{:S(2)}) collective-permute-start(f32[8,128]{1,0:T(8,128)S(1)} %get-tuple-element.39), channel_id=1, source_target_pairs={{1,0},{2,1},{3,2},{5,4},{6,5},{7,6},{9,8},{10,9},{11,10},{13,12},{... | collective-permute-start | bytes 12296 | tf_op jit(solution)/shard_map/ppermute | solution.py:576
  12.6 1.3 collective-permute-done.1.after_ref.right_ref
  13.9 2.1 %collective-permute-done.other_ref.sib_ref = f32[256,256]{1,0:T(8,128)S(1)} collective-permute-done((f32[256,256]{1,0:T(8,128)S(1)}, f32[256,256]{1,0:T(8,128)S(1)}, u32[]{:S(2)}, u32[]{:S(2)}) %collective-permute-start) | collective-permute-done | bytes 262176 | tf_op jit(solution)/shard_map/ppermute | solution.py:566
  16.0 0.3 shard_map.67
  16.3 4.9 %collective-permute-start.2 = (f32[256,256]{1,0:T(8,128)S(1)}, f32[256,256]{1,0:T(8,128)S(1)}, u32[]{:S(2)}, u32[]{:S(2)}) collective-permute-start(f32[256,256]{1,0:T(8,128)S(1)} %get-tuple-element.40.own_ref.two_ref), channel_id=1, source_target_pairs={{0,16},{8,24},{16,0},{24,8},{1,17},{9,25},{17,1},{25,9},{2,18},{10... | collective-permute-start | bytes 786440 | tf_op jit(solution)/shard_map/ppermute | solution.py:583
  21.2 0.7 collective-permute-start.3
  21.9 0.0 collective-permute-done.3.after_ref.cross_ref
  21.9 5.3 %collective-permute-done.2.other_ref.far_ref = f32[256,256]{1,0:T(8,128)S(1)} collective-permute-done((f32[256,256]{1,0:T(8,128)S(1)}, f32[256,256]{1,0:T(8,128)S(1)}, u32[]{:S(2)}, u32[]{:S(2)}) %collective-permute-start.2) | collective-permute-done | bytes 262176 | tf_op jit(solution)/shard_map/ppermute | solution.py:583
  27.2 0.3 shard_map.68
  27.5 4.8 %collective-permute-start.5 = (f32[256,256]{1,0:T(8,128)S(1)}, f32[256,256]{1,0:T(8,128)S(1)}, u32[]{:S(2)}, u32[]{:S(2)}) collective-permute-start(f32[256,256]{1,0:T(8,128)S(1)} %get-tuple-element.45.own_ref), channel_id=1, source_target_pairs={{0,32},{32,0},{64,96},{96,64},{128,160},{160,128},{192,224},{224,1... | collective-permute-start | bytes 786440 | tf_op jit(solution)/shard_map/ppermute | solution.py:592
  32.4 1.3 collective-permute-start.4
  33.7 4.2 %collective-permute-done.4.rest_0_.left_ref = f32[8,128]{1,0:T(8,128)S(1)} collective-permute-done((f32[8,128]{1,0:T(8,128)S(1)}, f32[8,128]{1,0:T(8,128)S(1)}, u32[]{:S(2)}, u32[]{:S(2)}) %collective-permute-start.4) | collective-permute-done | bytes 4128 | tf_op jit(solution)/shard_map/ppermute | solution.py:594
  37.9 0.1 collective-permute-done.5.other_ref.one_ref
  38.0 0.3 shard_map.69
  38.3 5.2 %collective-permute-start.6 = (f32[256,128]{1,0:T(8,128)S(1)}, f32[256,128]{1,0:T(8,128)S(1)}, u32[]{:S(2)}, u32[]{:S(2)}) collective-permute-start(f32[256,128]{1,0:T(8,128)S(1)} %get-tuple-element.48), channel_id=1, source_target_pairs={{0,64},{32,96},{64,0},{96,32},{128,192},{160,224},{192,128},{224,1... | collective-permute-start | bytes 393224 | tf_op jit(solution)/shard_map/ppermute | solution.py:599
  43.5 0.0 copy-done.5
  43.5 0.0 copy-done
  43.5 0.0 copy-start.3
  43.6 0.7 copy-done.3
  44.3 0.0 copy-start.4
  44.3 0.7 copy-done.4
  45.0 0.0 copy-start.6
  45.0 0.7 copy-done.6
  45.7 1.9 %shard_map.70 = (f32[3,8,256]{2,1,0:T(8,128)S(1)}, f32[8,256]{1,0:T(8,128)S(1)}, f32[3,8,256]{2,1,0:T(8,128)S(1)}, f32[2,8,512]{2,1,0:T(8,128)S(1)}, f32[8,256]{1,0:T(8,128)S(1)}) custom-call(f32[3,8,256]{2,1,0:T(8,128)S(1)} %copy-done.3, f32[3,8,256]{2,1,0:T(8,128)S(1)} %copy-done.4, f32[8,256]{1,0:T(8,128)S(1)} %copy-done.5, f32[3,8,256]{2,1,0:T(8,128)S(1)} %copy-done.1, ...), custom_call_target="tpu_custom_call" | custom-call | flops 100000000 | bytes 3000000 | tf_op jit(solution)/shard_map/pallas_call | solution.py:70
  47.6 0.9 collective-permute-done.6.half_ref.two_ref
  48.4 0.3 shard_map.71.after_ref
  48.7 1.3 collective-permute-start.7
  50.0 1.3 shard_map.72
  51.3 0.2 shard_map.73
  51.5 10.7 %all_to_all.20.got_ref = f32[8,3,256]{2,1,0:T(4,128)S(1)} all-to-all(f32[8,3,256]{2,1,0:T(4,128)S(1)} %shard_map.73), channel_id=1, replica_groups=mesh['zh'=4,'zl'=4,'x'=4,'c'=2,'y'=4] {'x','c'}, dimensions={0} | all-to-all | bytes 49152 | tf_op jit(solution)/shard_map/all_to_all | solution.py:541
  62.2 0.4 shard_map.74.after_ref.both_ref
  62.6 4.2 %collective-permute-done.7.far_ref = f32[256,128]{1,0:T(8,128)S(1)} collective-permute-done((f32[256,128]{1,0:T(8,128)S(1)}, f32[256,128]{1,0:T(8,128)S(1)}, u32[]{:S(2)}, u32[]{:S(2)}) %collective-permute-start.7) | collective-permute-done | bytes 131104 | tf_op jit(solution)/shard_map/ppermute | solution.py:616
  66.8 1.9 %collective-permute-start.8 = (f32[2,256,128]{2,1,0:T(8,128)S(1)}, f32[2,256,128]{2,1,0:T(8,128)S(1)}, u32[]{:S(2)}, u32[]{:S(2)}) collective-permute-start(f32[2,256,128]{2,1,0:T(8,128)S(1)} %shard_map.75.mine_ref), channel_id=1, source_target_pairs={{0,4},{4,0},{1,5},{5,1},{2,6},{6,2},{3,7},{7,3},{8,12},{12,8},{9,1... | collective-permute-start | bytes 786440 | tf_op jit(solution)/shard_map/ppermute | solution.py:639
  68.8 1.5 %collective-permute-done.8.other_ref = f32[2,256,128]{2,1,0:T(8,128)S(1)} collective-permute-done((f32[2,256,128]{2,1,0:T(8,128)S(1)}, f32[2,256,128]{2,1,0:T(8,128)S(1)}, u32[]{:S(2)}, u32[]{:S(2)}) %collective-permute-start.8) | collective-permute-done | bytes 262176 | tf_op jit(solution)/shard_map/ppermute | solution.py:639
  70.3 1.0 shard_map.76
  71.3 23.6 %all_to_all.21.got_ref = f32[16,3,256]{2,1,0:T(4,128)S(1)} all-to-all(f32[16,3,256]{2,1,0:T(4,128)S(1)} %get-tuple-element.53), channel_id=1, replica_groups=mesh['zh'=4,'zl'=4,'x'=4,'c'=2,'y'=4] {'zh','zl'}, dimensions={0} | all-to-all | bytes 98304 | tf_op jit(solution)/shard_map/all_to_all | solution.py:541
  94.9 1.0 shard_map.77
  95.9 2.7 %collective-permute-start.10 = (f32[8,128]{1,0:T(8,128)S(1)}, f32[8,128]{1,0:T(8,128)S(1)}, u32[]{:S(2)}, u32[]{:S(2)}) collective-permute-start(f32[8,128]{1,0:T(8,128)S(1)} %get-tuple-element.60), channel_id=1, source_target_pairs={{1,0},{2,1},{3,2},{5,4},{6,5},{7,6},{9,8},{10,9},{11,10},{13,12},{... | collective-permute-start | bytes 12296 | tf_op jit(solution)/shard_map/ppermute | solution.py:656
  98.6 1.3 collective-permute-start.11
  99.9 1.3 collective-permute-start.9
  101.2 0.0 collective-permute-done.10.right_ref
  101.2 0.4 collective-permute-done.11.row_ref
  101.6 3.7 %collective-permute-done.9.left_ref = f32[8,128]{1,0:T(8,128)S(1)} collective-permute-done((f32[8,128]{1,0:T(8,128)S(1)}, f32[8,128]{1,0:T(8,128)S(1)}, u32[]{:S(2)}, u32[]{:S(2)}) %collective-permute-start.9) | collective-permute-done | bytes 4128 | tf_op jit(solution)/shard_map/ppermute | solution.py:657
  105.4 1.5 %shard_map.78 = (f32[3,8,256]{2,1,0:T(8,128)S(1)}, f32[8,3,256]{2,1,0:T(4,128)S(1)}) custom-call(f32[4,8,256]{2,1,0:T(8,128)S(1)} %get-tuple-element.58.u_ref, f32[3,8,256]{2,1,0:T(8,128)S(1)} %copy-done.1, f32[8,128]{1,0:T(8,128)S(1)} %collective-permute-done.9.left_ref, f32[8,128]{1,0:T(8,128)S(1)} %collective-permute-done.10.right_ref, ...), custom_call_target="tpu_custom_call" | custom-call | flops 100000000 | bytes 3000000 | tf_op jit(solution)/shard_map/pallas_call | solution.py:70
  106.9 8.3 %all_to_all.22.got_ref = f32[8,3,256]{2,1,0:T(4,128)S(1)} all-to-all(f32[8,3,256]{2,1,0:T(4,128)S(1)} %get-tuple-element.65), channel_id=1, replica_groups=mesh['zh'=4,'zl'=4,'x'=4,'c'=2,'y'=4] {'x','c'}, dimensions={0} | all-to-all | bytes 49152 | tf_op jit(solution)/shard_map/all_to_all | solution.py:541
  115.2 0.6 shard_map.79
  115.8 17.5 %all_to_all.23.got_ref = f32[16,3,256]{2,1,0:T(4,128)S(1)} all-to-all(f32[16,3,256]{2,1,0:T(4,128)S(1)} %get-tuple-element.66), channel_id=1, replica_groups=mesh['zh'=4,'zl'=4,'x'=4,'c'=2,'y'=4] {'zh','zl'}, dimensions={0} | all-to-all | bytes 98304 | tf_op jit(solution)/shard_map/all_to_all | solution.py:541
  133.3 1.6 %shard_map.80 = f32[3,8,256]{2,1,0:T(8,128)} custom-call(f32[16,3,256]{2,1,0:T(4,128)S(1)} %all_to_all.23.got_ref, f32[8,512]{1,0:T(8,128)S(1)} %get-tuple-element.67.both_ref, bf16[8,256,256]{2,1,0:T(8,128)(2,1)S(1)} %get-tuple-element.54.maps_ref, bf16[2,256,256]{2,1,0:T(8,128)(2,1)S(1)} %get-tuple-element.55.joint_ref, ...), custom_call_target="tpu_custom_call" | custom-call | flops 100000000 | bytes 1000000 | tf_op jit(solution)/shard_map/pallas_call | solution.py:70
  (1 shorter events, 0.0 us)
Async XLA Ops:
  0.0 9.1 %copy-start.1 = (f32[3,8,256]{2,1,0:T(8,128)S(1)}, f32[3,8,256]{2,1,0:T(8,128)}, u32[]{:S(2)}) copy-start(f32[3,8,256]{2,1,0:T(8,128)} %stiff_ref.9) | copy-start | bytes 73732
  0.0 43.5 %copy-start.5 = (f32[8,256]{1,0:T(8,128)S(1)}, f32[8,256]{1,0:T(8,128)}, u32[]{:S(2)}) copy-start(f32[8,256]{1,0:T(8,128)} %inertia_ref.1) | copy-start | bytes 24580
  2.9 40.6 %copy-start = (bf16[4,512,512]{2,1,0:T(8,128)(2,1)S(1)}, bf16[4,512,512]{2,1,0:T(8,128)(2,1)}, u32[]{:S(2)}) copy-start(bf16[4,512,512]{2,1,0:T(8,128)(2,1)} %inv_ref.7) | copy-start | bytes 6291460
  5.7 10.2 %collective-permute-start = (f32[256,256]{1,0:T(8,128)S(1)}, f32[256,256]{1,0:T(8,128)S(1)}, u32[]{:S(2)}, u32[]{:S(2)}) collective-permute-start(f32[256,256]{1,0:T(8,128)S(1)} %get-tuple-element.37.after_ref.own_ref), channel_id=1, source_target_pairs={{0,8},{8,0},{16,24},{24,16},{1,9},{9,1},{17,25},{25,17},{2,10},{10... | collective-permute-start | bytes 786440 | tf_op jit(solution)/shard_map/ppermute | solution.py:566
  9.2 0.7 copy-start.2
  10.0 4.0 %collective-permute-start.1 = (f32[8,128]{1,0:T(8,128)S(1)}, f32[8,128]{1,0:T(8,128)S(1)}, u32[]{:S(2)}, u32[]{:S(2)}) collective-permute-start(f32[8,128]{1,0:T(8,128)S(1)} %get-tuple-element.39), channel_id=1, source_target_pairs={{1,0},{2,1},{3,2},{5,4},{6,5},{7,6},{9,8},{10,9},{11,10},{13,12},{... | collective-permute-start | bytes 12296 | tf_op jit(solution)/shard_map/ppermute | solution.py:576
  16.3 11.0 %collective-permute-start.2 = (f32[256,256]{1,0:T(8,128)S(1)}, f32[256,256]{1,0:T(8,128)S(1)}, u32[]{:S(2)}, u32[]{:S(2)}) collective-permute-start(f32[256,256]{1,0:T(8,128)S(1)} %get-tuple-element.40.own_ref.two_ref), channel_id=1, source_target_pairs={{0,16},{8,24},{16,0},{24,8},{1,17},{9,25},{17,1},{25,9},{2,18},{10... | collective-permute-start | bytes 786440 | tf_op jit(solution)/shard_map/ppermute | solution.py:583
  21.2 0.7 collective-permute-start.3
  27.5 10.5 %collective-permute-start.5 = (f32[256,256]{1,0:T(8,128)S(1)}, f32[256,256]{1,0:T(8,128)S(1)}, u32[]{:S(2)}, u32[]{:S(2)}) collective-permute-start(f32[256,256]{1,0:T(8,128)S(1)} %get-tuple-element.45.own_ref), channel_id=1, source_target_pairs={{0,32},{32,0},{64,96},{96,64},{128,160},{160,128},{192,224},{224,1... | collective-permute-start | bytes 786440 | tf_op jit(solution)/shard_map/ppermute | solution.py:592
  32.4 5.5 %collective-permute-start.4 = (f32[8,128]{1,0:T(8,128)S(1)}, f32[8,128]{1,0:T(8,128)S(1)}, u32[]{:S(2)}, u32[]{:S(2)}) collective-permute-start(f32[8,128]{1,0:T(8,128)S(1)} %get-tuple-element.43), channel_id=1, source_target_pairs={{0,1},{1,2},{2,3},{4,5},{5,6},{6,7},{8,9},{9,10},{10,11},{12,13},{... | collective-permute-start | bytes 12296 | tf_op jit(solution)/shard_map/ppermute | solution.py:594
  38.3 10.1 %collective-permute-start.6 = (f32[256,128]{1,0:T(8,128)S(1)}, f32[256,128]{1,0:T(8,128)S(1)}, u32[]{:S(2)}, u32[]{:S(2)}) collective-permute-start(f32[256,128]{1,0:T(8,128)S(1)} %get-tuple-element.48), channel_id=1, source_target_pairs={{0,64},{32,96},{64,0},{96,32},{128,192},{160,224},{192,128},{224,1... | collective-permute-start | bytes 393224 | tf_op jit(solution)/shard_map/ppermute | solution.py:599
  43.5 0.7 copy-start.3
  44.3 0.7 copy-start.4
  45.0 0.7 copy-start.6
  48.7 18.1 %collective-permute-start.7 = (f32[256,128]{1,0:T(8,128)S(1)}, f32[256,128]{1,0:T(8,128)S(1)}, u32[]{:S(2)}, u32[]{:S(2)}) collective-permute-start(f32[256,128]{1,0:T(8,128)S(1)} %shard_map.71.after_ref), channel_id=1, source_target_pairs={{128,0},{160,32},{192,64},{224,96},{256,384},{288,416},{320,448},{... | collective-permute-start | bytes 393224 | tf_op jit(solution)/shard_map/ppermute | solution.py:616
  66.8 3.4 %collective-permute-start.8 = (f32[2,256,128]{2,1,0:T(8,128)S(1)}, f32[2,256,128]{2,1,0:T(8,128)S(1)}, u32[]{:S(2)}, u32[]{:S(2)}) collective-permute-start(f32[2,256,128]{2,1,0:T(8,128)S(1)} %shard_map.75.mine_ref), channel_id=1, source_target_pairs={{0,4},{4,0},{1,5},{5,1},{2,6},{6,2},{3,7},{7,3},{8,12},{12,8},{9,1... | collective-permute-start | bytes 786440 | tf_op jit(solution)/shard_map/ppermute | solution.py:639
  95.9 5.3 %collective-permute-start.10 = (f32[8,128]{1,0:T(8,128)S(1)}, f32[8,128]{1,0:T(8,128)S(1)}, u32[]{:S(2)}, u32[]{:S(2)}) collective-permute-start(f32[8,128]{1,0:T(8,128)S(1)} %get-tuple-element.60), channel_id=1, source_target_pairs={{1,0},{2,1},{3,2},{5,4},{6,5},{7,6},{9,8},{10,9},{11,10},{13,12},{... | collective-permute-start | bytes 12296 | tf_op jit(solution)/shard_map/ppermute | solution.py:656
  98.6 3.1 %collective-permute-start.11 = (f32[4,256]{1,0:T(4,128)S(1)}, f32[4,256]{1,0:T(4,128)S(1)}, u32[]{:S(2)}, u32[]{:S(2)}) collective-permute-start(f32[4,256]{1,0:T(4,128)S(1)} %get-tuple-element.61), channel_id=1, source_target_pairs={{4,0},{8,4},{12,8},{16,12},{20,16},{24,20},{28,24},{32,28},{36,32}... | collective-permute-start | bytes 12296 | tf_op jit(solution)/shard_map/ppermute | solution.py:655
  99.9 5.5 %collective-permute-start.9 = (f32[8,128]{1,0:T(8,128)S(1)}, f32[8,128]{1,0:T(8,128)S(1)}, u32[]{:S(2)}, u32[]{:S(2)}) collective-permute-start(f32[8,128]{1,0:T(8,128)S(1)} %get-tuple-element.59), channel_id=1, source_target_pairs={{0,1},{1,2},{2,3},{4,5},{5,6},{6,7},{8,9},{9,10},{10,11},{12,13},{... | collective-permute-start | bytes 12296 | tf_op jit(solution)/shard_map/ppermute | solution.py:657

commit v5 on v4

--- a/solution.py
+++ b/solution.py
@@ -14,7 +14,7 @@
 CB = 256
 PIN = 20.0
 VMEM_LIMIT = 14 * 1024 * 1024
-WHOLE_VMEM = 64 * 1024 * 1024 - 96 * 1024
+WHOLE_VMEM = 64 * 1024 * 1024 - (64 + 280) * 1024
 
 
 def dot(a, b):
@@ -580,7 +580,7 @@
         (chip, sib_chip, cross, from_right),
         specs=[None] * 3 + [anywhere],
     )
-    far_chips = lax.ppermute(two_chips, "x", [(k, k ^ 2) for k in range(4)])
+    far_chips = lax.ppermute(two_chips, "x", [(k, 3 - k) for k in range(4)])
     pairs = [(2 * k + 1, 2 * k + 2) for k in range(63)]
     cross = lax.ppermute(cross, STRIP, pairs + [(b, a) for a, b in pairs])
     plane, right = call(

time: 136 us -> 135 us (level)
  blocking collectives: 62.7 us -> 66 us
  local copies, waits for them, and re-layouts: 2.87 us -> 0.03 us
    all_to_all x4, blocking collectives: 60.1 us -> 63.5 us  [swap(): return lax.all_to_all(value, axes, 0, 0)]
    ppermute x1, waiting for transfers between devices: 4.25 us -> 0.97 us  [shards(): far_mine = lax.ppermute(group_half, ZAX, steps)]
    unnamed x14 -> x12, local copies, waits for them, and re-layouts: 2.87 us -> 0.03 us
    ppermute x1, waiting for transfers between devices: 0.87 us -> 2.4 us  [shards(): two_mine = lax.ppermute(two_half, ZAX, [(k, k ^ 2) for k in range(16)])]
  transfers between devices with their start and end apart: 12 -> 12, of which waited for: 10 -> 9; matrix products, arithmetic and copies ran while one was open for 0% -> 0% of each run, Pallas kernels for 3% -> 3%
where the time goes in v5:
time: 135 us; the launch traced here: 134 us
  blocking collectives  66 us (49%)
  starting transfers between devices  31.2 us (23%)
  waiting for transfers between devices  22.6 us (17%)
  Pallas kernels  13.8 us (10%)
    all_to_all x4, blocking collectives, swap(): return lax.all_to_all(value, axes, 0, 0)  63.5 us
    pallas_call x17, Pallas kernels, call(): pl.pallas_call(kernel, out_shape=outs, in_specs=in_specs, out_specs=out_s...  13.8 us
    ppermute x2, waiting for transfers between devices, shards(): from_left = lax.ppermute(right, 'y', to_right)  7.94 us
    ppermute x2, starting transfers between devices, shards(): from_right = lax.ppermute(left, 'y', to_left)  5.29 us
    ppermute x1, waiting for transfers between devices, shards(): far_chips = lax.ppermute(two_chips, 'x', [(k, 3 - k) for k in range(4)])  5.27 us
    ppermute x1, starting transfers between devices, shards(): two_mine = lax.ppermute(two_half, ZAX, [(k, k ^ 2) for k in range(16)])  5.18 us
    ppermute x1, starting transfers between devices, shards(): beside = lax.ppermute(plane, ZAX, [(k, k ^ 1) for k in range(16)])  4.92 us
    ppermute x1, starting transfers between devices, shards(): far_chips = lax.ppermute(two_chips, 'x', [(k, 3 - k) for k in range(4)])  4.67 us
  transfers between devices with their start and end apart: 12, of which 9 were waited for; matrix products, arithmetic and copies ran while one was open for 0% of the time, Pallas kernels for 3%

profile of v5, /device:TPU:24, one launch (start us, length us, event | category | flops | bytes accessed | tf_op | source)
XLA Modules:
  0.0 134.0 jit_solution(13906400445188036617)
XLA Ops:
  0.0 0.0 copy-start.2
  0.0 0.0 copy-start.1
  0.0 2.9 %shard_map.64 = f32[264,256]{1,0:T(8,128)} custom-call(bf16[4,512,512]{2,1,0:T(8,128)(2,1)} %inv_ref.7, f32[3,8,256]{2,1,0:T(8,128)} %stiff_ref.9, f32[3,8,256]{2,1,0:T(8,128)} %u_ref.3), custom_call_target="tpu_custom_call" | custom-call | flops 100000000 | bytes 1000000 | tf_op jit(solution)/shard_map/pallas_call | solution.py:70
  2.9 0.0 copy-start
  2.9 0.0 copy-start.3
  2.9 0.0 copy-start.4
  3.0 0.0 copy-start.5
  3.0 2.5 %all-gather = f32[528,256]{1,0:T(8,128)S(1)} all-gather(f32[264,256]{1,0:T(8,128)} %shard_map.64), channel_id=2, replica_groups=mesh['zh'=4,'zl'=4,'x'=4,'c'=2,'y'=4] {'c'}, dimensions={0}, use_global_device_ids=true | all-gather | bytes 811008 | tf_op jit(solution)/shard_map/all_gather | solution.py:563
  5.5 0.3 shard_map.65
  5.8 3.4 %collective-permute-start = (f32[256,256]{1,0:T(8,128)S(1)}, f32[256,256]{1,0:T(8,128)S(1)}, u32[]{:S(2)}, u32[]{:S(2)}) collective-permute-start(f32[256,256]{1,0:T(8,128)S(1)} %get-tuple-element.37.after_ref.own_ref), channel_id=1, source_target_pairs={{0,8},{8,0},{16,24},{24,16},{1,9},{9,1},{17,25},{25,17},{2,10},{10... | collective-permute-start | bytes 786440 | tf_op jit(solution)/shard_map/ppermute | solution.py:566
  9.2 0.0 copy-done.2
  9.2 0.0 copy-done.1
  9.2 0.1 shard_map.66
  9.3 2.6 %collective-permute-start.1 = (f32[8,128]{1,0:T(8,128)S(1)}, f32[8,128]{1,0:T(8,128)S(1)}, u32[]{:S(2)}, u32[]{:S(2)}) collective-permute-start(f32[8,128]{1,0:T(8,128)S(1)} %get-tuple-element.39), channel_id=1, source_target_pairs={{1,0},{2,1},{3,2},{5,4},{6,5},{7,6},{9,8},{10,9},{11,10},{13,12},{... | collective-permute-start | bytes 12296 | tf_op jit(solution)/shard_map/ppermute | solution.py:576
  11.9 1.3 collective-permute-done.1.after_ref.right_ref
  13.2 2.8 %collective-permute-done.other_ref.sib_ref = f32[256,256]{1,0:T(8,128)S(1)} collective-permute-done((f32[256,256]{1,0:T(8,128)S(1)}, f32[256,256]{1,0:T(8,128)S(1)}, u32[]{:S(2)}, u32[]{:S(2)}) %collective-permute-start) | collective-permute-done | bytes 262176 | tf_op jit(solution)/shard_map/ppermute | solution.py:566
  16.0 0.3 shard_map.67
  16.3 4.7 %collective-permute-start.2 = (f32[256,256]{1,0:T(8,128)S(1)}, f32[256,256]{1,0:T(8,128)S(1)}, u32[]{:S(2)}, u32[]{:S(2)}) collective-permute-start(f32[256,256]{1,0:T(8,128)S(1)} %get-tuple-element.40.own_ref.two_ref), channel_id=1, source_target_pairs={{0,24},{8,16},{16,8},{24,0},{1,25},{9,17},{17,9},{25,1},{2,26},{10... | collective-permute-start | bytes 786440 | tf_op jit(solution)/shard_map/ppermute | solution.py:583
  21.0 0.7 collective-permute-start.3
  21.7 0.0 collective-permute-done.3.after_ref.cross_ref
  21.7 5.3 %collective-permute-done.2.other_ref.far_ref = f32[256,256]{1,0:T(8,128)S(1)} collective-permute-done((f32[256,256]{1,0:T(8,128)S(1)}, f32[256,256]{1,0:T(8,128)S(1)}, u32[]{:S(2)}, u32[]{:S(2)}) %collective-permute-start.2) | collective-permute-done | bytes 262176 | tf_op jit(solution)/shard_map/ppermute | solution.py:583
  26.9 0.3 shard_map.68
  27.2 4.9 %collective-permute-start.5 = (f32[256,256]{1,0:T(8,128)S(1)}, f32[256,256]{1,0:T(8,128)S(1)}, u32[]{:S(2)}, u32[]{:S(2)}) collective-permute-start(f32[256,256]{1,0:T(8,128)S(1)} %get-tuple-element.45.own_ref), channel_id=1, source_target_pairs={{0,32},{32,0},{64,96},{96,64},{128,160},{160,128},{192,224},{224,1... | collective-permute-start | bytes 786440 | tf_op jit(solution)/shard_map/ppermute | solution.py:592
  32.2 1.3 collective-permute-start.4
  33.5 4.2 %collective-permute-done.4.rest_0_.left_ref = f32[8,128]{1,0:T(8,128)S(1)} collective-permute-done((f32[8,128]{1,0:T(8,128)S(1)}, f32[8,128]{1,0:T(8,128)S(1)}, u32[]{:S(2)}, u32[]{:S(2)}) %collective-permute-start.4) | collective-permute-done | bytes 4128 | tf_op jit(solution)/shard_map/ppermute | solution.py:594
  37.7 0.0 collective-permute-done.5.other_ref.one_ref
  37.7 0.3 shard_map.69
  38.0 5.2 %collective-permute-start.6 = (f32[256,128]{1,0:T(8,128)S(1)}, f32[256,128]{1,0:T(8,128)S(1)}, u32[]{:S(2)}, u32[]{:S(2)}) collective-permute-start(f32[256,128]{1,0:T(8,128)S(1)} %get-tuple-element.48), channel_id=1, source_target_pairs={{0,64},{32,96},{64,0},{96,32},{128,192},{160,224},{192,128},{224,1... | collective-permute-start | bytes 393224 | tf_op jit(solution)/shard_map/ppermute | solution.py:599
  43.2 0.0 copy-done
  43.2 0.0 copy-done.3
  43.2 0.0 copy-done.4
  43.2 0.0 copy-done.5
  43.2 1.9 %shard_map.70 = (f32[3,8,256]{2,1,0:T(8,128)S(1)}, f32[8,256]{1,0:T(8,128)S(1)}, f32[3,8,256]{2,1,0:T(8,128)S(1)}, f32[2,8,512]{2,1,0:T(8,128)S(1)}, f32[8,256]{1,0:T(8,128)S(1)}) custom-call(f32[3,8,256]{2,1,0:T(8,128)S(1)} %copy-done.2, f32[3,8,256]{2,1,0:T(8,128)S(1)} %copy-done.3, f32[8,256]{1,0:T(8,128)S(1)} %copy-done.4, f32[3,8,256]{2,1,0:T(8,128)S(1)} %copy-done.1, ...), custom_call_target="tpu_custom_call" | custom-call | flops 100000000 | bytes 3000000 | tf_op jit(solution)/shard_map/pallas_call | solution.py:70
  45.1 2.4 %collective-permute-done.6.half_ref.two_ref = f32[256,128]{1,0:T(8,128)S(1)} collective-permute-done((f32[256,128]{1,0:T(8,128)S(1)}, f32[256,128]{1,0:T(8,128)S(1)}, u32[]{:S(2)}, u32[]{:S(2)}) %collective-permute-start.6) | collective-permute-done | bytes 131104 | tf_op jit(solution)/shard_map/ppermute | solution.py:599
  47.5 0.3 shard_map.71.after_ref
  47.8 1.3 collective-permute-start.7
  49.1 1.3 shard_map.72
  50.4 0.2 shard_map.73
  50.6 11.4 %all_to_all.20.got_ref = f32[8,3,256]{2,1,0:T(4,128)S(1)} all-to-all(f32[8,3,256]{2,1,0:T(4,128)S(1)} %shard_map.73), channel_id=1, replica_groups=mesh['zh'=4,'zl'=4,'x'=4,'c'=2,'y'=4] {'x','c'}, dimensions={0} | all-to-all | bytes 49152 | tf_op jit(solution)/shard_map/all_to_all | solution.py:541
  62.0 0.4 shard_map.74.after_ref.both_ref
  62.4 1.0 collective-permute-done.7.far_ref
  63.4 1.9 %collective-permute-start.8 = (f32[2,256,128]{2,1,0:T(8,128)S(1)}, f32[2,256,128]{2,1,0:T(8,128)S(1)}, u32[]{:S(2)}, u32[]{:S(2)}) collective-permute-start(f32[2,256,128]{2,1,0:T(8,128)S(1)} %shard_map.75.mine_ref), channel_id=1, source_target_pairs={{0,4},{4,0},{1,5},{5,1},{2,6},{6,2},{3,7},{7,3},{8,12},{12,8},{9,1... | collective-permute-start | bytes 786440 | tf_op jit(solution)/shard_map/ppermute | solution.py:639
  65.3 1.5 %collective-permute-done.8.other_ref = f32[2,256,128]{2,1,0:T(8,128)S(1)} collective-permute-done((f32[2,256,128]{2,1,0:T(8,128)S(1)}, f32[2,256,128]{2,1,0:T(8,128)S(1)}, u32[]{:S(2)}, u32[]{:S(2)}) %collective-permute-start.8) | collective-permute-done | bytes 262176 | tf_op jit(solution)/shard_map/ppermute | solution.py:639
  66.8 1.0 shard_map.76
  67.8 26.3 %all_to_all.21.got_ref = f32[16,3,256]{2,1,0:T(4,128)S(1)} all-to-all(f32[16,3,256]{2,1,0:T(4,128)S(1)} %get-tuple-element.53), channel_id=1, replica_groups=mesh['zh'=4,'zl'=4,'x'=4,'c'=2,'y'=4] {'zh','zl'}, dimensions={0} | all-to-all | bytes 98304 | tf_op jit(solution)/shard_map/all_to_all | solution.py:541
  94.1 1.0 shard_map.77
  95.1 2.7 %collective-permute-start.10 = (f32[8,128]{1,0:T(8,128)S(1)}, f32[8,128]{1,0:T(8,128)S(1)}, u32[]{:S(2)}, u32[]{:S(2)}) collective-permute-start(f32[8,128]{1,0:T(8,128)S(1)} %get-tuple-element.60), channel_id=1, source_target_pairs={{1,0},{2,1},{3,2},{5,4},{6,5},{7,6},{9,8},{10,9},{11,10},{13,12},{... | collective-permute-start | bytes 12296 | tf_op jit(solution)/shard_map/ppermute | solution.py:656
  97.7 1.3 collective-permute-start.11
  99.0 1.3 collective-permute-start.9
  100.3 0.0 collective-permute-done.10.right_ref
  100.3 0.4 collective-permute-done.11.row_ref
  100.8 3.7 %collective-permute-done.9.left_ref = f32[8,128]{1,0:T(8,128)S(1)} collective-permute-done((f32[8,128]{1,0:T(8,128)S(1)}, f32[8,128]{1,0:T(8,128)S(1)}, u32[]{:S(2)}, u32[]{:S(2)}) %collective-permute-start.9) | collective-permute-done | bytes 4128 | tf_op jit(solution)/shard_map/ppermute | solution.py:657
  104.5 1.5 %shard_map.78 = (f32[3,8,256]{2,1,0:T(8,128)S(1)}, f32[8,3,256]{2,1,0:T(4,128)S(1)}) custom-call(f32[4,8,256]{2,1,0:T(8,128)S(1)} %get-tuple-element.58.u_ref, f32[3,8,256]{2,1,0:T(8,128)S(1)} %copy-done.1, f32[8,128]{1,0:T(8,128)S(1)} %collective-permute-done.9.left_ref, f32[8,128]{1,0:T(8,128)S(1)} %collective-permute-done.10.right_ref, ...), custom_call_target="tpu_custom_call" | custom-call | flops 100000000 | bytes 3000000 | tf_op jit(solution)/shard_map/pallas_call | solution.py:70
  106.0 8.3 %all_to_all.22.got_ref = f32[8,3,256]{2,1,0:T(4,128)S(1)} all-to-all(f32[8,3,256]{2,1,0:T(4,128)S(1)} %get-tuple-element.65), channel_id=1, replica_groups=mesh['zh'=4,'zl'=4,'x'=4,'c'=2,'y'=4] {'x','c'}, dimensions={0} | all-to-all | bytes 49152 | tf_op jit(solution)/shard_map/all_to_all | solution.py:541
  114.4 0.6 shard_map.79
  114.9 17.5 %all_to_all.23.got_ref = f32[16,3,256]{2,1,0:T(4,128)S(1)} all-to-all(f32[16,3,256]{2,1,0:T(4,128)S(1)} %get-tuple-element.66), channel_id=1, replica_groups=mesh['zh'=4,'zl'=4,'x'=4,'c'=2,'y'=4] {'zh','zl'}, dimensions={0} | all-to-all | bytes 98304 | tf_op jit(solution)/shard_map/all_to_all | solution.py:541
  132.4 1.6 %shard_map.80 = f32[3,8,256]{2,1,0:T(8,128)} custom-call(f32[16,3,256]{2,1,0:T(4,128)S(1)} %all_to_all.23.got_ref, f32[8,512]{1,0:T(8,128)S(1)} %get-tuple-element.67.both_ref, bf16[8,256,256]{2,1,0:T(8,128)(2,1)S(1)} %get-tuple-element.54.maps_ref, bf16[2,256,256]{2,1,0:T(8,128)(2,1)S(1)} %get-tuple-element.55.joint_ref, ...), custom_call_target="tpu_custom_call" | custom-call | flops 100000000 | bytes 1000000 | tf_op jit(solution)/shard_map/pallas_call | solution.py:70
  (1 shorter events, 0.0 us)
Async XLA Ops:
  0.0 9.2 %copy-start.2 = (f32[3,8,256]{2,1,0:T(8,128)S(1)}, f32[3,8,256]{2,1,0:T(8,128)}, u32[]{:S(2)}) copy-start(f32[3,8,256]{2,1,0:T(8,128)} %u_ref.3) | copy-start | bytes 73732
  0.0 9.2 %copy-start.1 = (f32[3,8,256]{2,1,0:T(8,128)S(1)}, f32[3,8,256]{2,1,0:T(8,128)}, u32[]{:S(2)}) copy-start(f32[3,8,256]{2,1,0:T(8,128)} %stiff_ref.9) | copy-start | bytes 73732
  2.9 40.2 %copy-start = (bf16[4,512,512]{2,1,0:T(8,128)(2,1)S(1)}, bf16[4,512,512]{2,1,0:T(8,128)(2,1)}, u32[]{:S(2)}) copy-start(bf16[4,512,512]{2,1,0:T(8,128)(2,1)} %inv_ref.7) | copy-start | bytes 6291460
  2.9 40.2 %copy-start.3 = (f32[3,8,256]{2,1,0:T(8,128)S(1)}, f32[3,8,256]{2,1,0:T(8,128)}, u32[]{:S(2)}) copy-start(f32[3,8,256]{2,1,0:T(8,128)} %target_ref.1) | copy-start | bytes 73732
  2.9 40.2 %copy-start.4 = (f32[8,256]{1,0:T(8,128)S(1)}, f32[8,256]{1,0:T(8,128)}, u32[]{:S(2)}) copy-start(f32[8,256]{1,0:T(8,128)} %inertia_ref.1) | copy-start | bytes 24580
  3.0 40.2 %copy-start.5 = (s32[64]{0:T(128)S(1)}, s32[64]{0:T(128)}, u32[]{:S(2)}) copy-start(s32[64]{0:T(128)} %pin_ref.1) | copy-start | bytes 772
  5.8 10.2 %collective-permute-start = (f32[256,256]{1,0:T(8,128)S(1)}, f32[256,256]{1,0:T(8,128)S(1)}, u32[]{:S(2)}, u32[]{:S(2)}) collective-permute-start(f32[256,256]{1,0:T(8,128)S(1)} %get-tuple-element.37.after_ref.own_ref), channel_id=1, source_target_pairs={{0,8},{8,0},{16,24},{24,16},{1,9},{9,1},{17,25},{25,17},{2,10},{10... | collective-permute-start | bytes 786440 | tf_op jit(solution)/shard_map/ppermute | solution.py:566
  9.3 4.0 %collective-permute-start.1 = (f32[8,128]{1,0:T(8,128)S(1)}, f32[8,128]{1,0:T(8,128)S(1)}, u32[]{:S(2)}, u32[]{:S(2)}) collective-permute-start(f32[8,128]{1,0:T(8,128)S(1)} %get-tuple-element.39), channel_id=1, source_target_pairs={{1,0},{2,1},{3,2},{5,4},{6,5},{7,6},{9,8},{10,9},{11,10},{13,12},{... | collective-permute-start | bytes 12296 | tf_op jit(solution)/shard_map/ppermute | solution.py:576
  16.3 10.6 %collective-permute-start.2 = (f32[256,256]{1,0:T(8,128)S(1)}, f32[256,256]{1,0:T(8,128)S(1)}, u32[]{:S(2)}, u32[]{:S(2)}) collective-permute-start(f32[256,256]{1,0:T(8,128)S(1)} %get-tuple-element.40.own_ref.two_ref), channel_id=1, source_target_pairs={{0,24},{8,16},{16,8},{24,0},{1,25},{9,17},{17,9},{25,1},{2,26},{10... | collective-permute-start | bytes 786440 | tf_op jit(solution)/shard_map/ppermute | solution.py:583
  21.0 0.7 collective-permute-start.3
  27.2 10.4 %collective-permute-start.5 = (f32[256,256]{1,0:T(8,128)S(1)}, f32[256,256]{1,0:T(8,128)S(1)}, u32[]{:S(2)}, u32[]{:S(2)}) collective-permute-start(f32[256,256]{1,0:T(8,128)S(1)} %get-tuple-element.45.own_ref), channel_id=1, source_target_pairs={{0,32},{32,0},{64,96},{96,64},{128,160},{160,128},{192,224},{224,1... | collective-permute-start | bytes 786440 | tf_op jit(solution)/shard_map/ppermute | solution.py:592
  32.2 5.5 %collective-permute-start.4 = (f32[8,128]{1,0:T(8,128)S(1)}, f32[8,128]{1,0:T(8,128)S(1)}, u32[]{:S(2)}, u32[]{:S(2)}) collective-permute-start(f32[8,128]{1,0:T(8,128)S(1)} %get-tuple-element.43), channel_id=1, source_target_pairs={{0,1},{1,2},{2,3},{4,5},{5,6},{6,7},{8,9},{9,10},{10,11},{12,13},{... | collective-permute-start | bytes 12296 | tf_op jit(solution)/shard_map/ppermute | solution.py:594
  38.0 9.5 %collective-permute-start.6 = (f32[256,128]{1,0:T(8,128)S(1)}, f32[256,128]{1,0:T(8,128)S(1)}, u32[]{:S(2)}, u32[]{:S(2)}) collective-permute-start(f32[256,128]{1,0:T(8,128)S(1)} %get-tuple-element.48), channel_id=1, source_target_pairs={{0,64},{32,96},{64,0},{96,32},{128,192},{160,224},{192,128},{224,1... | collective-permute-start | bytes 393224 | tf_op jit(solution)/shard_map/ppermute | solution.py:599
  47.8 15.5 %collective-permute-start.7 = (f32[256,128]{1,0:T(8,128)S(1)}, f32[256,128]{1,0:T(8,128)S(1)}, u32[]{:S(2)}, u32[]{:S(2)}) collective-permute-start(f32[256,128]{1,0:T(8,128)S(1)} %shard_map.71.after_ref), channel_id=1, source_target_pairs={{128,0},{160,32},{192,64},{224,96},{256,384},{288,416},{320,448},{... | collective-permute-start | bytes 393224 | tf_op jit(solution)/shard_map/ppermute | solution.py:616
  63.4 3.4 %collective-permute-start.8 = (f32[2,256,128]{2,1,0:T(8,128)S(1)}, f32[2,256,128]{2,1,0:T(8,128)S(1)}, u32[]{:S(2)}, u32[]{:S(2)}) collective-permute-start(f32[2,256,128]{2,1,0:T(8,128)S(1)} %shard_map.75.mine_ref), channel_id=1, source_target_pairs={{0,4},{4,0},{1,5},{5,1},{2,6},{6,2},{3,7},{7,3},{8,12},{12,8},{9,1... | collective-permute-start | bytes 786440 | tf_op jit(solution)/shard_map/ppermute | solution.py:639
  95.1 5.3 %collective-permute-start.10 = (f32[8,128]{1,0:T(8,128)S(1)}, f32[8,128]{1,0:T(8,128)S(1)}, u32[]{:S(2)}, u32[]{:S(2)}) collective-permute-start(f32[8,128]{1,0:T(8,128)S(1)} %get-tuple-element.60), channel_id=1, source_target_pairs={{1,0},{2,1},{3,2},{5,4},{6,5},{7,6},{9,8},{10,9},{11,10},{13,12},{... | collective-permute-start | bytes 12296 | tf_op jit(solution)/shard_map/ppermute | solution.py:656
  97.7 3.1 %collective-permute-start.11 = (f32[4,256]{1,0:T(4,128)S(1)}, f32[4,256]{1,0:T(4,128)S(1)}, u32[]{:S(2)}, u32[]{:S(2)}) collective-permute-start(f32[4,256]{1,0:T(4,128)S(1)} %get-tuple-element.61), channel_id=1, source_target_pairs={{4,0},{8,4},{12,8},{16,12},{20,16},{24,20},{28,24},{32,28},{36,32}... | collective-permute-start | bytes 12296 | tf_op jit(solution)/shard_map/ppermute | solution.py:655
  99.0 5.5 %collective-permute-start.9 = (f32[8,128]{1,0:T(8,128)S(1)}, f32[8,128]{1,0:T(8,128)S(1)}, u32[]{:S(2)}, u32[]{:S(2)}) collective-permute-start(f32[8,128]{1,0:T(8,128)S(1)} %get-tuple-element.59), channel_id=1, source_target_pairs={{0,1},{1,2},{2,3},{4,5},{5,6},{6,7},{8,9},{9,10},{10,11},{12,13},{... | collective-permute-start | bytes 12296 | tf_op jit(solution)/shard_map/ppermute | solution.py:657

commit v6 on v5

--- a/solution.py
+++ b/solution.py
@@ -112,7 +112,10 @@
 
 def chip_map_kernel(both_ref, out_ref, near_ref):
     core = lax.axis_index("c")
-    out_ref[...] = mm(pair(both_ref[0, 0:CB, :]), pair(both_ref[1, 0:CB, :]))
+    start = pl.multiple_of(core * 128, 128)
+    half = mm(pair(both_ref[0, pl.ds(start, 128), :]), pair(both_ref[1, 0:CB, :]))
+    for k in range(4):
+        out_ref[k] = half
     tails = [both_ref[k, CB : CB + 8, :] for k in range(2)]
     near_ref[...] = jnp.where(core == 0, tails[1], tails[0])
 
@@ -129,16 +132,23 @@
     return jnp.where(right, other, own), jnp.where(right, own, other)
 
 
-def two_chips_kernel(own_ref, other_ref, cross_ref, after_ref, out_ref, row_ref):
-    left_map, right_map = in_order(own_ref[...], other_ref[...], low_bit("x") == 1)
-    out_ref[...] = mm(pair(left_map), pair(right_map))
-    row_ref[...] = cross_ref[...]
-
-
-def four_chips_kernel(own_ref, other_ref, edge_ref, after_ref, out_ref, tile_ref):
+def chips_kernel(
+    mine_ref, other_ref, edge_ref, own_ref, sib_ref, two_ref, far_ref, plane_ref, tile_ref
+):
+    core, x = lax.axis_index("c"), lax.axis_index("x")
     tile_ref[...] = edge_ref[...]
-    left_map, right_map = in_order(own_ref[...], other_ref[...], high_bit("x") == 1)
-    out_ref[...] = mm(pair(left_map), pair(right_map))
+    chips = []
+    for k in range(4):
+        top, bottom = in_order(mine_ref[k], other_ref[k], core == 1)
+        chips.append(jnp.concatenate([top, bottom], axis=0))
+    left = mm(pair(chips[0]), pair(chips[1]))
+    right = mm(pair(chips[2]), pair(chips[3]))
+    plane_ref[...] = mm(pair(left), pair(right))
+    even, odd = in_order(chips[0], chips[2], high_bit("x") == 1)[0], in_order(
+        chips[1], chips[3], high_bit("x") == 1
+    )[0]
+    own_ref[...], sib_ref[...] = in_order(even, odd, low_bit("x") == 1)
+    two_ref[...], far_ref[...] = in_order(left, right, high_bit("x") == 1)
 
 
 def rows_of_half(half):
@@ -157,8 +167,8 @@
     return jnp.where(high_bit() == 0, columns, rows)
 
 
-def two_planes_kernel(own_ref, other_ref, *rest):
-    out_ref, half_ref = rest[-2:]
+def two_planes_kernel(own_ref, other_ref, cross_ref, after_ref, out_ref, half_ref, row_ref):
+    row_ref[...] = cross_ref[...]
     core = lax.axis_index("c")
     left_map, right_map = in_order(own_ref[...], other_ref[...], low_bit() == 1)
     product = mm(pair(left_map), pair(right_map))
@@ -562,41 +572,46 @@
     )
     core_maps = lax.all_gather(own_map, "c")
     square = sds((CB, CB))
-    chip, near = call(chip_map_kernel, [square, sds((8, CB))], (core_maps,))
-    sib_chip = lax.ppermute(chip, "x", [(k, k ^ 1) for k in range(4)])
+    square = sds((CB, CB))
+    chip_halves, near = call(
+        chip_map_kernel, [sds((4, 128, CB)), sds((8, CB))], (core_maps,)
+    )
+    mine = swap(chip_halves, "x")
 
     tile = sds((8, 128))
     rows = sds((4, CB))
     left, right, cross = call(
-        halo_kernel, [tile, tile, rows], (positions, stiffness, chip), specs=[None, None, anywhere]
+        halo_kernel,
+        [tile, tile, rows],
+        (positions, stiffness, near),
+        specs=[None, None, anywhere],
     )
     to_left = [(1, 0), (2, 1), (3, 2)]
     to_right = [(0, 1), (1, 2), (2, 3)]
     cores = [(0, 1), (1, 0)]
     from_right = lax.ppermute(left, "y", to_left)
-    two_chips, cross = call(
-        two_chips_kernel,
-        [square, rows],
-        (chip, sib_chip, cross, from_right),
+    mine, from_right = lax.optimization_barrier((mine, from_right))
+    other = lax.ppermute(mine, "c", cores)
+    chip, sib_chip, two_chips, far_chips, plane, right = call(
+        chips_kernel, [square] * 5 + [tile], (mine, other, right)
+    )
+    beside = lax.ppermute(plane, ZAX, [(k, k ^ 1) for k in range(16)])
+    from_left = lax.ppermute(right, "y", to_right)
+    half = sds((CB, 128))
+    two, two_half, cross = call(
+        two_planes_kernel,
+        [square, half, rows],
+        (plane, beside, cross, from_left),
         specs=[None] * 3 + [anywhere],
     )
-    far_chips = lax.ppermute(two_chips, "x", [(k, 3 - k) for k in range(4)])
+    two_mine = lax.ppermute(two_half, ZAX, [(k, k ^ 2) for k in range(16)])
     pairs = [(2 * k + 1, 2 * k + 2) for k in range(63)]
     cross = lax.ppermute(cross, STRIP, pairs + [(b, a) for a, b in pairs])
-    plane, right = call(
-        four_chips_kernel,
-        [square, tile],
-        (two_chips, far_chips, right, cross),
-        specs=[None] * 3 + [anywhere],
-    )
-    beside = lax.ppermute(plane, ZAX, [(k, k ^ 1) for k in range(16)])
-
-    from_left = lax.ppermute(right, "y", to_right)
-    half = sds((CB, 128))
-    two, two_half = call(
-        two_planes_kernel, [square, half], (plane, beside, from_left), specs=[None, None, anywhere]
-    )
-    two_mine = lax.ppermute(two_half, ZAX, [(k, k ^ 2) for k in range(16)])
+    group_half = call(
+        four_planes_kernel, half, (two, two_mine, cross), specs=[None, None, anywhere]
+    )
+    steps = [(4 + k, k) for k in range(4)] + [(8 + k, 12 + k) for k in range(4)]
+    far_mine = lax.ppermute(group_half, ZAX, steps)
 
     halos = (from_left, from_right, near, cross)
     field = sds((3, 8, CB))
@@ -604,17 +619,11 @@
     base, offset, inertial, ext, above = call(
         first_side_kernel,
         [field, vector, field, sds((2, 8, 512)), vector],
-        (positions, target, inertia, stiffness, pin_columns) + halos + (inverses, two),
+        (positions, target, inertia, stiffness, pin_columns) + halos + (inverses, group_half),
         specs=[None] * 4 + [smem] + [None] * 5 + [anywhere],
         flops=10**8,
         size=3 * 10**6,
     )
-    group_half = call(
-        four_planes_kernel, half, (two, two_mine, base), specs=[None, None, anywhere]
-    )
-    steps = [(4 + k, k) for k in range(4)] + [(8 + k, 12 + k) for k in range(4)]
-    far_mine = lax.ppermute(group_half, ZAX, steps)
-
     wide = sds((4 * CB, 2 * CB), BF16)
     narrow = sds((CB, CB), BF16)
     xh, xl, eh, el, sends = call(

time: 135 us -> 138 us (1.022); the launches traced: 134 us -> 135 us
  waiting for transfers between devices: 22.6 us -> 28.2 us
  blocking collectives: 66 us -> 61.8 us
    ppermute x2 -> x0, starting transfers between devices: 8.07 us -> none  [the longest x1 4.67 us: shards(): far_chips = lax.ppermute(two_chips, 'x', [(k, 3 - k) for k in range(4)])]
    ppermute x2 -> x0, waiting for transfers between devices: 8.05 us -> none  [the longest x1 5.27 us: shards(): far_chips = lax.ppermute(two_chips, 'x', [(k, 3 - k) for k in range(4)])]
    all_to_all x0 -> x1, waiting for transfers between devices: none -> 5.74 us  [swap(): return lax.all_to_all(value, axes, 0, 0)]
    ppermute x1, waiting for transfers between devices: 0.97 us -> 5.89 us  [shards(): far_mine = lax.ppermute(group_half, ZAX, steps)]
    all_to_all x0 -> x1, starting transfers between devices: none -> 4.29 us  [swap(): return lax.all_to_all(value, axes, 0, 0)]
    all_to_all x4, blocking collectives: 63.5 us -> 59.3 us  [swap(): return lax.all_to_all(value, axes, 0, 0)]
    ppermute x2, waiting for transfers between devices: 7.94 us -> 4.2 us  [shards(): from_left = lax.ppermute(right, 'y', to_right)]
    ppermute x1, waiting for transfers between devices: 2.4 us -> 5.34 us  [shards(): two_mine = lax.ppermute(two_half, ZAX, [(k, k ^ 2) for k in range(16)])]
where the time goes in v6:
time: 138 us; the launch traced here: 135 us
  blocking collectives  61.8 us (45%)
  starting transfers between devices  30.1 us (22%)
  waiting for transfers between devices  28.2 us (20%)
  Pallas kernels  14.1 us (10%)
    all_to_all x4, blocking collectives, swap(): return lax.all_to_all(value, axes, 0, 0)  59.3 us
    pallas_call x16, Pallas kernels, call(): pl.pallas_call(kernel, out_shape=outs, in_specs=in_specs, out_specs=out_s...  14.1 us
    ppermute x2, starting transfers between devices, shards(): from_right = lax.ppermute(left, 'y', to_left)  7.18 us
    ppermute x1, waiting for transfers between devices, shards(): far_mine = lax.ppermute(group_half, ZAX, steps)  5.89 us
    all_to_all x1, waiting for transfers between devices, swap(): return lax.all_to_all(value, axes, 0, 0)  5.74 us
    ppermute x1, waiting for transfers between devices, shards(): two_mine = lax.ppermute(two_half, ZAX, [(k, k ^ 2) for k in range(16)])  5.34 us
    ppermute x1, starting transfers between devices, shards(): two_mine = lax.ppermute(two_half, ZAX, [(k, k ^ 2) for k in range(16)])  5.18 us
    all_to_all x1, starting transfers between devices, swap(): return lax.all_to_all(value, axes, 0, 0)  4.29 us
  transfers between devices with their start and end apart: 12, of which 9 were waited for; matrix products, arithmetic and copies ran while one was open for 0% of the time, Pallas kernels for 3%

profile of v6, /device:TPU:24, one launch (start us, length us, event | category | flops | bytes accessed | tf_op | source)
XLA Modules:
  0.0 135.4 jit_solution(5152195862800319059)
XLA Ops:
  0.0 0.0 copy-start.3
  0.0 0.0 copy-start.1
  0.0 2.9 %shard_map.64 = f32[264,256]{1,0:T(8,128)} custom-call(bf16[4,512,512]{2,1,0:T(8,128)(2,1)} %inv_ref.7, f32[3,8,256]{2,1,0:T(8,128)} %stiff_ref.9, f32[3,8,256]{2,1,0:T(8,128)} %u_ref.3), custom_call_target="tpu_custom_call" | custom-call | flops 100000000 | bytes 1000000 | tf_op jit(solution)/shard_map/pallas_call | solution.py:70
  2.9 0.0 copy-start
  2.9 0.0 copy-start.4
  2.9 0.0 copy-start.5
  2.9 0.0 copy-start.6
  3.0 2.5 %all-gather = f32[528,256]{1,0:T(8,128)S(1)} all-gather(f32[264,256]{1,0:T(8,128)} %shard_map.64), channel_id=2, replica_groups=mesh['zh'=4,'zl'=4,'x'=4,'c'=2,'y'=4] {'c'}, dimensions={0}, use_global_device_ids=true | all-gather | bytes 811008 | tf_op jit(solution)/shard_map/all_gather | solution.py:573
  5.5 0.2 shard_map.65
  5.7 0.0 copy-start.2
  5.7 0.8 copy-done.2
  6.5 4.3 %all-to-all-start = ((f32[4,128,256]{2,1,0:T(8,128)}), f32[4,128,256]{2,1,0:T(8,128)S(1)}, u32[]{:S(2)}, u32[]{:S(2)}) async-start(f32[4,128,256]{2,1,0:T(8,128)} %copy-done.2), calls=%async_computation | async-start | bytes 1048576 | tf_op jit(solution)/shard_map/all_to_all | solution.py:551
  10.8 0.0 copy-done.3
  10.8 0.0 copy-done.1
  10.8 0.1 shard_map.66
  10.9 2.6 %collective-permute-start = (f32[8,128]{1,0:T(8,128)S(1)}, f32[8,128]{1,0:T(8,128)S(1)}, u32[]{:S(2)}, u32[]{:S(2)}) collective-permute-start(f32[8,128]{1,0:T(8,128)S(1)} %get-tuple-element.44), channel_id=1, source_target_pairs={{1,0},{2,1},{3,2},{5,4},{6,5},{7,6},{9,8},{10,9},{11,10},{13,12},{... | collective-permute-start | bytes 12296 | tf_op jit(solution)/shard_map/ppermute | solution.py:592
  13.6 1.3 collective-permute-done.right_ref
  14.9 5.7 %all-to-all-done.mine_ref = f32[4,128,256]{2,1,0:T(8,128)S(1)} async-done(((f32[4,128,256]{2,1,0:T(8,128)}), f32[4,128,256]{2,1,0:T(8,128)S(1)}, u32[]{:S(2)}, u32[]{:S(2)}) %all-to-all-start) | async-done | bytes 524320 | tf_op jit(solution)/shard_map/all_to_all | solution.py:551
  20.6 1.9 %collective-permute-start.1 = (f32[4,128,256]{2,1,0:T(8,128)S(1)}, f32[4,128,256]{2,1,0:T(8,128)S(1)}, u32[]{:S(2)}, u32[]{:S(2)}) collective-permute-start(f32[4,128,256]{2,1,0:T(8,128)S(1)} %all-to-all-done.mine_ref), channel_id=1, source_target_pairs={{0,4},{4,0},{1,5},{5,1},{2,6},{6,2},{3,7},{7,3},{8,12},{12,8},{9,1... | collective-permute-start | bytes 1572872 | tf_op jit(solution)/shard_map/ppermute | solution.py:594
  22.5 1.9 %collective-permute-done.1.other_ref = f32[4,128,256]{2,1,0:T(8,128)S(1)} collective-permute-done((f32[4,128,256]{2,1,0:T(8,128)S(1)}, f32[4,128,256]{2,1,0:T(8,128)S(1)}, u32[]{:S(2)}, u32[]{:S(2)}) %collective-permute-start.1) | collective-permute-done | bytes 524320 | tf_op jit(solution)/shard_map/ppermute | solution.py:594
  24.4 0.9 shard_map.67
  25.3 3.8 %collective-permute-start.3 = (f32[256,256]{1,0:T(8,128)S(1)}, f32[256,256]{1,0:T(8,128)S(1)}, u32[]{:S(2)}, u32[]{:S(2)}) collective-permute-start(f32[256,256]{1,0:T(8,128)S(1)} %get-tuple-element.49.own_ref), channel_id=1, source_target_pairs={{0,32},{32,0},{64,96},{96,64},{128,160},{160,128},{192,224},{224,1... | collective-permute-start | bytes 786440 | tf_op jit(solution)/shard_map/ppermute | solution.py:598
  29.1 1.3 collective-permute-start.2
  30.4 4.2 %collective-permute-done.2.after_ref.left_ref = f32[8,128]{1,0:T(8,128)S(1)} collective-permute-done((f32[8,128]{1,0:T(8,128)S(1)}, f32[8,128]{1,0:T(8,128)S(1)}, u32[]{:S(2)}, u32[]{:S(2)}) %collective-permute-start.2) | collective-permute-done | bytes 4128 | tf_op jit(solution)/shard_map/ppermute | solution.py:599
  34.6 1.1 collective-permute-done.3.other_ref.one_ref
  35.7 0.3 shard_map.68
  36.0 5.2 %collective-permute-start.5 = (f32[256,128]{1,0:T(8,128)S(1)}, f32[256,128]{1,0:T(8,128)S(1)}, u32[]{:S(2)}, u32[]{:S(2)}) collective-permute-start(f32[256,128]{1,0:T(8,128)S(1)} %get-tuple-element.53), channel_id=1, source_target_pairs={{0,64},{32,96},{64,0},{96,32},{128,192},{160,224},{192,128},{224,1... | collective-permute-start | bytes 393224 | tf_op jit(solution)/shard_map/ppermute | solution.py:607
  41.2 0.7 collective-permute-start.4
  41.9 0.0 collective-permute-done.4.after_ref.cross_ref
  41.9 5.3 %collective-permute-done.5.half_ref.two_ref = f32[256,128]{1,0:T(8,128)S(1)} collective-permute-done((f32[256,128]{1,0:T(8,128)S(1)}, f32[256,128]{1,0:T(8,128)S(1)}, u32[]{:S(2)}, u32[]{:S(2)}) %collective-permute-start.5) | collective-permute-done | bytes 131104 | tf_op jit(solution)/shard_map/ppermute | solution.py:607
  47.2 0.3 shard_map.69.after_ref
  47.5 1.3 collective-permute-start.6
  48.8 0.0 copy-done
  48.8 0.0 copy-done.4
  48.9 0.0 copy-done.5
  48.9 0.0 copy-done.6
  48.9 1.9 %shard_map.70 = (f32[3,8,256]{2,1,0:T(8,128)S(1)}, f32[8,256]{1,0:T(8,128)S(1)}, f32[3,8,256]{2,1,0:T(8,128)S(1)}, f32[2,8,512]{2,1,0:T(8,128)S(1)}, f32[8,256]{1,0:T(8,128)S(1)}) custom-call(f32[3,8,256]{2,1,0:T(8,128)S(1)} %copy-done.3, f32[3,8,256]{2,1,0:T(8,128)S(1)} %copy-done.4, f32[8,256]{1,0:T(8,128)S(1)} %copy-done.5, f32[3,8,256]{2,1,0:T(8,128)S(1)} %copy-done.1, ...), custom_call_target="tpu_custom_call" | custom-call | flops 100000000 | bytes 3000000 | tf_op jit(solution)/shard_map/pallas_call | solution.py:70
  50.8 1.3 shard_map.71
  52.1 0.2 shard_map.72
  52.2 8.2 %all_to_all.25.got_ref = f32[8,3,256]{2,1,0:T(4,128)S(1)} all-to-all(f32[8,3,256]{2,1,0:T(4,128)S(1)} %shard_map.72), channel_id=1, replica_groups=mesh['zh'=4,'zl'=4,'x'=4,'c'=2,'y'=4] {'x','c'}, dimensions={0} | all-to-all | bytes 49152 | tf_op jit(solution)/shard_map/all_to_all | solution.py:551
  60.5 0.4 shard_map.73.after_ref.both_ref
  60.9 5.9 %collective-permute-done.6.far_ref = f32[256,128]{1,0:T(8,128)S(1)} collective-permute-done((f32[256,128]{1,0:T(8,128)S(1)}, f32[256,128]{1,0:T(8,128)S(1)}, u32[]{:S(2)}, u32[]{:S(2)}) %collective-permute-start.6) | collective-permute-done | bytes 131104 | tf_op jit(solution)/shard_map/ppermute | solution.py:614
  66.8 1.9 %collective-permute-start.7 = (f32[2,256,128]{2,1,0:T(8,128)S(1)}, f32[2,256,128]{2,1,0:T(8,128)S(1)}, u32[]{:S(2)}, u32[]{:S(2)}) collective-permute-start(f32[2,256,128]{2,1,0:T(8,128)S(1)} %shard_map.74.mine_ref), channel_id=1, source_target_pairs={{0,4},{4,0},{1,5},{5,1},{2,6},{6,2},{3,7},{7,3},{8,12},{12,8},{9,1... | collective-permute-start | bytes 786440 | tf_op jit(solution)/shard_map/ppermute | solution.py:648
  68.7 1.5 %collective-permute-done.7.other_ref = f32[2,256,128]{2,1,0:T(8,128)S(1)} collective-permute-done((f32[2,256,128]{2,1,0:T(8,128)S(1)}, f32[2,256,128]{2,1,0:T(8,128)S(1)}, u32[]{:S(2)}, u32[]{:S(2)}) %collective-permute-start.7) | collective-permute-done | bytes 262176 | tf_op jit(solution)/shard_map/ppermute | solution.py:648
  70.2 1.0 shard_map.75
  71.2 25.0 %all_to_all.26.got_ref = f32[16,3,256]{2,1,0:T(4,128)S(1)} all-to-all(f32[16,3,256]{2,1,0:T(4,128)S(1)} %get-tuple-element.62), channel_id=1, replica_groups=mesh['zh'=4,'zl'=4,'x'=4,'c'=2,'y'=4] {'zh','zl'}, dimensions={0} | all-to-all | bytes 98304 | tf_op jit(solution)/shard_map/all_to_all | solution.py:551
  96.2 1.0 shard_map.76
  97.2 1.3 collective-permute-start.10
  98.5 1.3 collective-permute-start.8
  99.8 4.5 %collective-permute-start.9 = (f32[8,128]{1,0:T(8,128)S(1)}, f32[8,128]{1,0:T(8,128)S(1)}, u32[]{:S(2)}, u32[]{:S(2)}) collective-permute-start(f32[8,128]{1,0:T(8,128)S(1)} %get-tuple-element.70), channel_id=1, source_target_pairs={{1,0},{2,1},{3,2},{5,4},{6,5},{7,6},{9,8},{10,9},{11,10},{13,12},{... | collective-permute-start | bytes 12296 | tf_op jit(solution)/shard_map/ppermute | solution.py:665
  104.4 0.0 collective-permute-done.10.row_ref
  104.4 0.0 collective-permute-done.8.left_ref
  104.4 1.3 collective-permute-done.9.right_ref
  105.7 1.5 %shard_map.77 = (f32[3,8,256]{2,1,0:T(8,128)S(1)}, f32[8,3,256]{2,1,0:T(4,128)S(1)}) custom-call(f32[4,8,256]{2,1,0:T(8,128)S(1)} %get-tuple-element.68.u_ref, f32[3,8,256]{2,1,0:T(8,128)S(1)} %copy-done.1, f32[8,128]{1,0:T(8,128)S(1)} %collective-permute-done.8.left_ref, f32[8,128]{1,0:T(8,128)S(1)} %collective-permute-done.9.right_ref, ...), custom_call_target="tpu_custom_call" | custom-call | flops 100000000 | bytes 3000000 | tf_op jit(solution)/shard_map/pallas_call | solution.py:70
  107.2 8.3 %all_to_all.27.got_ref = f32[8,3,256]{2,1,0:T(4,128)S(1)} all-to-all(f32[8,3,256]{2,1,0:T(4,128)S(1)} %get-tuple-element.75), channel_id=1, replica_groups=mesh['zh'=4,'zl'=4,'x'=4,'c'=2,'y'=4] {'x','c'}, dimensions={0} | all-to-all | bytes 49152 | tf_op jit(solution)/shard_map/all_to_all | solution.py:551
  115.5 0.6 shard_map.78
  116.1 17.7 %all_to_all.28.got_ref = f32[16,3,256]{2,1,0:T(4,128)S(1)} all-to-all(f32[16,3,256]{2,1,0:T(4,128)S(1)} %get-tuple-element.76), channel_id=1, replica_groups=mesh['zh'=4,'zl'=4,'x'=4,'c'=2,'y'=4] {'zh','zl'}, dimensions={0} | all-to-all | bytes 98304 | tf_op jit(solution)/shard_map/all_to_all | solution.py:551
  133.8 1.6 %shard_map.79 = f32[3,8,256]{2,1,0:T(8,128)} custom-call(f32[16,3,256]{2,1,0:T(4,128)S(1)} %all_to_all.28.got_ref, f32[8,512]{1,0:T(8,128)S(1)} %get-tuple-element.77.both_ref, bf16[8,256,256]{2,1,0:T(8,128)(2,1)S(1)} %get-tuple-element.63.maps_ref, bf16[2,256,256]{2,1,0:T(8,128)(2,1)S(1)} %get-tuple-element.64.joint_ref, ...), custom_call_target="tpu_custom_call" | custom-call | flops 100000000 | bytes 1000000 | tf_op jit(solution)/shard_map/pallas_call | solution.py:70
  (1 shorter events, 0.0 us)
Async XLA Ops:
  0.0 10.8 %copy-start.3 = (f32[3,8,256]{2,1,0:T(8,128)S(1)}, f32[3,8,256]{2,1,0:T(8,128)}, u32[]{:S(2)}) copy-start(f32[3,8,256]{2,1,0:T(8,128)} %u_ref.3) | copy-start | bytes 73732
  0.0 10.8 %copy-start.1 = (f32[3,8,256]{2,1,0:T(8,128)S(1)}, f32[3,8,256]{2,1,0:T(8,128)}, u32[]{:S(2)}) copy-start(f32[3,8,256]{2,1,0:T(8,128)} %stiff_ref.9) | copy-start | bytes 73732
  2.9 45.9 %copy-start = (bf16[4,512,512]{2,1,0:T(8,128)(2,1)S(1)}, bf16[4,512,512]{2,1,0:T(8,128)(2,1)}, u32[]{:S(2)}) copy-start(bf16[4,512,512]{2,1,0:T(8,128)(2,1)} %inv_ref.7) | copy-start | bytes 6291460
  2.9 45.9 %copy-start.4 = (f32[3,8,256]{2,1,0:T(8,128)S(1)}, f32[3,8,256]{2,1,0:T(8,128)}, u32[]{:S(2)}) copy-start(f32[3,8,256]{2,1,0:T(8,128)} %target_ref.1) | copy-start | bytes 73732
  2.9 45.9 %copy-start.5 = (f32[8,256]{1,0:T(8,128)S(1)}, f32[8,256]{1,0:T(8,128)}, u32[]{:S(2)}) copy-start(f32[8,256]{1,0:T(8,128)} %inertia_ref.1) | copy-start | bytes 24580
  2.9 45.9 %copy-start.6 = (s32[64]{0:T(128)S(1)}, s32[64]{0:T(128)}, u32[]{:S(2)}) copy-start(s32[64]{0:T(128)} %pin_ref.1) | copy-start | bytes 772
  5.7 0.8 copy-start.2
  6.5 14.1 %all-to-all-start = ((f32[4,128,256]{2,1,0:T(8,128)}), f32[4,128,256]{2,1,0:T(8,128)S(1)}, u32[]{:S(2)}, u32[]{:S(2)}) async-start(f32[4,128,256]{2,1,0:T(8,128)} %copy-done.2), calls=%async_computation | async-start | bytes 1048576 | tf_op jit(solution)/shard_map/all_to_all | solution.py:551
  10.9 4.0 %collective-permute-start = (f32[8,128]{1,0:T(8,128)S(1)}, f32[8,128]{1,0:T(8,128)S(1)}, u32[]{:S(2)}, u32[]{:S(2)}) collective-permute-start(f32[8,128]{1,0:T(8,128)S(1)} %get-tuple-element.44), channel_id=1, source_target_pairs={{1,0},{2,1},{3,2},{5,4},{6,5},{7,6},{9,8},{10,9},{11,10},{13,12},{... | collective-permute-start | bytes 12296 | tf_op jit(solution)/shard_map/ppermute | solution.py:592
  20.6 3.8 %collective-permute-start.1 = (f32[4,128,256]{2,1,0:T(8,128)S(1)}, f32[4,128,256]{2,1,0:T(8,128)S(1)}, u32[]{:S(2)}, u32[]{:S(2)}) collective-permute-start(f32[4,128,256]{2,1,0:T(8,128)S(1)} %all-to-all-done.mine_ref), channel_id=1, source_target_pairs={{0,4},{4,0},{1,5},{5,1},{2,6},{6,2},{3,7},{7,3},{8,12},{12,8},{9,1... | collective-permute-start | bytes 1572872 | tf_op jit(solution)/shard_map/ppermute | solution.py:594
  25.3 10.4 %collective-permute-start.3 = (f32[256,256]{1,0:T(8,128)S(1)}, f32[256,256]{1,0:T(8,128)S(1)}, u32[]{:S(2)}, u32[]{:S(2)}) collective-permute-start(f32[256,256]{1,0:T(8,128)S(1)} %get-tuple-element.49.own_ref), channel_id=1, source_target_pairs={{0,32},{32,0},{64,96},{96,64},{128,160},{160,128},{192,224},{224,1... | collective-permute-start | bytes 786440 | tf_op jit(solution)/shard_map/ppermute | solution.py:598
  29.1 5.5 %collective-permute-start.2 = (f32[8,128]{1,0:T(8,128)S(1)}, f32[8,128]{1,0:T(8,128)S(1)}, u32[]{:S(2)}, u32[]{:S(2)}) collective-permute-start(f32[8,128]{1,0:T(8,128)S(1)} %get-tuple-element.47), channel_id=1, source_target_pairs={{0,1},{1,2},{2,3},{4,5},{5,6},{6,7},{8,9},{9,10},{10,11},{12,13},{... | collective-permute-start | bytes 12296 | tf_op jit(solution)/shard_map/ppermute | solution.py:599
  36.0 11.2 %collective-permute-start.5 = (f32[256,128]{1,0:T(8,128)S(1)}, f32[256,128]{1,0:T(8,128)S(1)}, u32[]{:S(2)}, u32[]{:S(2)}) collective-permute-start(f32[256,128]{1,0:T(8,128)S(1)} %get-tuple-element.53), channel_id=1, source_target_pairs={{0,64},{32,96},{64,0},{96,32},{128,192},{160,224},{192,128},{224,1... | collective-permute-start | bytes 393224 | tf_op jit(solution)/shard_map/ppermute | solution.py:607
  41.2 0.7 collective-permute-start.4
  47.5 19.2 %collective-permute-start.6 = (f32[256,128]{1,0:T(8,128)S(1)}, f32[256,128]{1,0:T(8,128)S(1)}, u32[]{:S(2)}, u32[]{:S(2)}) collective-permute-start(f32[256,128]{1,0:T(8,128)S(1)} %shard_map.69.after_ref), channel_id=1, source_target_pairs={{128,0},{160,32},{192,64},{224,96},{256,384},{288,416},{320,448},{... | collective-permute-start | bytes 393224 | tf_op jit(solution)/shard_map/ppermute | solution.py:614
  66.8 3.4 %collective-permute-start.7 = (f32[2,256,128]{2,1,0:T(8,128)S(1)}, f32[2,256,128]{2,1,0:T(8,128)S(1)}, u32[]{:S(2)}, u32[]{:S(2)}) collective-permute-start(f32[2,256,128]{2,1,0:T(8,128)S(1)} %shard_map.74.mine_ref), channel_id=1, source_target_pairs={{0,4},{4,0},{1,5},{5,1},{2,6},{6,2},{3,7},{7,3},{8,12},{12,8},{9,1... | collective-permute-start | bytes 786440 | tf_op jit(solution)/shard_map/ppermute | solution.py:648
  97.2 7.2 %collective-permute-start.10 = (f32[4,256]{1,0:T(4,128)S(1)}, f32[4,256]{1,0:T(4,128)S(1)}, u32[]{:S(2)}, u32[]{:S(2)}) collective-permute-start(f32[4,256]{1,0:T(4,128)S(1)} %get-tuple-element.71), channel_id=1, source_target_pairs={{4,0},{8,4},{12,8},{16,12},{20,16},{24,20},{28,24},{32,28},{36,32}... | collective-permute-start | bytes 12296 | tf_op jit(solution)/shard_map/ppermute | solution.py:664
  98.5 5.9 %collective-permute-start.8 = (f32[8,128]{1,0:T(8,128)S(1)}, f32[8,128]{1,0:T(8,128)S(1)}, u32[]{:S(2)}, u32[]{:S(2)}) collective-permute-start(f32[8,128]{1,0:T(8,128)S(1)} %get-tuple-element.69), channel_id=1, source_target_pairs={{0,1},{1,2},{2,3},{4,5},{5,6},{6,7},{8,9},{9,10},{10,11},{12,13},{... | collective-permute-start | bytes 12296 | tf_op jit(solution)/shard_map/ppermute | solution.py:666
  99.8 5.9 %collective-permute-start.9 = (f32[8,128]{1,0:T(8,128)S(1)}, f32[8,128]{1,0:T(8,128)S(1)}, u32[]{:S(2)}, u32[]{:S(2)}) collective-permute-start(f32[8,128]{1,0:T(8,128)S(1)} %get-tuple-element.70), channel_id=1, source_target_pairs={{1,0},{2,1},{3,2},{5,4},{6,5},{7,6},{9,8},{10,9},{11,10},{13,12},{... | collective-permute-start | bytes 12296 | tf_op jit(solution)/shard_map/ppermute | solution.py:665

commit v7 on v5

--- a/solution.py
+++ b/solution.py
@@ -149,9 +149,7 @@
     return jnp.concatenate([rows[:, :128], rows[:, 128:]], axis=0)
 
 
-def joined(mine_ref, other_ref):
-    core = lax.axis_index("c")
-    first, second = in_order(mine_ref[...], other_ref[...], core == 1)
+def joined(first, second):
     columns = jnp.concatenate([first, second], axis=1)
     rows = jnp.concatenate([rows_of_half(first), rows_of_half(second)], axis=0)
     return jnp.where(high_bit() == 0, columns, rows)
@@ -221,12 +219,12 @@
     out_ref[1] = far_ref[...]
 
 
-def group_maps_kernel(both_ref, one_ref, mine_ref, other_ref, out_ref, joint_ref, msg_ref):
+def group_maps_kernel(both_ref, one_ref, halves_ref, out_ref, joint_ref, msg_ref):
     zh = lax.axis_index("zh")
     one = eye()
     sibling = one_ref[...]
-    two = pair(joined(mine_ref.at[0], other_ref.at[0]))
-    far = joined(mine_ref.at[1], other_ref.at[1])
+    two = pair(joined(halves_ref[0, 0], halves_ref[1, 0]))
+    far = joined(halves_ref[0, 1], halves_ref[1, 1])
     send = jnp.where(low_bit() == 0, sibling, one)
     take = jnp.where(low_bit() == 1, sibling, one)
     for k, value in ((0, send), (4, take)):
@@ -609,21 +607,21 @@
         flops=10**8,
         size=3 * 10**6,
     )
-    group_half = call(
-        four_planes_kernel, half, (two, two_mine, base), specs=[None, None, anywhere]
-    )
-    steps = [(4 + k, k) for k in range(4)] + [(8 + k, 12 + k) for k in range(4)]
-    far_mine = lax.ppermute(group_half, ZAX, steps)
-
     wide = sds((4 * CB, 2 * CB), BF16)
     narrow = sds((CB, CB), BF16)
     xh, xl, eh, el, sends = call(
         plane_maps_kernel,
         [wide, wide, narrow, narrow, sds((4, CB, CB), BF16)],
-        (chip, sib_chip, two_chips, far_chips, core_maps, group_half),
+        (chip, sib_chip, two_chips, far_chips, core_maps, base),
         specs=[None] * 5 + [anywhere],
         flops=10**9,
     )
+    group_half = call(
+        four_planes_kernel, half, (two, two_mine, sends), specs=[None, None, anywhere]
+    )
+    steps = [(4 + k, k) for k in range(4)] + [(8 + k, 12 + k) for k in range(4)]
+    far_mine = lax.ppermute(group_half, ZAX, steps)
+
     msg = call(offsets_kernel, sds((8, 3, CB)), (offset, sends))
     got = swap(msg, PLANE)
     both = call(
@@ -636,11 +634,11 @@
     mine = call(
         bundle_kernel, sds((2, CB, 128)), (two_mine, far_mine, both), specs=[None, None, anywhere]
     )
-    other = lax.ppermute(mine, "c", cores)
+    halves = lax.all_gather(mine, "c")
     maps, joint, msg = call(
         group_maps_kernel,
         [sds((8, CB, CB), BF16), sds((2, CB, CB), BF16), sds((16, 3, CB))],
-        (both, beside, mine, other),
+        (both, beside, halves),
         flops=5 * 10**8,
     )
     got = swap(msg, ZAX)

time: 135 us -> 133 us (0.985)
  waiting for transfers between devices: 22.6 us -> 18.6 us
  blocking collectives: 66 us -> 68.1 us
    ppermute x2, waiting for transfers between devices: 7.94 us -> 4.2 us  [shards(): from_left = lax.ppermute(right, 'y', to_right)]
    all_gather x0 -> x1, blocking collectives: none -> 2.18 us  [shards(): halves = lax.all_gather(mine, 'c')]
    ppermute x1 -> x0, starting transfers between devices: 1.92 us -> none  [shards(): other = lax.ppermute(mine, 'c', cores)]
    ppermute x2, starting transfers between devices: 5.29 us -> 7.18 us  [shards(): from_right = lax.ppermute(left, 'y', to_left)]
    ppermute x1 -> x0, waiting for transfers between devices: 1.5 us -> none  [shards(): other = lax.ppermute(mine, 'c', cores)]
  transfers between devices with their start and end apart: 12 -> 11, of which waited for: 9 -> 7; matrix products, arithmetic and copies ran while one was open for 0% -> 0% of each run, Pallas kernels for 3% -> 3%
where the time goes in v7:
time: 133 us; the launch traced here: 132 us
  blocking collectives  68.1 us (51%)
  starting transfers between devices  31.2 us (23%)
  waiting for transfers between devices  18.6 us (14%)
  Pallas kernels  13.8 us (10%)
    all_to_all x4, blocking collectives, swap(): return lax.all_to_all(value, axes, 0, 0)  63.4 us
    pallas_call x17, Pallas kernels, call(): pl.pallas_call(kernel, out_shape=outs, in_specs=in_specs, out_specs=out_s...  13.8 us
    ppermute x2, starting transfers between devices, shards(): from_right = lax.ppermute(left, 'y', to_left)  7.18 us
    ppermute x1, waiting for transfers between devices, shards(): far_chips = lax.ppermute(two_chips, 'x', [(k, 3 - k) for k in range(4)])  5.27 us
    ppermute x1, starting transfers between devices, shards(): two_mine = lax.ppermute(two_half, ZAX, [(k, k ^ 2) for k in range(16)])  5.18 us
    ppermute x1, starting transfers between devices, shards(): beside = lax.ppermute(plane, ZAX, [(k, k ^ 1) for k in range(16)])  4.92 us
    ppermute x1, starting transfers between devices, shards(): far_chips = lax.ppermute(two_chips, 'x', [(k, 3 - k) for k in range(4)])  4.67 us
    ppermute x2, waiting for transfers between devices, shards(): from_left = lax.ppermute(right, 'y', to_right)  4.2 us
  transfers between devices with their start and end apart: 11, of which 7 were waited for; matrix products, arithmetic and copies ran while one was open for 0% of the time, Pallas kernels for 3%

profile of v7, /device:TPU:24, one launch (start us, length us, event | category | flops | bytes accessed | tf_op | source)
XLA Modules:
  0.0 132.1 jit_solution(16999146072799516954)
XLA Ops:
  0.0 0.0 copy-start.1
  0.0 0.0 copy-start.2
  0.0 2.9 %shard_map.64 = f32[264,256]{1,0:T(8,128)} custom-call(bf16[4,512,512]{2,1,0:T(8,128)(2,1)} %inv_ref.7, f32[3,8,256]{2,1,0:T(8,128)} %stiff_ref.9, f32[3,8,256]{2,1,0:T(8,128)} %u_ref.3), custom_call_target="tpu_custom_call" | custom-call | flops 100000000 | bytes 1000000 | tf_op jit(solution)/shard_map/pallas_call | solution.py:70
  2.9 0.0 copy-start
  2.9 0.0 copy-start.3
  2.9 0.0 copy-start.4
  2.9 0.0 copy-start.5
  3.0 2.5 %all-gather = f32[528,256]{1,0:T(8,128)S(1)} all-gather(f32[264,256]{1,0:T(8,128)} %shard_map.64), channel_id=2, replica_groups=mesh['zh'=4,'zl'=4,'x'=4,'c'=2,'y'=4] {'c'}, dimensions={0}, use_global_device_ids=true | all-gather | bytes 811008 | tf_op jit(solution)/shard_map/all_gather | solution.py:561
  5.5 0.3 shard_map.65
  5.8 3.4 %collective-permute-start = (f32[256,256]{1,0:T(8,128)S(1)}, f32[256,256]{1,0:T(8,128)S(1)}, u32[]{:S(2)}, u32[]{:S(2)}) collective-permute-start(f32[256,256]{1,0:T(8,128)S(1)} %get-tuple-element.37.after_ref.own_ref), channel_id=1, source_target_pairs={{0,8},{8,0},{16,24},{24,16},{1,9},{9,1},{17,25},{25,17},{2,10},{10... | collective-permute-start | bytes 786440 | tf_op jit(solution)/shard_map/ppermute | solution.py:564
  9.2 0.0 copy-done.1
  9.2 0.0 copy-done.2
  9.2 0.1 shard_map.66
  9.3 2.6 %collective-permute-start.1 = (f32[8,128]{1,0:T(8,128)S(1)}, f32[8,128]{1,0:T(8,128)S(1)}, u32[]{:S(2)}, u32[]{:S(2)}) collective-permute-start(f32[8,128]{1,0:T(8,128)S(1)} %get-tuple-element.39), channel_id=1, source_target_pairs={{1,0},{2,1},{3,2},{5,4},{6,5},{7,6},{9,8},{10,9},{11,10},{13,12},{... | collective-permute-start | bytes 12296 | tf_op jit(solution)/shard_map/ppermute | solution.py:574
  11.9 1.3 collective-permute-done.1.after_ref.right_ref
  13.2 2.8 %collective-permute-done.other_ref.sib_ref = f32[256,256]{1,0:T(8,128)S(1)} collective-permute-done((f32[256,256]{1,0:T(8,128)S(1)}, f32[256,256]{1,0:T(8,128)S(1)}, u32[]{:S(2)}, u32[]{:S(2)}) %collective-permute-start) | collective-permute-done | bytes 262176 | tf_op jit(solution)/shard_map/ppermute | solution.py:564
  16.0 0.3 shard_map.67
  16.3 4.7 %collective-permute-start.2 = (f32[256,256]{1,0:T(8,128)S(1)}, f32[256,256]{1,0:T(8,128)S(1)}, u32[]{:S(2)}, u32[]{:S(2)}) collective-permute-start(f32[256,256]{1,0:T(8,128)S(1)} %get-tuple-element.40.own_ref.two_ref), channel_id=1, source_target_pairs={{0,24},{8,16},{16,8},{24,0},{1,25},{9,17},{17,9},{25,1},{2,26},{10... | collective-permute-start | bytes 786440 | tf_op jit(solution)/shard_map/ppermute | solution.py:581
  21.0 0.7 collective-permute-start.3
  21.7 0.0 collective-permute-done.3.after_ref.cross_ref
  21.7 5.3 %collective-permute-done.2.other_ref.far_ref = f32[256,256]{1,0:T(8,128)S(1)} collective-permute-done((f32[256,256]{1,0:T(8,128)S(1)}, f32[256,256]{1,0:T(8,128)S(1)}, u32[]{:S(2)}, u32[]{:S(2)}) %collective-permute-start.2) | collective-permute-done | bytes 262176 | tf_op jit(solution)/shard_map/ppermute | solution.py:581
  26.9 0.3 shard_map.68
  27.2 4.9 %collective-permute-start.5 = (f32[256,256]{1,0:T(8,128)S(1)}, f32[256,256]{1,0:T(8,128)S(1)}, u32[]{:S(2)}, u32[]{:S(2)}) collective-permute-start(f32[256,256]{1,0:T(8,128)S(1)} %get-tuple-element.45.own_ref), channel_id=1, source_target_pairs={{0,32},{32,0},{64,96},{96,64},{128,160},{160,128},{192,224},{224,1... | collective-permute-start | bytes 786440 | tf_op jit(solution)/shard_map/ppermute | solution.py:590
  32.2 1.3 collective-permute-start.4
  33.5 4.2 %collective-permute-done.4.rest_0_.left_ref = f32[8,128]{1,0:T(8,128)S(1)} collective-permute-done((f32[8,128]{1,0:T(8,128)S(1)}, f32[8,128]{1,0:T(8,128)S(1)}, u32[]{:S(2)}, u32[]{:S(2)}) %collective-permute-start.4) | collective-permute-done | bytes 4128 | tf_op jit(solution)/shard_map/ppermute | solution.py:592
  37.7 0.0 collective-permute-done.5.other_ref.one_ref
  37.7 0.3 shard_map.69
  38.0 5.2 %collective-permute-start.6 = (f32[256,128]{1,0:T(8,128)S(1)}, f32[256,128]{1,0:T(8,128)S(1)}, u32[]{:S(2)}, u32[]{:S(2)}) collective-permute-start(f32[256,128]{1,0:T(8,128)S(1)} %get-tuple-element.52), channel_id=1, source_target_pairs={{0,64},{32,96},{64,0},{96,32},{128,192},{160,224},{192,128},{224,1... | collective-permute-start | bytes 393224 | tf_op jit(solution)/shard_map/ppermute | solution.py:597
  43.2 0.0 copy-done
  43.2 0.0 copy-done.3
  43.2 0.0 copy-done.4
  43.2 0.0 copy-done.5
  43.2 1.9 %shard_map.70 = (f32[3,8,256]{2,1,0:T(8,128)S(1)}, f32[8,256]{1,0:T(8,128)S(1)}, f32[3,8,256]{2,1,0:T(8,128)S(1)}, f32[2,8,512]{2,1,0:T(8,128)S(1)}, f32[8,256]{1,0:T(8,128)S(1)}) custom-call(f32[3,8,256]{2,1,0:T(8,128)S(1)} %copy-done.2, f32[3,8,256]{2,1,0:T(8,128)S(1)} %copy-done.3, f32[8,256]{1,0:T(8,128)S(1)} %copy-done.4, f32[3,8,256]{2,1,0:T(8,128)S(1)} %copy-done.1, ...), custom_call_target="tpu_custom_call" | custom-call | flops 100000000 | bytes 3000000 | tf_op jit(solution)/shard_map/pallas_call | solution.py:70
  45.1 1.3 shard_map.71
  46.4 1.1 collective-permute-done.6.half_ref.two_ref
  47.5 0.3 shard_map.74
  47.8 1.3 collective-permute-start.7
  49.1 0.2 shard_map.72
  49.3 11.4 %all_to_all.20.got_ref = f32[8,3,256]{2,1,0:T(4,128)S(1)} all-to-all(f32[8,3,256]{2,1,0:T(4,128)S(1)} %shard_map.72), channel_id=1, replica_groups=mesh['zh'=4,'zl'=4,'x'=4,'c'=2,'y'=4] {'x','c'}, dimensions={0} | all-to-all | bytes 49152 | tf_op jit(solution)/shard_map/all_to_all | solution.py:539
  60.7 0.4 shard_map.73.after_ref.both_ref
  61.1 2.3 %collective-permute-done.7.far_ref = f32[256,128]{1,0:T(8,128)S(1)} collective-permute-done((f32[256,128]{1,0:T(8,128)S(1)}, f32[256,128]{1,0:T(8,128)S(1)}, u32[]{:S(2)}, u32[]{:S(2)}) %collective-permute-start.7) | collective-permute-done | bytes 131104 | tf_op jit(solution)/shard_map/ppermute | solution.py:623
  63.4 2.2 %all-gather.1 = f32[4,256,128]{2,1,0:T(8,128)S(1)} all-gather(f32[2,256,128]{2,1,0:T(8,128)S(1)} %shard_map.75), channel_id=3, replica_groups=mesh['zh'=4,'zl'=4,'x'=4,'c'=2,'y'=4] {'c'}, dimensions={0}, use_global_device_ids=true | all-gather | bytes 786432 | tf_op jit(solution)/shard_map/all_gather | solution.py:637
  65.6 1.0 shard_map.76
  66.5 25.0 %all_to_all.21.got_ref = f32[16,3,256]{2,1,0:T(4,128)S(1)} all-to-all(f32[16,3,256]{2,1,0:T(4,128)S(1)} %get-tuple-element.53), channel_id=1, replica_groups=mesh['zh'=4,'zl'=4,'x'=4,'c'=2,'y'=4] {'zh','zl'}, dimensions={0} | all-to-all | bytes 98304 | tf_op jit(solution)/shard_map/all_to_all | solution.py:539
  91.5 1.0 shard_map.77
  92.5 1.3 collective-permute-start.8
  93.8 4.5 %collective-permute-start.9 = (f32[8,128]{1,0:T(8,128)S(1)}, f32[8,128]{1,0:T(8,128)S(1)}, u32[]{:S(2)}, u32[]{:S(2)}) collective-permute-start(f32[8,128]{1,0:T(8,128)S(1)} %get-tuple-element.60), channel_id=1, source_target_pairs={{1,0},{2,1},{3,2},{5,4},{6,5},{7,6},{9,8},{10,9},{11,10},{13,12},{... | collective-permute-start | bytes 12296 | tf_op jit(solution)/shard_map/ppermute | solution.py:654
  98.4 1.3 collective-permute-start.10
  99.7 0.0 collective-permute-done.8.left_ref
  99.7 0.0 collective-permute-done.9.right_ref
  99.7 1.7 %collective-permute-done.10.row_ref = f32[4,256]{1,0:T(4,128)S(1)} collective-permute-done((f32[4,256]{1,0:T(4,128)S(1)}, f32[4,256]{1,0:T(4,128)S(1)}, u32[]{:S(2)}, u32[]{:S(2)}) %collective-permute-start.10) | collective-permute-done | bytes 4128 | tf_op jit(solution)/shard_map/ppermute | solution.py:653
  101.4 1.5 %shard_map.78 = (f32[3,8,256]{2,1,0:T(8,128)S(1)}, f32[8,3,256]{2,1,0:T(4,128)S(1)}) custom-call(f32[4,8,256]{2,1,0:T(8,128)S(1)} %get-tuple-element.58.u_ref, f32[3,8,256]{2,1,0:T(8,128)S(1)} %copy-done.1, f32[8,128]{1,0:T(8,128)S(1)} %collective-permute-done.8.left_ref, f32[8,128]{1,0:T(8,128)S(1)} %collective-permute-done.9.right_ref, ...), custom_call_target="tpu_custom_call" | custom-call | flops 100000000 | bytes 3000000 | tf_op jit(solution)/shard_map/pallas_call | solution.py:70
  102.9 10.1 %all_to_all.22.got_ref = f32[8,3,256]{2,1,0:T(4,128)S(1)} all-to-all(f32[8,3,256]{2,1,0:T(4,128)S(1)} %get-tuple-element.65), channel_id=1, replica_groups=mesh['zh'=4,'zl'=4,'x'=4,'c'=2,'y'=4] {'x','c'}, dimensions={0} | all-to-all | bytes 49152 | tf_op jit(solution)/shard_map/all_to_all | solution.py:539
  113.0 0.6 shard_map.79
  113.6 16.9 %all_to_all.23.got_ref = f32[16,3,256]{2,1,0:T(4,128)S(1)} all-to-all(f32[16,3,256]{2,1,0:T(4,128)S(1)} %get-tuple-element.66), channel_id=1, replica_groups=mesh['zh'=4,'zl'=4,'x'=4,'c'=2,'y'=4] {'zh','zl'}, dimensions={0} | all-to-all | bytes 98304 | tf_op jit(solution)/shard_map/all_to_all | solution.py:539
  130.5 1.6 %shard_map.80 = f32[3,8,256]{2,1,0:T(8,128)} custom-call(f32[16,3,256]{2,1,0:T(4,128)S(1)} %all_to_all.23.got_ref, f32[8,512]{1,0:T(8,128)S(1)} %get-tuple-element.67.both_ref, bf16[8,256,256]{2,1,0:T(8,128)(2,1)S(1)} %get-tuple-element.54.maps_ref, bf16[2,256,256]{2,1,0:T(8,128)(2,1)S(1)} %get-tuple-element.55.joint_ref, ...), custom_call_target="tpu_custom_call" | custom-call | flops 100000000 | bytes 1000000 | tf_op jit(solution)/shard_map/pallas_call | solution.py:70
  (1 shorter events, 0.0 us)
Async XLA Ops:
  0.0 9.2 %copy-start.1 = (f32[3,8,256]{2,1,0:T(8,128)S(1)}, f32[3,8,256]{2,1,0:T(8,128)}, u32[]{:S(2)}) copy-start(f32[3,8,256]{2,1,0:T(8,128)} %stiff_ref.9) | copy-start | bytes 73732
  0.0 9.2 %copy-start.2 = (f32[3,8,256]{2,1,0:T(8,128)S(1)}, f32[3,8,256]{2,1,0:T(8,128)}, u32[]{:S(2)}) copy-start(f32[3,8,256]{2,1,0:T(8,128)} %u_ref.3) | copy-start | bytes 73732
  2.9 40.2 %copy-start = (bf16[4,512,512]{2,1,0:T(8,128)(2,1)S(1)}, bf16[4,512,512]{2,1,0:T(8,128)(2,1)}, u32[]{:S(2)}) copy-start(bf16[4,512,512]{2,1,0:T(8,128)(2,1)} %inv_ref.7) | copy-start | bytes 6291460
  2.9 40.2 %copy-start.3 = (f32[3,8,256]{2,1,0:T(8,128)S(1)}, f32[3,8,256]{2,1,0:T(8,128)}, u32[]{:S(2)}) copy-start(f32[3,8,256]{2,1,0:T(8,128)} %target_ref.1) | copy-start | bytes 73732
  2.9 40.2 %copy-start.4 = (f32[8,256]{1,0:T(8,128)S(1)}, f32[8,256]{1,0:T(8,128)}, u32[]{:S(2)}) copy-start(f32[8,256]{1,0:T(8,128)} %inertia_ref.1) | copy-start | bytes 24580
  2.9 40.2 %copy-start.5 = (s32[64]{0:T(128)S(1)}, s32[64]{0:T(128)}, u32[]{:S(2)}) copy-start(s32[64]{0:T(128)} %pin_ref.1) | copy-start | bytes 772
  5.8 10.2 %collective-permute-start = (f32[256,256]{1,0:T(8,128)S(1)}, f32[256,256]{1,0:T(8,128)S(1)}, u32[]{:S(2)}, u32[]{:S(2)}) collective-permute-start(f32[256,256]{1,0:T(8,128)S(1)} %get-tuple-element.37.after_ref.own_ref), channel_id=1, source_target_pairs={{0,8},{8,0},{16,24},{24,16},{1,9},{9,1},{17,25},{25,17},{2,10},{10... | collective-permute-start | bytes 786440 | tf_op jit(solution)/shard_map/ppermute | solution.py:564
  9.3 4.0 %collective-permute-start.1 = (f32[8,128]{1,0:T(8,128)S(1)}, f32[8,128]{1,0:T(8,128)S(1)}, u32[]{:S(2)}, u32[]{:S(2)}) collective-permute-start(f32[8,128]{1,0:T(8,128)S(1)} %get-tuple-element.39), channel_id=1, source_target_pairs={{1,0},{2,1},{3,2},{5,4},{6,5},{7,6},{9,8},{10,9},{11,10},{13,12},{... | collective-permute-start | bytes 12296 | tf_op jit(solution)/shard_map/ppermute | solution.py:574
  16.3 10.6 %collective-permute-start.2 = (f32[256,256]{1,0:T(8,128)S(1)}, f32[256,256]{1,0:T(8,128)S(1)}, u32[]{:S(2)}, u32[]{:S(2)}) collective-permute-start(f32[256,256]{1,0:T(8,128)S(1)} %get-tuple-element.40.own_ref.two_ref), channel_id=1, source_target_pairs={{0,24},{8,16},{16,8},{24,0},{1,25},{9,17},{17,9},{25,1},{2,26},{10... | collective-permute-start | bytes 786440 | tf_op jit(solution)/shard_map/ppermute | solution.py:581
  21.0 0.7 collective-permute-start.3
  27.2 10.4 %collective-permute-start.5 = (f32[256,256]{1,0:T(8,128)S(1)}, f32[256,256]{1,0:T(8,128)S(1)}, u32[]{:S(2)}, u32[]{:S(2)}) collective-permute-start(f32[256,256]{1,0:T(8,128)S(1)} %get-tuple-element.45.own_ref), channel_id=1, source_target_pairs={{0,32},{32,0},{64,96},{96,64},{128,160},{160,128},{192,224},{224,1... | collective-permute-start | bytes 786440 | tf_op jit(solution)/shard_map/ppermute | solution.py:590
  32.2 5.5 %collective-permute-start.4 = (f32[8,128]{1,0:T(8,128)S(1)}, f32[8,128]{1,0:T(8,128)S(1)}, u32[]{:S(2)}, u32[]{:S(2)}) collective-permute-start(f32[8,128]{1,0:T(8,128)S(1)} %get-tuple-element.43), channel_id=1, source_target_pairs={{0,1},{1,2},{2,3},{4,5},{5,6},{6,7},{8,9},{9,10},{10,11},{12,13},{... | collective-permute-start | bytes 12296 | tf_op jit(solution)/shard_map/ppermute | solution.py:592
  38.0 9.5 %collective-permute-start.6 = (f32[256,128]{1,0:T(8,128)S(1)}, f32[256,128]{1,0:T(8,128)S(1)}, u32[]{:S(2)}, u32[]{:S(2)}) collective-permute-start(f32[256,128]{1,0:T(8,128)S(1)} %get-tuple-element.52), channel_id=1, source_target_pairs={{0,64},{32,96},{64,0},{96,32},{128,192},{160,224},{192,128},{224,1... | collective-permute-start | bytes 393224 | tf_op jit(solution)/shard_map/ppermute | solution.py:597
  47.8 15.5 %collective-permute-start.7 = (f32[256,128]{1,0:T(8,128)S(1)}, f32[256,128]{1,0:T(8,128)S(1)}, u32[]{:S(2)}, u32[]{:S(2)}) collective-permute-start(f32[256,128]{1,0:T(8,128)S(1)} %shard_map.74), channel_id=1, source_target_pairs={{128,0},{160,32},{192,64},{224,96},{256,384},{288,416},{320,448},{... | collective-permute-start | bytes 393224 | tf_op jit(solution)/shard_map/ppermute | solution.py:623
  92.5 7.2 %collective-permute-start.8 = (f32[8,128]{1,0:T(8,128)S(1)}, f32[8,128]{1,0:T(8,128)S(1)}, u32[]{:S(2)}, u32[]{:S(2)}) collective-permute-start(f32[8,128]{1,0:T(8,128)S(1)} %get-tuple-element.59), channel_id=1, source_target_pairs={{0,1},{1,2},{2,3},{4,5},{5,6},{6,7},{8,9},{9,10},{10,11},{12,13},{... | collective-permute-start | bytes 12296 | tf_op jit(solution)/shard_map/ppermute | solution.py:655
  93.8 5.9 %collective-permute-start.9 = (f32[8,128]{1,0:T(8,128)S(1)}, f32[8,128]{1,0:T(8,128)S(1)}, u32[]{:S(2)}, u32[]{:S(2)}) collective-permute-start(f32[8,128]{1,0:T(8,128)S(1)} %get-tuple-element.60), channel_id=1, source_target_pairs={{1,0},{2,1},{3,2},{5,4},{6,5},{7,6},{9,8},{10,9},{11,10},{13,12},{... | collective-permute-start | bytes 12296 | tf_op jit(solution)/shard_map/ppermute | solution.py:654
  98.4 3.1 %collective-permute-start.10 = (f32[4,256]{1,0:T(4,128)S(1)}, f32[4,256]{1,0:T(4,128)S(1)}, u32[]{:S(2)}, u32[]{:S(2)}) collective-permute-start(f32[4,256]{1,0:T(4,128)S(1)} %get-tuple-element.61), channel_id=1, source_target_pairs={{4,0},{8,4},{12,8},{16,12},{20,16},{24,20},{28,24},{32,28},{36,32}... | collective-permute-start | bytes 12296 | tf_op jit(solution)/shard_map/ppermute | solution.py:653

commit v8 on v7

--- a/solution.py
+++ b/solution.py
@@ -407,7 +407,7 @@
 
 
 def second_side_kernel(
-    u_ref, stiff_ref, left_ref, right_ref, row_ref, inv_ref, sends_ref, inertial_ref, ext_ref,
+    u_ref, stiff_ref, row_ref, left_ref, right_ref, inv_ref, sends_ref, inertial_ref, ext_ref,
     above_ref, base_ref, msg_ref,
 ):
     core = lax.axis_index("c")
@@ -656,7 +656,7 @@
     base, msg = call(
         second_side_kernel,
         [field, sds((8, 3, CB))],
-        (middle, stiffness, from_left, from_right, low_row, inverses, sends)
+        (middle, stiffness, low_row, from_left, from_right, inverses, sends)
         + (inertial, ext, above),
         flops=10**8,
         size=3 * 10**6,

time: 133 us -> 133 us (level); the launches traced: 132 us -> 131 us
    ppermute x1, waiting for transfers between devices: 1.74 us -> 0.01 us  [shards(): low_row = lax.ppermute(low_row, STRIP, [(k + 1, k) for k in range(127)])]
where the time goes in v8:
time: 133 us; the launch traced here: 131 us
  blocking collectives  67.2 us (51%)
  starting transfers between devices  31.2 us (23%)
  waiting for transfers between devices  18.2 us (14%)
  Pallas kernels  13.8 us (10%)
    all_to_all x4, blocking collectives, swap(): return lax.all_to_all(value, axes, 0, 0)  62.5 us
    pallas_call x17, Pallas kernels, call(): pl.pallas_call(kernel, out_shape=outs, in_specs=in_specs, out_specs=out_s...  13.8 us
    ppermute x2, starting transfers between devices, shards(): from_right = lax.ppermute(left, 'y', to_left)  7.18 us
    ppermute x1, waiting for transfers between devices, shards(): far_chips = lax.ppermute(two_chips, 'x', [(k, 3 - k) for k in range(4)])  5.27 us
    ppermute x1, starting transfers between devices, shards(): two_mine = lax.ppermute(two_half, ZAX, [(k, k ^ 2) for k in range(16)])  5.18 us
    ppermute x1, starting transfers between devices, shards(): beside = lax.ppermute(plane, ZAX, [(k, k ^ 1) for k in range(16)])  4.92 us
    ppermute x1, starting transfers between devices, shards(): far_chips = lax.ppermute(two_chips, 'x', [(k, 3 - k) for k in range(4)])  4.67 us
    ppermute x2, waiting for transfers between devices, shards(): from_left = lax.ppermute(right, 'y', to_right)  4.2 us
  transfers between devices with their start and end apart: 11, of which 7 were waited for; matrix products, arithmetic and copies ran while one was open for 0% of the time, Pallas kernels for 3%

profile of v8, /device:TPU:24, one launch (start us, length us, event | category | flops | bytes accessed | tf_op | source)
XLA Modules:
  0.0 130.7 jit_solution(18428642642137659062)
XLA Ops:
  0.0 0.0 copy-start.1
  0.0 0.0 copy-start.2
  0.0 2.9 %shard_map.64 = f32[264,256]{1,0:T(8,128)} custom-call(bf16[4,512,512]{2,1,0:T(8,128)(2,1)} %inv_ref.7, f32[3,8,256]{2,1,0:T(8,128)} %stiff_ref.9, f32[3,8,256]{2,1,0:T(8,128)} %u_ref.3), custom_call_target="tpu_custom_call" | custom-call | flops 100000000 | bytes 1000000 | tf_op jit(solution)/shard_map/pallas_call | solution.py:70
  2.9 0.0 copy-start
  2.9 0.0 copy-start.3
  2.9 0.0 copy-start.4
  2.9 0.0 copy-start.5
  3.0 2.5 %all-gather = f32[528,256]{1,0:T(8,128)S(1)} all-gather(f32[264,256]{1,0:T(8,128)} %shard_map.64), channel_id=2, replica_groups=mesh['zh'=4,'zl'=4,'x'=4,'c'=2,'y'=4] {'c'}, dimensions={0}, use_global_device_ids=true | all-gather | bytes 811008 | tf_op jit(solution)/shard_map/all_gather | solution.py:561
  5.5 0.3 shard_map.65
  5.8 3.4 %collective-permute-start = (f32[256,256]{1,0:T(8,128)S(1)}, f32[256,256]{1,0:T(8,128)S(1)}, u32[]{:S(2)}, u32[]{:S(2)}) collective-permute-start(f32[256,256]{1,0:T(8,128)S(1)} %get-tuple-element.37.after_ref.own_ref), channel_id=1, source_target_pairs={{0,8},{8,0},{16,24},{24,16},{1,9},{9,1},{17,25},{25,17},{2,10},{10... | collective-permute-start | bytes 786440 | tf_op jit(solution)/shard_map/ppermute | solution.py:564
  9.2 0.0 copy-done.1
  9.2 0.0 copy-done.2
  9.2 0.1 shard_map.66
  9.3 2.6 %collective-permute-start.1 = (f32[8,128]{1,0:T(8,128)S(1)}, f32[8,128]{1,0:T(8,128)S(1)}, u32[]{:S(2)}, u32[]{:S(2)}) collective-permute-start(f32[8,128]{1,0:T(8,128)S(1)} %get-tuple-element.39), channel_id=1, source_target_pairs={{1,0},{2,1},{3,2},{5,4},{6,5},{7,6},{9,8},{10,9},{11,10},{13,12},{... | collective-permute-start | bytes 12296 | tf_op jit(solution)/shard_map/ppermute | solution.py:574
  11.9 1.3 %collective-permute-done.1.after_ref.right_ref = f32[8,128]{1,0:T(8,128)S(1)} collective-permute-done((f32[8,128]{1,0:T(8,128)S(1)}, f32[8,128]{1,0:T(8,128)S(1)}, u32[]{:S(2)}, u32[]{:S(2)}) %collective-permute-start.1) | collective-permute-done | bytes 4128 | tf_op jit(solution)/shard_map/ppermute | solution.py:574
  13.2 2.8 %collective-permute-done.other_ref.sib_ref = f32[256,256]{1,0:T(8,128)S(1)} collective-permute-done((f32[256,256]{1,0:T(8,128)S(1)}, f32[256,256]{1,0:T(8,128)S(1)}, u32[]{:S(2)}, u32[]{:S(2)}) %collective-permute-start) | collective-permute-done | bytes 262176 | tf_op jit(solution)/shard_map/ppermute | solution.py:564
  16.0 0.3 shard_map.67
  16.3 4.7 %collective-permute-start.2 = (f32[256,256]{1,0:T(8,128)S(1)}, f32[256,256]{1,0:T(8,128)S(1)}, u32[]{:S(2)}, u32[]{:S(2)}) collective-permute-start(f32[256,256]{1,0:T(8,128)S(1)} %get-tuple-element.40.own_ref.two_ref), channel_id=1, source_target_pairs={{0,24},{8,16},{16,8},{24,0},{1,25},{9,17},{17,9},{25,1},{2,26},{10... | collective-permute-start | bytes 786440 | tf_op jit(solution)/shard_map/ppermute | solution.py:581
  21.0 0.7 collective-permute-start.3
  21.7 0.0 collective-permute-done.3.after_ref.cross_ref
  21.7 5.3 %collective-permute-done.2.other_ref.far_ref = f32[256,256]{1,0:T(8,128)S(1)} collective-permute-done((f32[256,256]{1,0:T(8,128)S(1)}, f32[256,256]{1,0:T(8,128)S(1)}, u32[]{:S(2)}, u32[]{:S(2)}) %collective-permute-start.2) | collective-permute-done | bytes 262176 | tf_op jit(solution)/shard_map/ppermute | solution.py:581
  26.9 0.3 shard_map.68
  27.2 4.9 %collective-permute-start.5 = (f32[256,256]{1,0:T(8,128)S(1)}, f32[256,256]{1,0:T(8,128)S(1)}, u32[]{:S(2)}, u32[]{:S(2)}) collective-permute-start(f32[256,256]{1,0:T(8,128)S(1)} %get-tuple-element.45.own_ref), channel_id=1, source_target_pairs={{0,32},{32,0},{64,96},{96,64},{128,160},{160,128},{192,224},{224,1... | collective-permute-start | bytes 786440 | tf_op jit(solution)/shard_map/ppermute | solution.py:590
  32.2 1.3 collective-permute-start.4
  33.5 4.2 %collective-permute-done.4.rest_0_.left_ref = f32[8,128]{1,0:T(8,128)S(1)} collective-permute-done((f32[8,128]{1,0:T(8,128)S(1)}, f32[8,128]{1,0:T(8,128)S(1)}, u32[]{:S(2)}, u32[]{:S(2)}) %collective-permute-start.4) | collective-permute-done | bytes 4128 | tf_op jit(solution)/shard_map/ppermute | solution.py:592
  37.7 0.0 collective-permute-done.5.other_ref.one_ref
  37.7 0.3 shard_map.69
  38.0 5.2 %collective-permute-start.6 = (f32[256,128]{1,0:T(8,128)S(1)}, f32[256,128]{1,0:T(8,128)S(1)}, u32[]{:S(2)}, u32[]{:S(2)}) collective-permute-start(f32[256,128]{1,0:T(8,128)S(1)} %get-tuple-element.52), channel_id=1, source_target_pairs={{0,64},{32,96},{64,0},{96,32},{128,192},{160,224},{192,128},{224,1... | collective-permute-start | bytes 393224 | tf_op jit(solution)/shard_map/ppermute | solution.py:597
  43.2 0.0 copy-done
  43.2 0.0 copy-done.3
  43.2 0.0 copy-done.4
  43.2 0.0 copy-done.5
  43.2 1.9 %shard_map.70 = (f32[3,8,256]{2,1,0:T(8,128)S(1)}, f32[8,256]{1,0:T(8,128)S(1)}, f32[3,8,256]{2,1,0:T(8,128)S(1)}, f32[2,8,512]{2,1,0:T(8,128)S(1)}, f32[8,256]{1,0:T(8,128)S(1)}) custom-call(f32[3,8,256]{2,1,0:T(8,128)S(1)} %copy-done.2, f32[3,8,256]{2,1,0:T(8,128)S(1)} %copy-done.3, f32[8,256]{1,0:T(8,128)S(1)} %copy-done.4, f32[3,8,256]{2,1,0:T(8,128)S(1)} %copy-done.1, ...), custom_call_target="tpu_custom_call" | custom-call | flops 100000000 | bytes 3000000 | tf_op jit(solution)/shard_map/pallas_call | solution.py:70
  45.1 1.3 shard_map.71
  46.4 1.1 collective-permute-done.6.half_ref.two_ref
  47.5 0.3 shard_map.74
  47.8 1.3 collective-permute-start.7
  49.1 0.2 shard_map.72
  49.3 11.4 %all_to_all.20.got_ref = f32[8,3,256]{2,1,0:T(4,128)S(1)} all-to-all(f32[8,3,256]{2,1,0:T(4,128)S(1)} %shard_map.72), channel_id=1, replica_groups=mesh['zh'=4,'zl'=4,'x'=4,'c'=2,'y'=4] {'x','c'}, dimensions={0} | all-to-all | bytes 49152 | tf_op jit(solution)/shard_map/all_to_all | solution.py:539
  60.7 0.4 shard_map.73.after_ref.both_ref
  61.1 2.3 %collective-permute-done.7.far_ref = f32[256,128]{1,0:T(8,128)S(1)} collective-permute-done((f32[256,128]{1,0:T(8,128)S(1)}, f32[256,128]{1,0:T(8,128)S(1)}, u32[]{:S(2)}, u32[]{:S(2)}) %collective-permute-start.7) | collective-permute-done | bytes 131104 | tf_op jit(solution)/shard_map/ppermute | solution.py:623
  63.4 2.2 %all-gather.1 = f32[4,256,128]{2,1,0:T(8,128)S(1)} all-gather(f32[2,256,128]{2,1,0:T(8,128)S(1)} %shard_map.75), channel_id=3, replica_groups=mesh['zh'=4,'zl'=4,'x'=4,'c'=2,'y'=4] {'c'}, dimensions={0}, use_global_device_ids=true | all-gather | bytes 786432 | tf_op jit(solution)/shard_map/all_gather | solution.py:637
  65.6 1.0 shard_map.76
  66.5 25.0 %all_to_all.21.got_ref = f32[16,3,256]{2,1,0:T(4,128)S(1)} all-to-all(f32[16,3,256]{2,1,0:T(4,128)S(1)} %get-tuple-element.53), channel_id=1, replica_groups=mesh['zh'=4,'zl'=4,'x'=4,'c'=2,'y'=4] {'zh','zl'}, dimensions={0} | all-to-all | bytes 98304 | tf_op jit(solution)/shard_map/all_to_all | solution.py:539
  91.5 1.0 shard_map.77
  92.5 1.3 collective-permute-start.8
  93.8 1.3 collective-permute-start.9
  95.1 4.5 %collective-permute-start.10 = (f32[8,128]{1,0:T(8,128)S(1)}, f32[8,128]{1,0:T(8,128)S(1)}, u32[]{:S(2)}, u32[]{:S(2)}) collective-permute-start(f32[8,128]{1,0:T(8,128)S(1)} %get-tuple-element.61), channel_id=1, source_target_pairs={{1,0},{2,1},{3,2},{5,4},{6,5},{7,6},{9,8},{10,9},{11,10},{13,12},{... | collective-permute-start | bytes 12296 | tf_op jit(solution)/shard_map/ppermute | solution.py:654
  99.7 0.0 collective-permute-done.8.row_ref
  99.7 0.0 collective-permute-done.9.left_ref
  99.7 1.3 collective-permute-done.10.right_ref
  101.0 1.5 %shard_map.78 = (f32[3,8,256]{2,1,0:T(8,128)S(1)}, f32[8,3,256]{2,1,0:T(4,128)S(1)}) custom-call(f32[4,8,256]{2,1,0:T(8,128)S(1)} %get-tuple-element.58.u_ref, f32[3,8,256]{2,1,0:T(8,128)S(1)} %copy-done.1, f32[4,256]{1,0:T(4,128)S(1)} %collective-permute-done.8.row_ref, f32[8,128]{1,0:T(8,128)S(1)} %collective-permute-done.9.left_ref, ...), custom_call_target="tpu_custom_call" | custom-call | flops 100000000 | bytes 3000000 | tf_op jit(solution)/shard_map/pallas_call | solution.py:70
  102.5 9.0 %all_to_all.22.got_ref = f32[8,3,256]{2,1,0:T(4,128)S(1)} all-to-all(f32[8,3,256]{2,1,0:T(4,128)S(1)} %get-tuple-element.65), channel_id=1, replica_groups=mesh['zh'=4,'zl'=4,'x'=4,'c'=2,'y'=4] {'x','c'}, dimensions={0} | all-to-all | bytes 49152 | tf_op jit(solution)/shard_map/all_to_all | solution.py:539
  111.5 0.6 shard_map.79
  112.1 17.0 %all_to_all.23.got_ref = f32[16,3,256]{2,1,0:T(4,128)S(1)} all-to-all(f32[16,3,256]{2,1,0:T(4,128)S(1)} %get-tuple-element.66), channel_id=1, replica_groups=mesh['zh'=4,'zl'=4,'x'=4,'c'=2,'y'=4] {'zh','zl'}, dimensions={0} | all-to-all | bytes 98304 | tf_op jit(solution)/shard_map/all_to_all | solution.py:539
  129.1 1.6 %shard_map.80 = f32[3,8,256]{2,1,0:T(8,128)} custom-call(f32[16,3,256]{2,1,0:T(4,128)S(1)} %all_to_all.23.got_ref, f32[8,512]{1,0:T(8,128)S(1)} %get-tuple-element.67.both_ref, bf16[8,256,256]{2,1,0:T(8,128)(2,1)S(1)} %get-tuple-element.54.maps_ref, bf16[2,256,256]{2,1,0:T(8,128)(2,1)S(1)} %get-tuple-element.55.joint_ref, ...), custom_call_target="tpu_custom_call" | custom-call | flops 100000000 | bytes 1000000 | tf_op jit(solution)/shard_map/pallas_call | solution.py:70
  (1 shorter events, 0.0 us)
Async XLA Ops:
  0.0 9.2 %copy-start.1 = (f32[3,8,256]{2,1,0:T(8,128)S(1)}, f32[3,8,256]{2,1,0:T(8,128)}, u32[]{:S(2)}) copy-start(f32[3,8,256]{2,1,0:T(8,128)} %stiff_ref.9) | copy-start | bytes 73732
  0.0 9.2 %copy-start.2 = (f32[3,8,256]{2,1,0:T(8,128)S(1)}, f32[3,8,256]{2,1,0:T(8,128)}, u32[]{:S(2)}) copy-start(f32[3,8,256]{2,1,0:T(8,128)} %u_ref.3) | copy-start | bytes 73732
  2.9 40.2 %copy-start = (bf16[4,512,512]{2,1,0:T(8,128)(2,1)S(1)}, bf16[4,512,512]{2,1,0:T(8,128)(2,1)}, u32[]{:S(2)}) copy-start(bf16[4,512,512]{2,1,0:T(8,128)(2,1)} %inv_ref.7) | copy-start | bytes 6291460
  2.9 40.2 %copy-start.3 = (f32[3,8,256]{2,1,0:T(8,128)S(1)}, f32[3,8,256]{2,1,0:T(8,128)}, u32[]{:S(2)}) copy-start(f32[3,8,256]{2,1,0:T(8,128)} %target_ref.1) | copy-start | bytes 73732
  2.9 40.2 %copy-start.4 = (f32[8,256]{1,0:T(8,128)S(1)}, f32[8,256]{1,0:T(8,128)}, u32[]{:S(2)}) copy-start(f32[8,256]{1,0:T(8,128)} %inertia_ref.1) | copy-start | bytes 24580
  2.9 40.2 %copy-start.5 = (s32[64]{0:T(128)S(1)}, s32[64]{0:T(128)}, u32[]{:S(2)}) copy-start(s32[64]{0:T(128)} %pin_ref.1) | copy-start | bytes 772
  5.8 10.2 %collective-permute-start = (f32[256,256]{1,0:T(8,128)S(1)}, f32[256,256]{1,0:T(8,128)S(1)}, u32[]{:S(2)}, u32[]{:S(2)}) collective-permute-start(f32[256,256]{1,0:T(8,128)S(1)} %get-tuple-element.37.after_ref.own_ref), channel_id=1, source_target_pairs={{0,8},{8,0},{16,24},{24,16},{1,9},{9,1},{17,25},{25,17},{2,10},{10... | collective-permute-start | bytes 786440 | tf_op jit(solution)/shard_map/ppermute | solution.py:564
  9.3 4.0 %collective-permute-start.1 = (f32[8,128]{1,0:T(8,128)S(1)}, f32[8,128]{1,0:T(8,128)S(1)}, u32[]{:S(2)}, u32[]{:S(2)}) collective-permute-start(f32[8,128]{1,0:T(8,128)S(1)} %get-tuple-element.39), channel_id=1, source_target_pairs={{1,0},{2,1},{3,2},{5,4},{6,5},{7,6},{9,8},{10,9},{11,10},{13,12},{... | collective-permute-start | bytes 12296 | tf_op jit(solution)/shard_map/ppermute | solution.py:574
  16.3 10.6 %collective-permute-start.2 = (f32[256,256]{1,0:T(8,128)S(1)}, f32[256,256]{1,0:T(8,128)S(1)}, u32[]{:S(2)}, u32[]{:S(2)}) collective-permute-start(f32[256,256]{1,0:T(8,128)S(1)} %get-tuple-element.40.own_ref.two_ref), channel_id=1, source_target_pairs={{0,24},{8,16},{16,8},{24,0},{1,25},{9,17},{17,9},{25,1},{2,26},{10... | collective-permute-start | bytes 786440 | tf_op jit(solution)/shard_map/ppermute | solution.py:581
  21.0 0.7 collective-permute-start.3
  27.2 10.4 %collective-permute-start.5 = (f32[256,256]{1,0:T(8,128)S(1)}, f32[256,256]{1,0:T(8,128)S(1)}, u32[]{:S(2)}, u32[]{:S(2)}) collective-permute-start(f32[256,256]{1,0:T(8,128)S(1)} %get-tuple-element.45.own_ref), channel_id=1, source_target_pairs={{0,32},{32,0},{64,96},{96,64},{128,160},{160,128},{192,224},{224,1... | collective-permute-start | bytes 786440 | tf_op jit(solution)/shard_map/ppermute | solution.py:590
  32.2 5.5 %collective-permute-start.4 = (f32[8,128]{1,0:T(8,128)S(1)}, f32[8,128]{1,0:T(8,128)S(1)}, u32[]{:S(2)}, u32[]{:S(2)}) collective-permute-start(f32[8,128]{1,0:T(8,128)S(1)} %get-tuple-element.43), channel_id=1, source_target_pairs={{0,1},{1,2},{2,3},{4,5},{5,6},{6,7},{8,9},{9,10},{10,11},{12,13},{... | collective-permute-start | bytes 12296 | tf_op jit(solution)/shard_map/ppermute | solution.py:592
  38.0 9.5 %collective-permute-start.6 = (f32[256,128]{1,0:T(8,128)S(1)}, f32[256,128]{1,0:T(8,128)S(1)}, u32[]{:S(2)}, u32[]{:S(2)}) collective-permute-start(f32[256,128]{1,0:T(8,128)S(1)} %get-tuple-element.52), channel_id=1, source_target_pairs={{0,64},{32,96},{64,0},{96,32},{128,192},{160,224},{192,128},{224,1... | collective-permute-start | bytes 393224 | tf_op jit(solution)/shard_map/ppermute | solution.py:597
  47.8 15.5 %collective-permute-start.7 = (f32[256,128]{1,0:T(8,128)S(1)}, f32[256,128]{1,0:T(8,128)S(1)}, u32[]{:S(2)}, u32[]{:S(2)}) collective-permute-start(f32[256,128]{1,0:T(8,128)S(1)} %shard_map.74), channel_id=1, source_target_pairs={{128,0},{160,32},{192,64},{224,96},{256,384},{288,416},{320,448},{... | collective-permute-start | bytes 393224 | tf_op jit(solution)/shard_map/ppermute | solution.py:623
  92.5 7.2 %collective-permute-start.8 = (f32[4,256]{1,0:T(4,128)S(1)}, f32[4,256]{1,0:T(4,128)S(1)}, u32[]{:S(2)}, u32[]{:S(2)}) collective-permute-start(f32[4,256]{1,0:T(4,128)S(1)} %get-tuple-element.59), channel_id=1, source_target_pairs={{4,0},{8,4},{12,8},{16,12},{20,16},{24,20},{28,24},{32,28},{36,32}... | collective-permute-start | bytes 12296 | tf_op jit(solution)/shard_map/ppermute | solution.py:653
  93.8 5.9 %collective-permute-start.9 = (f32[8,128]{1,0:T(8,128)S(1)}, f32[8,128]{1,0:T(8,128)S(1)}, u32[]{:S(2)}, u32[]{:S(2)}) collective-permute-start(f32[8,128]{1,0:T(8,128)S(1)} %get-tuple-element.60), channel_id=1, source_target_pairs={{0,1},{1,2},{2,3},{4,5},{5,6},{6,7},{8,9},{9,10},{10,11},{12,13},{... | collective-permute-start | bytes 12296 | tf_op jit(solution)/shard_map/ppermute | solution.py:655
  95.1 5.9 %collective-permute-start.10 = (f32[8,128]{1,0:T(8,128)S(1)}, f32[8,128]{1,0:T(8,128)S(1)}, u32[]{:S(2)}, u32[]{:S(2)}) collective-permute-start(f32[8,128]{1,0:T(8,128)S(1)} %get-tuple-element.61), channel_id=1, source_target_pairs={{1,0},{2,1},{3,2},{5,4},{6,5},{7,6},{9,8},{10,9},{11,10},{13,12},{... | collective-permute-start | bytes 12296 | tf_op jit(solution)/shard_map/ppermute | solution.py:654

commit v9 on v7

--- a/solution.py
+++ b/solution.py
@@ -510,7 +510,7 @@
 
 def middle_kernel(
     got_ref, both_ref, maps_ref, joint_ref, eh_ref, el_ref, stiff_ref, base_ref, inv_ref,
-    u_ref, left_ref, right_ref, row_ref, vec_ref,
+    u_ref, row_ref, vec_ref,
 ):
     state, came = finish(
         got_ref, both_ref, maps_ref, joint_ref, eh_ref, el_ref, stiff_ref, base_ref, inv_ref, vec_ref
@@ -518,10 +518,13 @@
     for k in range(3):
         u_ref[k] = state[k]
     u_ref[3] = came
-    left, right = edge_tiles(state, [])
+    row_ref[...] = jnp.concatenate([state[0][0:1], state[1][0:1], state[2][0:1], state[0][0:1]], axis=0)
+
+
+def edges_kernel(u_ref, left_ref, right_ref):
+    left, right = edge_tiles([u_ref[k] for k in range(3)], [])
     left_ref[...] = left
     right_ref[...] = right
-    row_ref[...] = jnp.concatenate([state[0][0:1], state[1][0:1], state[2][0:1], state[0][0:1]], axis=0)
 
 
 def final_kernel(
@@ -642,15 +645,16 @@
         flops=5 * 10**8,
     )
     got = swap(msg, ZAX)
-    middle, left, right, low_row = call(
+    middle, low_row = call(
         middle_kernel,
-        [sds((4, 8, CB)), tile, tile, rows],
+        [sds((4, 8, CB)), rows],
         (got, both, maps, joint, eh, el, stiffness, base, inverses),
         scratch=[pltpu.VMEM((16, 3 * CB), F32)],
         flops=10**8,
     )
 
     low_row = lax.ppermute(low_row, STRIP, [(k + 1, k) for k in range(127)])
+    left, right = call(edges_kernel, [tile, tile], (middle,))
     from_right = lax.ppermute(left, "y", to_left)
     from_left = lax.ppermute(right, "y", to_right)
     base, msg = call(

time: 133 us -> 133 us (level)
    pallas_call x17 -> x18, Pallas kernels: 13.8 us -> 13.8 us  [call(): pl.pallas_call(kernel, out_shape=outs, in_specs=in_specs, out_specs=out_s...]
where the time goes in v9:
time: 133 us; the launch traced here: 132 us
  blocking collectives  68.1 us (51%)
  starting transfers between devices  31.2 us (23%)
  waiting for transfers between devices  18.6 us (14%)
  Pallas kernels  13.8 us (10%)
    all_to_all x4, blocking collectives, swap(): return lax.all_to_all(value, axes, 0, 0)  63.4 us
    pallas_call x18, Pallas kernels, call(): pl.pallas_call(kernel, out_shape=outs, in_specs=in_specs, out_specs=out_s...  13.8 us
    ppermute x2, starting transfers between devices, shards(): from_right = lax.ppermute(left, 'y', to_left)  7.18 us
    ppermute x1, waiting for transfers between devices, shards(): far_chips = lax.ppermute(two_chips, 'x', [(k, 3 - k) for k in range(4)])  5.27 us
    ppermute x1, starting transfers between devices, shards(): two_mine = lax.ppermute(two_half, ZAX, [(k, k ^ 2) for k in range(16)])  5.17 us
    ppermute x1, starting transfers between devices, shards(): beside = lax.ppermute(plane, ZAX, [(k, k ^ 1) for k in range(16)])  4.92 us
    ppermute x1, starting transfers between devices, shards(): far_chips = lax.ppermute(two_chips, 'x', [(k, 3 - k) for k in range(4)])  4.67 us
    ppermute x2, waiting for transfers between devices, shards(): from_left = lax.ppermute(right, 'y', to_right)  4.2 us
  transfers between devices with their start and end apart: 11, of which 7 were waited for; matrix products, arithmetic and copies ran while one was open for 0% of the time, Pallas kernels for 3%

profile of v9, /device:TPU:24, one launch (start us, length us, event | category | flops | bytes accessed | tf_op | source)
XLA Modules:
  0.0 132.1 jit_solution(17555047376246960107)
XLA Ops:
  0.0 0.0 copy-start.1
  0.0 0.0 copy-start.2
  0.0 2.9 %shard_map.64 = f32[264,256]{1,0:T(8,128)} custom-call(bf16[4,512,512]{2,1,0:T(8,128)(2,1)} %inv_ref.7, f32[3,8,256]{2,1,0:T(8,128)} %stiff_ref.9, f32[3,8,256]{2,1,0:T(8,128)} %u_ref.3), custom_call_target="tpu_custom_call" | custom-call | flops 100000000 | bytes 1000000 | tf_op jit(solution)/shard_map/pallas_call | solution.py:70
  2.9 0.0 copy-start
  2.9 0.0 copy-start.3
  2.9 0.0 copy-start.4
  3.0 0.0 copy-start.5
  3.0 2.5 %all-gather = f32[528,256]{1,0:T(8,128)S(1)} all-gather(f32[264,256]{1,0:T(8,128)} %shard_map.64), channel_id=2, replica_groups=mesh['zh'=4,'zl'=4,'x'=4,'c'=2,'y'=4] {'c'}, dimensions={0}, use_global_device_ids=true | all-gather | bytes 811008 | tf_op jit(solution)/shard_map/all_gather | solution.py:564
  5.5 0.3 shard_map.65
  5.8 3.4 %collective-permute-start = (f32[256,256]{1,0:T(8,128)S(1)}, f32[256,256]{1,0:T(8,128)S(1)}, u32[]{:S(2)}, u32[]{:S(2)}) collective-permute-start(f32[256,256]{1,0:T(8,128)S(1)} %get-tuple-element.37.after_ref.own_ref), channel_id=1, source_target_pairs={{0,8},{8,0},{16,24},{24,16},{1,9},{9,1},{17,25},{25,17},{2,10},{10... | collective-permute-start | bytes 786440 | tf_op jit(solution)/shard_map/ppermute | solution.py:567
  9.2 0.0 copy-done.1
  9.2 0.0 copy-done.2
  9.2 0.1 shard_map.66
  9.3 2.6 %collective-permute-start.1 = (f32[8,128]{1,0:T(8,128)S(1)}, f32[8,128]{1,0:T(8,128)S(1)}, u32[]{:S(2)}, u32[]{:S(2)}) collective-permute-start(f32[8,128]{1,0:T(8,128)S(1)} %get-tuple-element.39), channel_id=1, source_target_pairs={{1,0},{2,1},{3,2},{5,4},{6,5},{7,6},{9,8},{10,9},{11,10},{13,12},{... | collective-permute-start | bytes 12296 | tf_op jit(solution)/shard_map/ppermute | solution.py:577
  11.9 1.3 collective-permute-done.1.after_ref.right_ref
  13.2 2.8 %collective-permute-done.other_ref.sib_ref = f32[256,256]{1,0:T(8,128)S(1)} collective-permute-done((f32[256,256]{1,0:T(8,128)S(1)}, f32[256,256]{1,0:T(8,128)S(1)}, u32[]{:S(2)}, u32[]{:S(2)}) %collective-permute-start) | collective-permute-done | bytes 262176 | tf_op jit(solution)/shard_map/ppermute | solution.py:567
  16.0 0.3 shard_map.67
  16.3 4.7 %collective-permute-start.2 = (f32[256,256]{1,0:T(8,128)S(1)}, f32[256,256]{1,0:T(8,128)S(1)}, u32[]{:S(2)}, u32[]{:S(2)}) collective-permute-start(f32[256,256]{1,0:T(8,128)S(1)} %get-tuple-element.40.own_ref.two_ref), channel_id=1, source_target_pairs={{0,24},{8,16},{16,8},{24,0},{1,25},{9,17},{17,9},{25,1},{2,26},{10... | collective-permute-start | bytes 786440 | tf_op jit(solution)/shard_map/ppermute | solution.py:584
  21.0 0.7 collective-permute-start.3
  21.7 0.0 collective-permute-done.3.after_ref.cross_ref
  21.7 5.3 %collective-permute-done.2.other_ref.far_ref = f32[256,256]{1,0:T(8,128)S(1)} collective-permute-done((f32[256,256]{1,0:T(8,128)S(1)}, f32[256,256]{1,0:T(8,128)S(1)}, u32[]{:S(2)}, u32[]{:S(2)}) %collective-permute-start.2) | collective-permute-done | bytes 262176 | tf_op jit(solution)/shard_map/ppermute | solution.py:584
  26.9 0.3 shard_map.68
  27.2 4.9 %collective-permute-start.5 = (f32[256,256]{1,0:T(8,128)S(1)}, f32[256,256]{1,0:T(8,128)S(1)}, u32[]{:S(2)}, u32[]{:S(2)}) collective-permute-start(f32[256,256]{1,0:T(8,128)S(1)} %get-tuple-element.45.own_ref), channel_id=1, source_target_pairs={{0,32},{32,0},{64,96},{96,64},{128,160},{160,128},{192,224},{224,1... | collective-permute-start | bytes 786440 | tf_op jit(solution)/shard_map/ppermute | solution.py:593
  32.2 1.3 collective-permute-start.4
  33.5 4.2 %collective-permute-done.4.rest_0_.left_ref = f32[8,128]{1,0:T(8,128)S(1)} collective-permute-done((f32[8,128]{1,0:T(8,128)S(1)}, f32[8,128]{1,0:T(8,128)S(1)}, u32[]{:S(2)}, u32[]{:S(2)}) %collective-permute-start.4) | collective-permute-done | bytes 4128 | tf_op jit(solution)/shard_map/ppermute | solution.py:595
  37.7 0.0 collective-permute-done.5.other_ref.one_ref
  37.7 0.3 shard_map.69
  38.0 5.2 %collective-permute-start.6 = (f32[256,128]{1,0:T(8,128)S(1)}, f32[256,128]{1,0:T(8,128)S(1)}, u32[]{:S(2)}, u32[]{:S(2)}) collective-permute-start(f32[256,128]{1,0:T(8,128)S(1)} %get-tuple-element.52), channel_id=1, source_target_pairs={{0,64},{32,96},{64,0},{96,32},{128,192},{160,224},{192,128},{224,1... | collective-permute-start | bytes 393224 | tf_op jit(solution)/shard_map/ppermute | solution.py:600
  43.2 0.0 copy-done
  43.2 0.0 copy-done.3
  43.2 0.0 copy-done.4
  43.2 0.0 copy-done.5
  43.2 1.9 %shard_map.70 = (f32[3,8,256]{2,1,0:T(8,128)S(1)}, f32[8,256]{1,0:T(8,128)S(1)}, f32[3,8,256]{2,1,0:T(8,128)S(1)}, f32[2,8,512]{2,1,0:T(8,128)S(1)}, f32[8,256]{1,0:T(8,128)S(1)}) custom-call(f32[3,8,256]{2,1,0:T(8,128)S(1)} %copy-done.2, f32[3,8,256]{2,1,0:T(8,128)S(1)} %copy-done.3, f32[8,256]{1,0:T(8,128)S(1)} %copy-done.4, f32[3,8,256]{2,1,0:T(8,128)S(1)} %copy-done.1, ...), custom_call_target="tpu_custom_call" | custom-call | flops 100000000 | bytes 3000000 | tf_op jit(solution)/shard_map/pallas_call | solution.py:70
  45.1 1.3 shard_map.71
  46.4 1.1 collective-permute-done.6.half_ref.two_ref
  47.5 0.3 shard_map.74
  47.8 1.3 collective-permute-start.7
  49.1 0.2 shard_map.72
  49.3 11.4 %all_to_all.20.got_ref = f32[8,3,256]{2,1,0:T(4,128)S(1)} all-to-all(f32[8,3,256]{2,1,0:T(4,128)S(1)} %shard_map.72), channel_id=1, replica_groups=mesh['zh'=4,'zl'=4,'x'=4,'c'=2,'y'=4] {'x','c'}, dimensions={0} | all-to-all | bytes 49152 | tf_op jit(solution)/shard_map/all_to_all | solution.py:542
  60.7 0.4 shard_map.73.after_ref.both_ref
  61.1 2.3 %collective-permute-done.7.far_ref = f32[256,128]{1,0:T(8,128)S(1)} collective-permute-done((f32[256,128]{1,0:T(8,128)S(1)}, f32[256,128]{1,0:T(8,128)S(1)}, u32[]{:S(2)}, u32[]{:S(2)}) %collective-permute-start.7) | collective-permute-done | bytes 131104 | tf_op jit(solution)/shard_map/ppermute | solution.py:626
  63.4 2.2 %all-gather.1 = f32[4,256,128]{2,1,0:T(8,128)S(1)} all-gather(f32[2,256,128]{2,1,0:T(8,128)S(1)} %shard_map.75), channel_id=3, replica_groups=mesh['zh'=4,'zl'=4,'x'=4,'c'=2,'y'=4] {'c'}, dimensions={0}, use_global_device_ids=true | all-gather | bytes 786432 | tf_op jit(solution)/shard_map/all_gather | solution.py:640
  65.6 1.0 shard_map.76
  66.5 25.0 %all_to_all.21.got_ref = f32[16,3,256]{2,1,0:T(4,128)S(1)} all-to-all(f32[16,3,256]{2,1,0:T(4,128)S(1)} %get-tuple-element.53), channel_id=1, replica_groups=mesh['zh'=4,'zl'=4,'x'=4,'c'=2,'y'=4] {'zh','zl'}, dimensions={0} | all-to-all | bytes 98304 | tf_op jit(solution)/shard_map/all_to_all | solution.py:542
  91.5 1.0 shard_map.77
  92.4 0.1 shard_map.78
  92.5 1.3 collective-permute-start.8
  93.8 4.5 %collective-permute-start.9 = (f32[8,128]{1,0:T(8,128)S(1)}, f32[8,128]{1,0:T(8,128)S(1)}, u32[]{:S(2)}, u32[]{:S(2)}) collective-permute-start(f32[8,128]{1,0:T(8,128)S(1)} %get-tuple-element.60), channel_id=1, source_target_pairs={{1,0},{2,1},{3,2},{5,4},{6,5},{7,6},{9,8},{10,9},{11,10},{13,12},{... | collective-permute-start | bytes 12296 | tf_op jit(solution)/shard_map/ppermute | solution.py:658
  98.4 1.3 collective-permute-start.10
  99.7 0.0 collective-permute-done.8.left_ref
  99.7 0.0 collective-permute-done.9.right_ref
  99.7 1.7 %collective-permute-done.10.row_ref = f32[4,256]{1,0:T(4,128)S(1)} collective-permute-done((f32[4,256]{1,0:T(4,128)S(1)}, f32[4,256]{1,0:T(4,128)S(1)}, u32[]{:S(2)}, u32[]{:S(2)}) %collective-permute-start.10) | collective-permute-done | bytes 4128 | tf_op jit(solution)/shard_map/ppermute | solution.py:656
  101.4 1.5 %shard_map.79 = (f32[3,8,256]{2,1,0:T(8,128)S(1)}, f32[8,3,256]{2,1,0:T(4,128)S(1)}) custom-call(f32[4,8,256]{2,1,0:T(8,128)S(1)} %get-tuple-element.58.u_ref, f32[3,8,256]{2,1,0:T(8,128)S(1)} %copy-done.1, f32[8,128]{1,0:T(8,128)S(1)} %collective-permute-done.8.left_ref, f32[8,128]{1,0:T(8,128)S(1)} %collective-permute-done.9.right_ref, ...), custom_call_target="tpu_custom_call" | custom-call | flops 100000000 | bytes 3000000 | tf_op jit(solution)/shard_map/pallas_call | solution.py:70
  102.9 10.1 %all_to_all.22.got_ref = f32[8,3,256]{2,1,0:T(4,128)S(1)} all-to-all(f32[8,3,256]{2,1,0:T(4,128)S(1)} %get-tuple-element.65), channel_id=1, replica_groups=mesh['zh'=4,'zl'=4,'x'=4,'c'=2,'y'=4] {'x','c'}, dimensions={0} | all-to-all | bytes 49152 | tf_op jit(solution)/shard_map/all_to_all | solution.py:542
  113.0 0.6 shard_map.80
  113.6 16.9 %all_to_all.23.got_ref = f32[16,3,256]{2,1,0:T(4,128)S(1)} all-to-all(f32[16,3,256]{2,1,0:T(4,128)S(1)} %get-tuple-element.66), channel_id=1, replica_groups=mesh['zh'=4,'zl'=4,'x'=4,'c'=2,'y'=4] {'zh','zl'}, dimensions={0} | all-to-all | bytes 98304 | tf_op jit(solution)/shard_map/all_to_all | solution.py:542
  130.5 1.6 %shard_map.81 = f32[3,8,256]{2,1,0:T(8,128)} custom-call(f32[16,3,256]{2,1,0:T(4,128)S(1)} %all_to_all.23.got_ref, f32[8,512]{1,0:T(8,128)S(1)} %get-tuple-element.67.both_ref, bf16[8,256,256]{2,1,0:T(8,128)(2,1)S(1)} %get-tuple-element.54.maps_ref, bf16[2,256,256]{2,1,0:T(8,128)(2,1)S(1)} %get-tuple-element.55.joint_ref, ...), custom_call_target="tpu_custom_call" | custom-call | flops 100000000 | bytes 1000000 | tf_op jit(solution)/shard_map/pallas_call | solution.py:70
  (1 shorter events, 0.0 us)
Async XLA Ops:
  0.0 9.2 %copy-start.1 = (f32[3,8,256]{2,1,0:T(8,128)S(1)}, f32[3,8,256]{2,1,0:T(8,128)}, u32[]{:S(2)}) copy-start(f32[3,8,256]{2,1,0:T(8,128)} %stiff_ref.9) | copy-start | bytes 73732
  0.0 9.2 %copy-start.2 = (f32[3,8,256]{2,1,0:T(8,128)S(1)}, f32[3,8,256]{2,1,0:T(8,128)}, u32[]{:S(2)}) copy-start(f32[3,8,256]{2,1,0:T(8,128)} %u_ref.3) | copy-start | bytes 73732
  2.9 40.2 %copy-start = (bf16[4,512,512]{2,1,0:T(8,128)(2,1)S(1)}, bf16[4,512,512]{2,1,0:T(8,128)(2,1)}, u32[]{:S(2)}) copy-start(bf16[4,512,512]{2,1,0:T(8,128)(2,1)} %inv_ref.7) | copy-start | bytes 6291460
  2.9 40.2 %copy-start.3 = (f32[3,8,256]{2,1,0:T(8,128)S(1)}, f32[3,8,256]{2,1,0:T(8,128)}, u32[]{:S(2)}) copy-start(f32[3,8,256]{2,1,0:T(8,128)} %target_ref.1) | copy-start | bytes 73732
  2.9 40.2 %copy-start.4 = (f32[8,256]{1,0:T(8,128)S(1)}, f32[8,256]{1,0:T(8,128)}, u32[]{:S(2)}) copy-start(f32[8,256]{1,0:T(8,128)} %inertia_ref.1) | copy-start | bytes 24580
  3.0 40.2 %copy-start.5 = (s32[64]{0:T(128)S(1)}, s32[64]{0:T(128)}, u32[]{:S(2)}) copy-start(s32[64]{0:T(128)} %pin_ref.1) | copy-start | bytes 772
  5.8 10.2 %collective-permute-start = (f32[256,256]{1,0:T(8,128)S(1)}, f32[256,256]{1,0:T(8,128)S(1)}, u32[]{:S(2)}, u32[]{:S(2)}) collective-permute-start(f32[256,256]{1,0:T(8,128)S(1)} %get-tuple-element.37.after_ref.own_ref), channel_id=1, source_target_pairs={{0,8},{8,0},{16,24},{24,16},{1,9},{9,1},{17,25},{25,17},{2,10},{10... | collective-permute-start | bytes 786440 | tf_op jit(solution)/shard_map/ppermute | solution.py:567
  9.3 4.0 %collective-permute-start.1 = (f32[8,128]{1,0:T(8,128)S(1)}, f32[8,128]{1,0:T(8,128)S(1)}, u32[]{:S(2)}, u32[]{:S(2)}) collective-permute-start(f32[8,128]{1,0:T(8,128)S(1)} %get-tuple-element.39), channel_id=1, source_target_pairs={{1,0},{2,1},{3,2},{5,4},{6,5},{7,6},{9,8},{10,9},{11,10},{13,12},{... | collective-permute-start | bytes 12296 | tf_op jit(solution)/shard_map/ppermute | solution.py:577
  16.3 10.6 %collective-permute-start.2 = (f32[256,256]{1,0:T(8,128)S(1)}, f32[256,256]{1,0:T(8,128)S(1)}, u32[]{:S(2)}, u32[]{:S(2)}) collective-permute-start(f32[256,256]{1,0:T(8,128)S(1)} %get-tuple-element.40.own_ref.two_ref), channel_id=1, source_target_pairs={{0,24},{8,16},{16,8},{24,0},{1,25},{9,17},{17,9},{25,1},{2,26},{10... | collective-permute-start | bytes 786440 | tf_op jit(solution)/shard_map/ppermute | solution.py:584
  21.0 0.7 collective-permute-start.3
  27.2 10.4 %collective-permute-start.5 = (f32[256,256]{1,0:T(8,128)S(1)}, f32[256,256]{1,0:T(8,128)S(1)}, u32[]{:S(2)}, u32[]{:S(2)}) collective-permute-start(f32[256,256]{1,0:T(8,128)S(1)} %get-tuple-element.45.own_ref), channel_id=1, source_target_pairs={{0,32},{32,0},{64,96},{96,64},{128,160},{160,128},{192,224},{224,1... | collective-permute-start | bytes 786440 | tf_op jit(solution)/shard_map/ppermute | solution.py:593
  32.2 5.5 %collective-permute-start.4 = (f32[8,128]{1,0:T(8,128)S(1)}, f32[8,128]{1,0:T(8,128)S(1)}, u32[]{:S(2)}, u32[]{:S(2)}) collective-permute-start(f32[8,128]{1,0:T(8,128)S(1)} %get-tuple-element.43), channel_id=1, source_target_pairs={{0,1},{1,2},{2,3},{4,5},{5,6},{6,7},{8,9},{9,10},{10,11},{12,13},{... | collective-permute-start | bytes 12296 | tf_op jit(solution)/shard_map/ppermute | solution.py:595
  38.0 9.5 %collective-permute-start.6 = (f32[256,128]{1,0:T(8,128)S(1)}, f32[256,128]{1,0:T(8,128)S(1)}, u32[]{:S(2)}, u32[]{:S(2)}) collective-permute-start(f32[256,128]{1,0:T(8,128)S(1)} %get-tuple-element.52), channel_id=1, source_target_pairs={{0,64},{32,96},{64,0},{96,32},{128,192},{160,224},{192,128},{224,1... | collective-permute-start | bytes 393224 | tf_op jit(solution)/shard_map/ppermute | solution.py:600
  47.8 15.5 %collective-permute-start.7 = (f32[256,128]{1,0:T(8,128)S(1)}, f32[256,128]{1,0:T(8,128)S(1)}, u32[]{:S(2)}, u32[]{:S(2)}) collective-permute-start(f32[256,128]{1,0:T(8,128)S(1)} %shard_map.74), channel_id=1, source_target_pairs={{128,0},{160,32},{192,64},{224,96},{256,384},{288,416},{320,448},{... | collective-permute-start | bytes 393224 | tf_op jit(solution)/shard_map/ppermute | solution.py:626
  92.5 7.2 %collective-permute-start.8 = (f32[8,128]{1,0:T(8,128)S(1)}, f32[8,128]{1,0:T(8,128)S(1)}, u32[]{:S(2)}, u32[]{:S(2)}) collective-permute-start(f32[8,128]{1,0:T(8,128)S(1)} %get-tuple-element.59), channel_id=1, source_target_pairs={{0,1},{1,2},{2,3},{4,5},{5,6},{6,7},{8,9},{9,10},{10,11},{12,13},{... | collective-permute-start | bytes 12296 | tf_op jit(solution)/shard_map/ppermute | solution.py:659
  93.8 5.9 %collective-permute-start.9 = (f32[8,128]{1,0:T(8,128)S(1)}, f32[8,128]{1,0:T(8,128)S(1)}, u32[]{:S(2)}, u32[]{:S(2)}) collective-permute-start(f32[8,128]{1,0:T(8,128)S(1)} %get-tuple-element.60), channel_id=1, source_target_pairs={{1,0},{2,1},{3,2},{5,4},{6,5},{7,6},{9,8},{10,9},{11,10},{13,12},{... | collective-permute-start | bytes 12296 | tf_op jit(solution)/shard_map/ppermute | solution.py:658
  98.4 3.1 %collective-permute-start.10 = (f32[4,256]{1,0:T(4,128)S(1)}, f32[4,256]{1,0:T(4,128)S(1)}, u32[]{:S(2)}, u32[]{:S(2)}) collective-permute-start(f32[4,256]{1,0:T(4,128)S(1)} %get-tuple-element.61), channel_id=1, source_target_pairs={{4,0},{8,4},{12,8},{16,12},{20,16},{24,20},{28,24},{32,28},{36,32}... | collective-permute-start | bytes 12296 | tf_op jit(solution)/shard_map/ppermute | solution.py:656
